TPU v7x, 256 devices: a whole 4x4x8 slice. The times are simulated.
256 devices in a mesh: rows: 64 (over z, x, core), ch: 4 (over y).
Axes of the slice: x: 4, y: 4, z: 8, core: 2. Of those that a mesh axis runs over, the one named last changes fastest.
Arguments:
- features: bfloat16 [256, 64, 2048], P('rows', None, 'ch'), may hold values from -6 to 6
- low_level: bfloat16 [1024, 256, 256], P('rows'), may hold values from -6 to 6
- labels: int32 [1024, 256], P('rows'), may hold values from 0 to 20
- crop_rows: int32 [8], replicated, may hold values from 1 to 144, 256 in all
- w_one: bfloat16 [2048, 256], P('rows', 'ch'), may hold values from -0.125 to 0.125
- w_atrous: bfloat16 [2048, 3, 3, 3, 256], P('rows', None, None, None, 'ch'), may hold values from -0.046875 to 0.046875
- w_pool: bfloat16 [2048, 256], P('rows', 'ch'), may hold values from -0.125 to 0.125
- w_proj: bfloat16 [1280, 256], P('rows', 'ch'), may hold values from -0.15625 to 0.15625
- w_low: bfloat16 [256, 48], P('rows', 'ch'), may hold values from -0.375 to 0.375
- w_unite_up: bfloat16 [256, 3, 3, 256], P('rows', None, None, 'ch'), may hold values from -0.109375 to 0.109375
- w_unite_low: bfloat16 [48, 3, 3, 256], P(None, None, None, 'ch'), may hold values from -0.109375 to 0.109375
- w_refine: bfloat16 [256, 3, 3, 256], P('rows', None, None, 'ch'), may hold values from -0.125 to 0.125
- w_classes: bfloat16 [256, 21], P('ch'), may hold values from -1 to 1
- b_classes: float32 [21], replicated, may hold values from -3 to 3
- gain_aspp: float32 [5, 256], P(None, 'ch'), may hold values from 0.1 to 1.9
- shift_aspp: float32 [5, 256], P(None, 'ch'), may hold values from -3 to 3
- gain_proj: float32 [256], P('ch'), may hold values from 0.1 to 1.9
- shift_proj: float32 [256], P('ch'), may hold values from -3 to 3
- gain_low: float32 [48], P('ch'), may hold values from 0.1 to 1.9
- shift_low: float32 [48], P('ch'), may hold values from -3 to 3
- gain_dec: float32 [2, 256], P(None, 'ch'), may hold values from 0.1 to 1.9
- shift_dec: float32 [2, 256], P(None, 'ch'), may hold values from -3 to 3
Outputs:
- loss: float32 [], replicated
- grad_features: float32 [256, 64, 2048], P('rows', None, 'ch')
- grad_low_level: float32 [1024, 256, 256], P('rows', 'ch')
- grad_w_one: float32 [2048, 256], P('rows', 'ch')
- grad_w_atrous: float32 [2048, 3, 3, 3, 256], P('rows', None, None, None, 'ch')
- grad_w_pool: float32 [2048, 256], P('rows', 'ch')
- grad_w_proj: float32 [1280, 256], P('rows', 'ch')
- grad_w_low: float32 [256, 48], P('rows', 'ch')
- grad_w_unite_up: float32 [256, 3, 3, 256], P('rows', None, None, 'ch')
- grad_w_unite_low: float32 [48, 3, 3, 256], P(None, None, None, 'ch')
- grad_w_refine: float32 [256, 3, 3, 256], P('rows', None, None, 'ch')
- grad_w_classes: float32 [256, 21], P('ch')
- grad_b_classes: float32 [21], replicated
- grad_gain_aspp: float32 [5, 256], P(None, 'ch')
- grad_shift_aspp: float32 [5, 256], P(None, 'ch')
- grad_gain_proj: float32 [256], P('ch')
- grad_shift_proj: float32 [256], P('ch')
- grad_gain_low: float32 [48], P('ch')
- grad_shift_low: float32 [48], P('ch')
- grad_gain_dec: float32 [2, 256], P(None, 'ch')
- grad_shift_dec: float32 [2, 256], P(None, 'ch')
Inputs may be any that keep to these rules, and one draw needn't show every extreme that they name: `crop_rows`: the crops' rows in order along rows; they sum to 256.
All inputs are finite; a program needn't handle non-finite values.
Results may differ from a plain program's by a relative error of at most 0.028.
Values may be sent and summed in bfloat16 or wider, within the bound.
No kernel may reach another device: no remote copies, remote signals or barrier semaphores. Data moves between devices by JAX's collectives and lax.ppermute only.
A program may use at most 256 MiB of HBM per device.

v0:
```python
import jax
import jax.numpy as jnp
from jax import lax
from jax.sharding import Mesh
from jax.sharding import PartitionSpec as P

RATE_SMALL = 6
RATE_MIDDLE = 12
RATE_LARGE = 18
ROWS = ("rows_0", "rows_1", "rows_2")


PRECISE = lax.Precision.HIGHEST
EPSILON = 1e-05


def by_axis(array, axes):
    for axis in axes:
        array = lax.psum(array, axis)
    return array


def from_behind(block, axis, distance):
    devices = range(lax.axis_size(axis))
    route = [(i - distance, i) for i in devices if i - distance in devices]
    return lax.ppermute(block, axis, route)


def padded_2(block, sides, width):
    for axis, dim in sides:
        count = lax.axis_size(axis)
        forward = [(i, i + 1) for i in range(count - 1)]
        backward = [(target, source) for source, target in forward]
        low = lax.ppermute(
            lax.slice_in_dim(block, block.shape[dim] - width, None, axis=dim), axis, forward
        )
        high = lax.ppermute(lax.slice_in_dim(block, 0, width, axis=dim), axis, backward)
        block = jnp.concatenate([low, block, high], axis=dim)
    return block


def in_one_piece(arrays, axis, dim, along):
    columns = [a.reshape(*a.shape[:along], -1) for a in arrays]
    both = jnp.concatenate(columns, axis=along)
    out, at, done = (lax.all_gather(both, axis, axis=dim, tiled=True), 0, [])
    for a, column in zip(arrays, columns):
        piece = out[..., at : at + column.shape[along]]
        done.append(piece.reshape(*piece.shape[:along], *a.shape[along:]))
        at += column.shape[along]
    return tuple(done)


def laid_out(pieces, dim):
    pieces = jnp.moveaxis(pieces, 0, dim)
    dims = pieces.shape
    return pieces.reshape(*dims[:dim], dims[dim] * dims[dim + 1], *dims[dim + 2 :])


def gather_in_order(array, axes, sequence):
    pieces = array[None]
    for k in sequence:
        pieces = lax.all_gather(pieces, axes[k], axis=0, tiled=True)
    current = [lax.axis_size(axes[k]) for k in reversed(sequence)]
    pieces = pieces.reshape(*current, *array.shape)
    turned = sorted(range(len(sequence)), key=lambda place: sequence[len(sequence) - 1 - place])
    return pieces.transpose(*turned, *range(len(sequence), pieces.ndim)).reshape(-1, *array.shape)


def gather_axes(array, axes, sequence, dim):
    return laid_out(gather_in_order(array, axes, sequence), dim)


def cut_along(array, dim, devices):
    before, after = (array.shape[:dim], array.shape[dim + 1 :])
    return jnp.moveaxis(array.reshape(*before, devices, -1, *after), dim, 0)


def sum_at_owner(array, axis, dim):
    devices = lax.axis_size(axis)
    pieces = lax.all_to_all(cut_along(array, dim, devices), axis, 0, 0, tiled=True)
    return jnp.sum(pieces, axis=0)


def sent_together(arrays, axis, dim, along):
    columns = [a.reshape(*a.shape[:along], -1) for a in arrays]
    both = jnp.concatenate(columns, axis=along)
    out, at, done = (sum_at_owner(both, axis, dim), 0, [])
    for a, column in zip(arrays, columns):
        piece = out[..., at : at + column.shape[along]]
        done.append(piece.reshape(*piece.shape[:along], *a.shape[along:]))
        at += column.shape[along]
    return tuple(done)


def image_of(row_ids, image_ends):
    return jnp.sum((row_ids[:, None] >= image_ends[None, :]).astype(jnp.int32), axis=1)


def same_image(row_ids, offset, image_ends, extent):
    neighbour = row_ids + offset
    inside = (row_ids >= 0) & (row_ids < extent) & (neighbour >= 0) & (neighbour < extent)
    return (inside & (image_of(row_ids, image_ends) == image_of(neighbour, image_ends))).astype(
        jnp.float32
    )


def blend_matrix(fine_ids, coarse_ids, image_ends, extent):
    source = fine_ids // 4
    quarter = fine_ids % 4
    weight = jnp.where((quarter == 0) | (quarter == 3), 0.375, 0.125).astype(jnp.float32)
    upper_share = (
        weight * (quarter < 2).astype(jnp.float32) * same_image(source, -1, image_ends, extent)
    )
    lower_share = (
        weight * (quarter >= 2).astype(jnp.float32) * same_image(source, 1, image_ends, extent)
    )
    target = coarse_ids[None, :]
    centre = source[:, None]
    return (
        (target == centre).astype(jnp.float32) * (1.0 - upper_share - lower_share)[:, None]
        + (target == centre - 1).astype(jnp.float32) * upper_share[:, None]
        + (target == centre + 1).astype(jnp.float32) * lower_share[:, None]
    )


def coarse_mix(product, dilation):
    extent = product.shape[1]
    padded = jnp.pad(product, ((0, 0), (dilation, dilation), (0, 0), (0, 0)))
    return (
        padded[:, 0:extent, 0]
        + padded[:, dilation : dilation + extent, 1]
        + padded[:, 2 * dilation : 2 * dilation + extent, 2]
    )


def coarse_spread(values, dilation):
    extent = values.shape[1]
    padded = jnp.pad(values, ((0, 0), (dilation, dilation), (0, 0)))
    return jnp.stack(
        [
            padded[:, 2 * dilation : 2 * dilation + extent],
            padded[:, dilation : dilation + extent],
            padded[:, 0:extent],
        ],
        axis=2,
    )


def fine_mix(product):
    extent = product.shape[3]
    padded = jnp.pad(product, ((0, 0), (0, 0), (0, 0), (1, 1)))
    return (
        padded[:, :, 0, 0:extent]
        + padded[:, :, 1, 1 : 1 + extent]
        + padded[:, :, 2, 2 : 2 + extent]
    )


def fine_spread(values):
    extent = values.shape[2]
    padded = jnp.pad(values, ((0, 0), (0, 0), (1, 1)))
    return jnp.stack(
        [padded[:, :, 2 : 2 + extent], padded[:, :, 1 : 1 + extent], padded[:, :, 0:extent]], axis=2
    )


def row_total(elements):
    flattened = jnp.concatenate([jnp.ravel(element) for element in elements])
    summed = by_axis(flattened, ROWS)
    results = []
    offset = 0
    for element in elements:
        results.append(summed[offset : offset + element.size].reshape(element.shape))
        offset += element.size
    return results


def stack_rim(values, extent, mover):
    height = values.shape[0]
    hops = -(-extent // height)
    above = []
    below = []
    for hop in range(1, hops + 1):
        above.insert(0, mover(values, hop))
        below.append(mover(values, -hop))
    upper_part = jnp.concatenate(above, axis=0)[hops * height - extent :]
    lower_part = jnp.concatenate(below, axis=0)[:extent]
    return jnp.concatenate([upper_part, values, lower_part], axis=0)


def coarse_rim(values, extent):

    def mover(values_in, step):
        return from_behind(values_in, ROWS, step)

    return stack_rim(values, extent, mover)


def product_rim(values, extent):

    def mover(values_in, step):
        return from_behind(values_in.astype(jnp.bfloat16), ROWS, step).astype(values_in.dtype)

    return stack_rim(values, extent, mover)


def fine_rim(values, extent):
    return padded_2(values, ((ROWS, 0),), extent)


def channel_gather(values):
    return lax.all_gather(values, "ch", axis=1, tiled=True)


def channel_sum(values):
    return lax.psum_scatter(
        values.astype(jnp.bfloat16), "ch", scatter_dimension=1, tiled=True
    ).astype(jnp.float32)


def norm_stats(values, axes, count_all, extras):
    local_sum = jnp.sum(values, axis=axes, keepdims=True)
    totals = row_total([local_sum, jnp.sum(jnp.square(values), axis=axes, keepdims=True)] + extras)
    average = totals[0] / count_all
    variance = totals[1] / count_all - jnp.square(average)
    riders = totals[2:]
    return (average, lax.rsqrt(variance + EPSILON), riders)


def norm_apply(values, average, inverse, gain, shift):
    normed = (values - average) * inverse
    return (normed, normed * gain + shift)


def silu_slope(pre_act):
    sigmoid_value = jax.nn.sigmoid(pre_act)
    return sigmoid_value * (1.0 + pre_act * (1.0 - sigmoid_value))


def norm_back(grad_out, normed, pre_act, inverse, gain, axes, count_all, extras):
    grad_pre = grad_out * silu_slope(pre_act)
    totals = row_total(
        [
            jnp.sum(grad_pre * normed, axis=axes, keepdims=True),
            jnp.sum(grad_pre, axis=axes, keepdims=True),
        ]
        + extras
    )
    grad_in = gain * inverse * (grad_pre - (totals[1] + normed * totals[0]) / count_all)
    return (grad_in, totals[0], totals[1], totals[2:])


def fine_conv(values, weight, local_fine, fine_ends, fine_total):
    height = values.shape[0]
    extended = fine_rim(values, 1)
    summed = None
    for row_tap in range(3):
        window = extended[row_tap : row_tap + height]
        product = jnp.einsum(
            "fcv,cjo->fojv", window, weight[:, row_tap], preferred_element_type=jnp.float32
        )
        addend = same_image(local_fine, row_tap - 1, fine_ends, fine_total)[
            :, None, None
        ] * fine_mix(product)
        summed = addend if summed is None else summed + addend
    return summed


def fine_conv_back(gradient, inputs, weight, local_fine, fine_ends, fine_total):
    height = gradient.shape[0]
    extended = fine_rim(gradient, 1)
    grad_in = None
    grad_taps = []
    for row_tap in range(3):
        offset = row_tap - 1
        window = extended[1 - offset : 1 - offset + height]
        keep_rows = same_image(local_fine - offset, offset, fine_ends, fine_total)
        window = jnp.where(keep_rows[:, None, None] > 0, window, jnp.zeros_like(window))
        spread = fine_spread(window)
        addend = jnp.einsum(
            "fojv,cjo->fcv", spread, weight[:, row_tap], preferred_element_type=jnp.float32
        )
        grad_in = addend if grad_in is None else grad_in + addend
        grad_taps.append(
            jnp.einsum("fcv,fojv->cjo", inputs, spread, preferred_element_type=jnp.float32)
        )
    return (grad_in, jnp.stack(grad_taps, axis=1))


def on_device(
    features,
    low_level,
    labels,
    crop_rows,
    w_one,
    w_atrous,
    w_pool,
    w_proj,
    w_low,
    w_unite_up,
    w_unite_low,
    w_refine,
    w_classes,
    b_classes,
    gain_aspp,
    shift_aspp,
    gain_proj,
    shift_proj,
    gain_low,
    shift_low,
    gain_dec,
    shift_dec,
):
    strip_rows = features.shape[0]
    columns = features.shape[1]
    fine_strip = low_level.shape[0]
    fine_columns = low_level.shape[2]
    groups = lax.axis_size(ROWS)
    parts_ch = lax.axis_size("ch")
    strip_index = lax.axis_index(ROWS)
    total_rows = strip_rows * groups
    fine_total = fine_strip * groups
    images = crop_rows.shape[0]
    pixels = float(total_rows * columns)
    fine_pixels = float(fine_total * fine_columns)
    image_ends = jnp.cumsum(crop_rows)
    fine_ends = 4 * image_ends
    local_rows = strip_index * strip_rows + jnp.arange(strip_rows, dtype=jnp.int32)
    local_fine = strip_index * fine_strip + jnp.arange(fine_strip, dtype=jnp.int32)
    dilations = (RATE_SMALL, RATE_MIDDLE, RATE_LARGE)
    reach_rows = RATE_LARGE
    one_all, atrous_all, pool_all, proj_all, shrink_all, unite_all, refine_all = (
        *in_one_piece((w_one, w_atrous, w_pool), ROWS, 0, 1),
        lax.all_gather(w_proj, ROWS, axis=0, tiled=True),
        *in_one_piece((w_low, w_unite_up, w_refine), ROWS, 0, 1),
    )
    up_share = unite_all.shape[0] // parts_ch
    unite_weight = jnp.concatenate(
        [
            unite_all.reshape((parts_ch, -1) + unite_all.shape[1:]),
            w_unite_low.reshape((parts_ch, -1) + w_unite_low.shape[1:]),
        ],
        axis=1,
    ).reshape((-1,) + unite_all.shape[1:])
    gathered = lax.all_gather(features, "ch", axis=2, tiled=True)
    branch_zero = jnp.einsum("rwc,co->rwo", gathered, one_all, preferred_element_type=jnp.float32)
    atrous_out = []
    centre_taps = []
    side_taps = []
    for branch_index in range(3):
        for row_tap in range(3):
            product = jnp.einsum(
                "rwc,cjo->rwjo",
                gathered,
                atrous_all[:, branch_index, row_tap],
                preferred_element_type=jnp.float32,
            )
            mixed = coarse_mix(product, dilations[branch_index])
            if row_tap == 1:
                centre_taps.append(mixed)
            else:
                side_taps.append(mixed)
    sides = product_rim(jnp.stack(side_taps, axis=2), reach_rows)
    for branch_index in range(3):
        dilation = dilations[branch_index]
        summed = (
            same_image(local_rows, 0, image_ends, total_rows)[:, None, None]
            * centre_taps[branch_index]
        )
        for side_index in range(2):
            offset = (2 * side_index - 1) * dilation
            window = sides[
                reach_rows + offset : reach_rows + offset + strip_rows,
                :,
                2 * branch_index + side_index,
            ]
            keep_rows = same_image(local_rows, offset, image_ends, total_rows)
            summed = summed + keep_rows[:, None, None] * window
        atrous_out.append(summed)
    spatial = jnp.stack([branch_zero] + atrous_out, axis=2)
    column_sums = jnp.sum(gathered, axis=1, dtype=jnp.float32)
    member = (
        image_of(local_rows, image_ends)[:, None] == jnp.arange(images, dtype=jnp.int32)[None, :]
    ).astype(jnp.float32)
    image_part = jnp.dot(member.T, column_sums, precision=PRECISE)
    counts_all = crop_rows.astype(jnp.float32) * float(columns)
    mean_sp, inverse_sp, riders = norm_stats(spatial, (0, 1), pixels, [image_part])
    pooled = riders[0] / counts_all[:, None]
    normed_sp, pre_sp = norm_apply(spatial, mean_sp, inverse_sp, gain_aspp[:4], shift_aspp[:4])
    act_spatial = jax.nn.silu(pre_sp)
    pooled_low = pooled.astype(jnp.bfloat16)
    pool_z = jnp.dot(pooled_low, pool_all, preferred_element_type=jnp.float32)
    pool_mean = jnp.mean(pool_z, axis=0, keepdims=True)
    pool_inverse = lax.rsqrt(
        jnp.mean(jnp.square(pool_z - pool_mean), axis=0, keepdims=True) + EPSILON
    )
    pool_normed, pool_pre = norm_apply(pool_z, pool_mean, pool_inverse, gain_aspp[4], shift_aspp[4])
    pool_act = jax.nn.silu(pool_pre)
    pool_map = jnp.dot(member, pool_act, precision=PRECISE)
    branches = jnp.concatenate(
        [
            act_spatial,
            jnp.broadcast_to(
                pool_map[:, None, None, :], (strip_rows, columns, 1, pool_map.shape[1])
            ),
        ],
        axis=2,
    ).astype(jnp.bfloat16)
    joined = lax.all_gather(branches, "ch", axis=3, tiled=True).reshape(strip_rows, columns, -1)
    proj_z = jnp.einsum("rwc,co->rwo", joined, proj_all, preferred_element_type=jnp.float32)
    mean_p, inverse_p, _ = norm_stats(proj_z, (0, 1), pixels, [])
    normed_p, pre_p = norm_apply(proj_z, mean_p, inverse_p, gain_proj, shift_proj)
    aspp_out = jax.nn.silu(pre_p).astype(jnp.bfloat16)
    aspp_ext = coarse_rim(aspp_out, 1)
    ext_rows = strip_index * strip_rows - 1 + jnp.arange(strip_rows + 2, dtype=jnp.int32)
    row_blend = blend_matrix(local_fine, ext_rows, image_ends, total_rows)
    column_blend = blend_matrix(
        jnp.arange(fine_columns, dtype=jnp.int32),
        jnp.arange(columns, dtype=jnp.int32),
        jnp.zeros((1,), jnp.int32),
        columns,
    )
    up_rows = jnp.einsum("fk,kwc->fwc", row_blend, aspp_ext.astype(jnp.float32), precision=PRECISE)
    upsampled = jnp.einsum("fwc,vw->fcv", up_rows, column_blend, precision=PRECISE).astype(
        jnp.bfloat16
    )
    low_z = jnp.einsum("fcv,co->fov", low_level, shrink_all, preferred_element_type=jnp.float32)
    mean_l, inverse_l, _ = norm_stats(low_z, (0, 2), fine_pixels, [])
    normed_l, pre_l = norm_apply(
        low_z, mean_l, inverse_l, gain_low[None, :, None], shift_low[None, :, None]
    )
    low_act = jax.nn.silu(pre_l).astype(jnp.bfloat16)
    united_in = channel_gather(jnp.concatenate([upsampled, low_act], axis=1))
    united_z = fine_conv(united_in, unite_weight, local_fine, fine_ends, fine_total)
    mean_1, inverse_1, _ = norm_stats(united_z, (0, 2), fine_pixels, [])
    normed_1, pre_1 = norm_apply(
        united_z, mean_1, inverse_1, gain_dec[0][None, :, None], shift_dec[0][None, :, None]
    )
    hidden = jax.nn.silu(pre_1).astype(jnp.bfloat16)
    hidden_all = channel_gather(hidden)
    refine_z = fine_conv(hidden_all, refine_all, local_fine, fine_ends, fine_total)
    mean_2, inverse_2, _ = norm_stats(refine_z, (0, 2), fine_pixels, [])
    normed_2, pre_2 = norm_apply(
        refine_z, mean_2, inverse_2, gain_dec[1][None, :, None], shift_dec[1][None, :, None]
    )
    refined = jax.nn.silu(pre_2).astype(jnp.bfloat16)
    logit_part = jnp.einsum("fcv,ck->fkv", refined, w_classes, preferred_element_type=jnp.float32)
    logits = (
        lax.psum(logit_part.astype(jnp.bfloat16), "ch").astype(jnp.float32)
        + b_classes[None, :, None]
    )
    highest = jnp.max(logits, axis=1, keepdims=True)
    exponent = jnp.exp(logits - highest)
    exp_total = jnp.sum(exponent, axis=1, keepdims=True)
    one_hot = (
        labels[:, None, :] == jnp.arange(logits.shape[1], dtype=jnp.int32)[None, :, None]
    ).astype(jnp.float32)
    entropy = jnp.log(exp_total[:, 0, :]) + highest[:, 0, :] - jnp.sum(logits * one_hot, axis=1)
    grad_logits = ((exponent / exp_total - one_hot) / images).astype(jnp.bfloat16)
    classes_part = jnp.einsum(
        "fcv,fkv->ck", refined, grad_logits, preferred_element_type=jnp.float32
    )
    bias_part = jnp.sum(grad_logits, axis=(0, 2), dtype=jnp.float32)
    grad_refined = jnp.einsum(
        "fkv,ck->fcv", grad_logits, w_classes, preferred_element_type=jnp.float32
    )
    grad_refine_z, gain_grad_2, shift_grad_2, riders = norm_back(
        grad_refined,
        normed_2,
        pre_2,
        inverse_2,
        gain_dec[1][None, :, None],
        (0, 2),
        fine_pixels,
        [classes_part, bias_part, jnp.sum(entropy)],
    )
    grad_classes, grad_bias, loss_sum = riders
    loss_value = loss_sum / images
    hidden_part, grad_refine_full = fine_conv_back(
        grad_refine_z.astype(jnp.bfloat16),
        hidden_all,
        refine_all,
        local_fine,
        fine_ends,
        fine_total,
    )
    grad_hidden = channel_sum(hidden_part)
    grad_united_z, gain_grad_1, shift_grad_1, _ = norm_back(
        grad_hidden, normed_1, pre_1, inverse_1, gain_dec[0][None, :, None], (0, 2), fine_pixels, []
    )
    united_part, grad_unite_full = fine_conv_back(
        grad_united_z.astype(jnp.bfloat16),
        united_in,
        unite_weight,
        local_fine,
        fine_ends,
        fine_total,
    )
    united_grad = channel_sum(united_part)
    grad_upsampled = united_grad[:, :up_share]
    grad_low_act = united_grad[:, up_share:]
    grad_unite_split = grad_unite_full.reshape((parts_ch, -1) + grad_unite_full.shape[1:])
    grad_unite_up_full = grad_unite_split[:, :up_share].reshape((-1,) + grad_unite_full.shape[1:])
    unite_low_part = grad_unite_split[:, up_share:].reshape((-1,) + grad_unite_full.shape[1:])
    grad_low_z, gain_grad_l, shift_grad_l, riders = norm_back(
        grad_low_act,
        normed_l,
        pre_l,
        inverse_l,
        gain_low[None, :, None],
        (0, 2),
        fine_pixels,
        [unite_low_part],
    )
    grad_unite_low = riders[0]
    grad_low_bf = grad_low_z.astype(jnp.bfloat16)
    grad_shrink_full = jnp.einsum(
        "fcv,fov->co", low_level, grad_low_bf, preferred_element_type=jnp.float32
    )
    low_part = jnp.einsum(
        "fov,co->fcv", grad_low_bf, shrink_all, preferred_element_type=jnp.float32
    )
    grad_low_level = channel_sum(low_part)
    up_grad = fine_rim(grad_upsampled.astype(jnp.bfloat16), 2)
    ext_fine = strip_index * fine_strip - 2 + jnp.arange(fine_strip + 4, dtype=jnp.int32)
    back_blend = blend_matrix(ext_fine, local_rows, image_ends, total_rows)
    grad_cols = jnp.einsum(
        "fcv,vw->fwc", up_grad.astype(jnp.float32), column_blend, precision=PRECISE
    )
    grad_aspp = jnp.einsum("fk,fwc->kwc", back_blend, grad_cols, precision=PRECISE)
    grad_proj_z, gain_grad_p, shift_grad_p, _ = norm_back(
        grad_aspp, normed_p, pre_p, inverse_p, gain_proj, (0, 1), pixels, []
    )
    grad_proj_bf = grad_proj_z.astype(jnp.bfloat16)
    grad_proj_full = jnp.einsum(
        "rwc,rwo->co", joined, grad_proj_bf, preferred_element_type=jnp.float32
    )
    joined_part = jnp.einsum(
        "rwo,co->rwc", grad_proj_bf, proj_all, preferred_element_type=jnp.float32
    ).reshape(strip_rows, columns, 5, -1)
    grad_branches = lax.psum_scatter(
        joined_part.astype(jnp.bfloat16), "ch", scatter_dimension=3, tiled=True
    ).astype(jnp.float32)
    pool_grad_part = jnp.dot(member.T, jnp.sum(grad_branches[:, :, 4], axis=1), precision=PRECISE)
    grad_spatial, gain_grad_sp, shift_grad_sp, riders = norm_back(
        grad_branches[:, :, :4],
        normed_sp,
        pre_sp,
        inverse_sp,
        gain_aspp[:4],
        (0, 1),
        pixels,
        [pool_grad_part],
    )
    pool_pre_grad = riders[0] * silu_slope(pool_pre)
    pool_gain_grad = jnp.sum(pool_pre_grad * pool_normed, axis=0)
    pool_shift_grad = jnp.sum(pool_pre_grad, axis=0)
    pool_z_grad = (
        gain_aspp[4]
        * pool_inverse
        * (pool_pre_grad - (pool_shift_grad + pool_normed * pool_gain_grad) / images)
    ).astype(jnp.bfloat16)
    grad_pool_full = jnp.einsum(
        "ic,io->co", pooled_low, pool_z_grad, preferred_element_type=jnp.float32
    )
    pool_rows = w_pool.shape[0]
    grad_pool = lax.dynamic_slice_in_dim(grad_pool_full, strip_index * pool_rows, pool_rows, 0)
    grad_pooled = (
        jnp.einsum("io,co->ic", pool_z_grad, pool_all, preferred_element_type=jnp.float32)
        / counts_all[:, None]
    )
    pixel_pool = jnp.dot(member, grad_pooled, precision=PRECISE)
    grad_spatial_bf = grad_spatial.astype(jnp.bfloat16)
    grad_input = (
        jnp.einsum(
            "rwo,co->rwc", grad_spatial_bf[:, :, 0], one_all, preferred_element_type=jnp.float32
        )
        + pixel_pool[:, None, :]
    )
    atrous_grad_ext = coarse_rim(grad_spatial_bf[:, :, 1:], reach_rows)
    grad_branch_list = []
    for branch_index in range(3):
        dilation = dilations[branch_index]
        grad_taps = []
        for row_tap in range(3):
            offset = (row_tap - 1) * dilation
            window = atrous_grad_ext[
                reach_rows - offset : reach_rows - offset + strip_rows, :, branch_index
            ]
            keep_rows = same_image(local_rows - offset, offset, image_ends, total_rows)
            window = jnp.where(keep_rows[:, None, None] > 0, window, jnp.zeros_like(window))
            spread = coarse_spread(window, dilation)
            grad_input = grad_input + jnp.einsum(
                "rwjo,cjo->rwc",
                spread,
                atrous_all[:, branch_index, row_tap],
                preferred_element_type=jnp.float32,
            )
        grad_branch_list.append(grad_taps)
    grad_features = lax.psum_scatter(
        grad_input.astype(jnp.bfloat16), "ch", scatter_dimension=2, tiled=True
    ).astype(jnp.float32)
    channel_block = lax.all_to_all(gathered, ROWS, split_axis=2, concat_axis=0, tiled=True)
    all_grads = gather_axes(grad_spatial_bf, ROWS, (1, 0, 2), 0)
    all_rows = jnp.arange(total_rows, dtype=jnp.int32)
    grad_one = jnp.einsum(
        "rwc,rwo->co", channel_block, all_grads[:, :, 0], preferred_element_type=jnp.float32
    )
    padded_grads = jnp.pad(all_grads, ((reach_rows, reach_rows), (0, 0), (0, 0), (0, 0)))
    block_list = []
    for branch_index in range(3):
        dilation = dilations[branch_index]
        block_taps = []
        for row_tap in range(3):
            offset = (row_tap - 1) * dilation
            window = padded_grads[
                reach_rows - offset : reach_rows - offset + total_rows, :, branch_index + 1
            ]
            keep_rows = same_image(all_rows - offset, offset, image_ends, total_rows)
            window = jnp.where(keep_rows[:, None, None] > 0, window, jnp.zeros_like(window))
            spread = coarse_spread(window, dilation)
            block_taps.append(
                jnp.einsum(
                    "rwc,rwjo->cjo", channel_block, spread, preferred_element_type=jnp.float32
                )
            )
        block_list.append(jnp.stack(block_taps, axis=1))
    grad_atrous = jnp.stack(block_list, axis=1)
    grad_proj, grad_shrink, grad_unite_up, grad_refine = (
        sum_at_owner(grad_proj_full, ROWS, 0),
        *sent_together((grad_shrink_full, grad_unite_up_full, grad_refine_full), ROWS, 0, 1),
    )
    grad_gain_aspp = jnp.concatenate([gain_grad_sp.reshape(4, -1), pool_gain_grad[None, :]], axis=0)
    grad_shift_aspp = jnp.concatenate(
        [shift_grad_sp.reshape(4, -1), pool_shift_grad[None, :]], axis=0
    )
    grad_gain_dec = jnp.stack([gain_grad_1.reshape(-1), gain_grad_2.reshape(-1)], axis=0)
    grad_shift_dec = jnp.stack([shift_grad_1.reshape(-1), shift_grad_2.reshape(-1)], axis=0)
    return (
        loss_value,
        grad_features,
        grad_low_level,
        grad_one,
        grad_atrous,
        grad_pool,
        grad_proj,
        grad_shrink,
        grad_unite_up,
        grad_unite_low,
        grad_refine,
        grad_classes,
        grad_bias,
        grad_gain_aspp,
        grad_shift_aspp,
        gain_grad_p.reshape(-1),
        shift_grad_p.reshape(-1),
        gain_grad_l.reshape(-1),
        shift_grad_l.reshape(-1),
        grad_gain_dec,
        grad_shift_dec,
    )


def solution(mesh):
    torus = Mesh(
        mesh.devices.reshape(8, 4, 2, mesh.shape["ch"]), ("rows_0", "rows_1", "rows_2", "ch")
    )
    in_specs = (
        P(ROWS, None, "ch"),
        P(ROWS, None, None),
        P(ROWS, None),
        P(),
        P(ROWS, "ch"),
        P(ROWS, None, None, None, "ch"),
        P(ROWS, "ch"),
        P(ROWS, "ch"),
        P(ROWS, "ch"),
        P(ROWS, None, None, "ch"),
        P(None, None, None, "ch"),
        P(ROWS, None, None, "ch"),
        P("ch", None),
        P(),
        P(None, "ch"),
        P(None, "ch"),
        P("ch"),
        P("ch"),
        P("ch"),
        P("ch"),
        P(None, "ch"),
        P(None, "ch"),
    )
    out_specs = (
        P(),
        P(ROWS, None, "ch"),
        P(ROWS, "ch", None),
        P(ROWS, "ch"),
        P(ROWS, None, None, None, "ch"),
        P(ROWS, "ch"),
        P(ROWS, "ch"),
        P(ROWS, "ch"),
        P(ROWS, None, None, "ch"),
        P(None, None, None, "ch"),
        P(ROWS, None, None, "ch"),
        P("ch", None),
        P(),
        P(None, "ch"),
        P(None, "ch"),
        P("ch"),
        P("ch"),
        P("ch"),
        P("ch"),
        P(None, "ch"),
        P(None, "ch"),
    )
    return jax.shard_map(
        on_device, mesh=torus, in_specs=in_specs, out_specs=out_specs, check_vma=False
    )
```

profile of v0, /device:TPU:1, one launch (start us, length us, event | category | flops | bytes accessed | tf_op | source)
XLA Modules:
  0.0 1418.6 jit_solution(12789732533215110098)
XLA Ops:
  13.2 53.3 %all-gather.2 = bf16[64,20,64]{2,1,0:T(8,128)(2,1)S(1)} all-gather(bf16[1,20,64]{2,1,0:T(8,128)(2,1)} %bitcast.875), channel_id=1, replica_groups=mesh['rows_0'=8,'rows_1'=4,'rows_2'=2,'ch'=4] {'rows_0','rows_1','rows_2'}, dimensions={0}, use_global_device_ids=true | all-gather | bytes 166400 | tf_op jit(solution)/shard_map/all_gather | solution.py:334
  67.5 48.5 %all-gather.1 = bf16[64,4,1164]{2,1,0:T(4,128)(2,1)S(1)} all-gather(bf16[1,4,1164]{2,1,0:T(4,128)(2,1)S(1)} %bitcast.870), channel_id=1, replica_groups=mesh['rows_0'=8,'rows_1'=4,'rows_2'=2,'ch'=4] {'rows_0','rows_1','rows_2'}, dimensions={0}, use_global_device_ids=true | all-gather | bytes 605280 | tf_op jit(solution)/shard_map/all_gather | solution.py:45
  198.1 13.2 collective-permute-start
  222.0 72.1 %all-reduce.51.cloned.1.call-done = f32[16896]{0:T(1024)} async-done(((f32[16896]{0:T(1024)}), f32[16896]{0:T(1024)}) %all-reduce.51.cloned.1.call-update) | async-done | bytes 67600 | tf_op jit(solution)/shard_map/psum | solution.py:19
  294.7 48.1 %all-reduce.53.cloned.1.call-done = f32[16896]{0:T(1024)} async-done(((f32[16896]{0:T(1024)}), f32[16896]{0:T(1024)}) %all-reduce.53.cloned.1.call-update) | async-done | bytes 67600 | tf_op jit(solution)/shard_map/psum | solution.py:19
  343.6 33.4 %all-reduce.55.cloned.1.call-done = f32[16896]{0:T(1024)} async-done(((f32[16896]{0:T(1024)}), f32[16896]{0:T(1024)}) %all-reduce.55.cloned.1.call-update) | async-done | bytes 67600 | tf_op jit(solution)/shard_map/psum | solution.py:19
  385.0 15.5 %all_gather.33 = bf16[4,64,5,256]{1,3,0,2:T(8,128)(2,1)} all-gather(bf16[4,64,5,64]{1,3,0,2:T(8,128)(2,1)S(1)} %pad_maximum_fusion.33), channel_id=1, replica_groups=mesh['rows_0'=8,'rows_1'=4,'rows_2'=2,'ch'=4] {'ch'}, dimensions={3}, use_global_device_ids=true | all-gather | bytes 819200 | tf_op jit(solution)/shard_map/all_gather | solution.py:409
  406.4 13.9 all-reduce.40
  462.5 25.0 %all-gather.14.cloned.1.call-done = bf16[16,304,256]{2,0,1:T(8,128)(2,1)} async-done(((bf16[16,76,256]{2,0,1:T(8,128)(2,1)}), bf16[16,304,256]{2,0,1:T(8,128)(2,1)}) %all-gather.14.cloned.1.call-update) | async-done | bytes 2490384 | tf_op jit(solution)/shard_map/all_gather | solution.py:212
  504.8 13.8 psum.226
  518.6 12.2 psum.227
  538.8 28.3 %all-gather.16.cloned.1.call-done = bf16[16,256,256]{2,1,0:T(8,128)(2,1)} async-done(((bf16[16,64,256]{2,1,0:T(8,128)(2,1)}), bf16[16,256,256]{2,1,0:T(8,128)(2,1)}) %all-gather.16.cloned.1.call-update) | async-done | bytes 2097168 | tf_op jit(solution)/shard_map/all_gather | solution.py:212
  582.7 14.3 %psum.229 = f32[128]{0:T(128)} all-reduce(f32[128]{0:T(128)} %pad_maximum_fusion.53), channel_id=1, replica_groups=mesh['rows_0'=8,'rows_1'=4,'rows_2'=2,'ch'=4] {'rows_0'}, use_global_device_ids=true, to_apply=%region_39.40 | all-reduce | flops 128 | bytes 1024 | tf_op jit(solution)/shard_map/psum | solution.py:19
  597.0 12.3 psum.230
  619.9 40.7 %all-reduce.57.cloned.1.call-done = bf16[16,21,256]{2,1,0:T(8,128)(2,1)} async-done(((bf16[16,21,256]{2,1,0:T(8,128)(2,1)}), bf16[16,21,256]{2,1,0:T(8,128)(2,1)}) %all-reduce.57.cloned.1.call-update) | async-done | bytes 172048 | tf_op jit(solution)/shard_map/psum | solution.py:449
  673.0 13.9 psum.233
  696.0 10.9 psum.235
  721.2 33.2 %reduce-scatter.6.cloned.1.call-done = bf16[16,64,256]{2,1,0:T(8,128)(2,1)} async-done(((bf16[16,256,256]{2,1,0:T(8,128)(2,1)}), bf16[16,64,256]{2,1,0:T(8,128)(2,1)}) %reduce-scatter.6.cloned.1.call-update) | async-done | bytes 524304 | tf_op jit(solution)/shard_map/reduce_scatter | solution.py:216
  757.8 14.3 %psum.236 = f32[128]{0:T(128)} all-reduce(f32[128]{0:T(128)} %pad_maximum_fusion.54), channel_id=1, replica_groups=mesh['rows_0'=8,'rows_1'=4,'rows_2'=2,'ch'=4] {'rows_0'}, use_global_device_ids=true, to_apply=%region_59.60 | all-reduce | flops 128 | bytes 1024 | tf_op jit(solution)/shard_map/psum | solution.py:19
  825.2 16.5 %reduce-scatter.8.cloned.1.call-done = bf16[16,76,256]{2,0,1:T(8,128)(2,1)} async-done(((bf16[16,304,256]{2,0,1:T(8,128)(2,1)}), bf16[16,76,256]{2,0,1:T(8,128)(2,1)}) %reduce-scatter.8.cloned.1.call-update) | async-done | bytes 622608 | tf_op jit(solution)/shard_map/reduce_scatter | solution.py:216
  858.7 13.9 psum.239
  888.7 35.4 %all-reduce.59.cloned.1.call-done = f32[27672]{0:T(1024)} async-done(((f32[27672]{0:T(1024)}), f32[27672]{0:T(1024)}) %all-reduce.59.cloned.1.call-update) | async-done | bytes 110704 | tf_op jit(solution)/shard_map/psum | solution.py:19
  929.0 43.5 %all-reduce.61.cloned.1.call-done = f32[27672]{0:T(1024)} async-done(((f32[27672]{0:T(1024)}), f32[27672]{0:T(1024)}) %all-reduce.61.cloned.1.call-update) | async-done | bytes 110704 | tf_op jit(solution)/shard_map/psum | solution.py:19
  972.6 31.0 %reduce-scatter.10.cloned.1.call-done = bf16[4,64,5,64]{1,3,0,2:T(8,128)(2,1)} async-done(((bf16[4,64,5,256]{1,3,0,2:T(8,128)(2,1)}), bf16[4,64,5,64]{1,3,0,2:T(8,128)(2,1)}) %reduce-scatter.10.cloned.1.call-update) | async-done | bytes 163856 | tf_op jit(solution)/shard_map/reduce_scatter | solution.py:541
  1006.4 13.8 psum.242
  1057.4 16.5 %all-gather = bf16[16,64,4,64]{1,3,0,2:T(8,128)(2,1)} all-gather(bf16[4,64,4,64]{1,3,0,2:T(8,128)(2,1)S(1)} %multiply_convert_fusion.4), channel_id=2, replica_groups=mesh['rows_0'=8,'rows_1'=4,'rows_2'=2,'ch'=4] {'rows_1'}, dimensions={0}, use_global_device_ids=true | all-gather | bytes 655360 | tf_op jit(solution)/shard_map/all_gather | solution.py:62
  1118.2 63.2 %all-gather.18.cloned.1.call-done = bf16[32,4,64,4,64]{4,2,3,1,0:T(8,128)(2,1)} async-done(((bf16[4,4,64,4,64]{4,2,3,1,0:T(8,128)(2,1)}), bf16[32,4,64,4,64]{4,2,3,1,0:T(8,128)(2,1)}) %all-gather.18.cloned.1.call-update) | async-done | bytes 4194320 | tf_op jit(solution)/shard_map/all_gather | solution.py:62
  1207.2 18.6 %all-to-all-done = bf16[64,2,4096]{2,1,0:T(2,128)(2,1)} async-done(((bf16[64,2,4096]{2,1,0:T(2,128)(2,1)}), bf16[64,2,4096]{2,1,0:T(2,128)(2,1)}, u32[]{:S(2)}, u32[]{:S(2)}) %all-to-all-start) | async-done | bytes 1048608 | tf_op jit(solution)/shard_map/all_to_all | solution.py:603
  1302.3 14.2 %copy.404 = bf16[8,4,2,4,64,4,64]{6,4,5,3,2,1,0:T(8,128)(2,1)} copy(bf16[8,4,2,4,64,4,64]{6,4,5,3,1,0,2:T(8,128)(2,1)} %bitcast.836) | data formatting | bytes 16777216 | tf_op jit(solution)/shard_map/transpose | solution.py:66
  1316.5 19.7 %copy.405 = bf16[256,64,4,64]{0,3,1,2:T(8,128)(2,1)} copy(bf16[256,64,4,64]{3,1,2,0:T(8,128)(2,1)} %bitcast.815) | data formatting | bytes 16777216 | tf_op jit(solution)/shard_map/reshape;reshape | solution.py:56
  1336.2 16.4 %broadcast_select_fusion.8 = (bf16[256,64,1,64]{0,3,1,2:T(8,128)(2,1)}, bf16[256,64,1,64]{0,3,1,2:T(8,128)(2,1)}, bf16[256,64,1,64]{0,3,1,2:T(8,128)(2,1)}, bf16...) fusion(pred[256]{0:T(512)(128)(4,1)S(1)} %get-tuple-element.317, ...), kind=kLoop, calls=%fused_computation.190 | loop fusion | flops 9437184 | bytes 33556224 | tf_op jit(solution)/shard_map/jit(_where)/select_n | solution.py:620
  1352.7 15.4 %bitcast_select_fusion.8 = (bf16[256,64,64]{0,2,1:T(8,128)(2,1)}, bf16[256,64,64]{0,2,1:T(8,128)(2,1)}, bf16[256,64,64]{0,2,1:T(8,128)(2,1)}, bf16[256,64,64]{0,...) fusion(pred[256]{0:T(512)(128)(4,1)S(1)} %get-tuple-element.317, ...), kind=kLoop, calls=%fused_computation.171 | loop fusion | flops 9437184 | bytes 33556224 | tf_op jit(solution)/shard_map/jit(_where)/select_n | solution.py:620
  (815 shorter events, 563.9 us)
Async XLA Ops:
  7.2 115.5 %all-gather.12.cloned.1.call-start = ((), (), s32[]{:S(2)}) async-start(), calls=%async_computation.9 | async-start | bytes 1310720 | tf_op jit(solution)/shard_map/all_gather | solution.py:345
  8.0 119.2 %all-gather.10.cloned.1.call-start = ((), (), s32[]{:S(2)}) async-start(), calls=%async_computation.8 | async-start | bytes 7987200 | tf_op jit(solution)/shard_map/all_gather | solution.py:45
  10.9 283.3 %all-reduce.51.cloned.1.call-start = ((), (), s32[]{:S(2)}) async-start(), calls=%async_computation.10 | async-start | bytes 139264 | tf_op jit(solution)/shard_map/psum | solution.py:19
  158.6 31.1 %collective-permute-start.7 = (bf16[4,64,6,64]{1,3,0,2:T(8,128)(2,1)S(1)}, bf16[4,64,6,64]{1,3,0,2:T(8,128)(2,1)S(1)}, u32[]{:S(2)}, u32[]{:S(2)}) collective-permute-start(bf16[4,64,6,64]{1,3,0,2:T(8,128)(2,1)S(1)} %fusion.359), channel_id=1, source_target_pairs={{0,16},{4,20},{8,24},{12,28},{16,32},{20,36},{24,40},{28,44},{32,4... | collective-permute-start | bytes 589832 | tf_op jit(solution)/shard_map/ppermute | solution.py:26
  164.9 27.1 %collective-permute-start.5 = (bf16[4,64,6,64]{1,3,0,2:T(8,128)(2,1)S(1)}, bf16[4,64,6,64]{1,3,0,2:T(8,128)(2,1)S(1)}, u32[]{:S(2)}, u32[]{:S(2)}) collective-permute-start(bf16[4,64,6,64]{1,3,0,2:T(8,128)(2,1)S(1)} %fusion.359), channel_id=1, source_target_pairs={{12,0},{16,4},{20,8},{24,12},{28,16},{32,20},{36,24},{40,28},{44,3... | collective-permute-start | bytes 589832 | tf_op jit(solution)/shard_map/ppermute | solution.py:26
  166.2 31.9 %collective-permute-start.4 = (bf16[4,64,6,64]{1,3,0,2:T(8,128)(2,1)S(1)}, bf16[4,64,6,64]{1,3,0,2:T(8,128)(2,1)S(1)}, u32[]{:S(2)}, u32[]{:S(2)}) collective-permute-start(bf16[4,64,6,64]{1,3,0,2:T(8,128)(2,1)S(1)} %fusion.359), channel_id=1, source_target_pairs={{0,12},{4,16},{8,20},{12,24},{16,28},{20,32},{24,36},{28,40},{32,4... | collective-permute-start | bytes 589832 | tf_op jit(solution)/shard_map/ppermute | solution.py:26
  175.7 35.7 %collective-permute-start.6 = (bf16[4,64,6,64]{1,3,0,2:T(8,128)(2,1)S(1)}, bf16[4,64,6,64]{1,3,0,2:T(8,128)(2,1)S(1)}, u32[]{:S(2)}, u32[]{:S(2)}) collective-permute-start(bf16[4,64,6,64]{1,3,0,2:T(8,128)(2,1)S(1)} %fusion.359), channel_id=1, source_target_pairs={{0,20},{4,24},{8,28},{12,32},{16,36},{20,40},{24,44},{28,48},{32,5... | collective-permute-start | bytes 589832 | tf_op jit(solution)/shard_map/ppermute | solution.py:26
  182.5 35.7 %collective-permute-start.3 = (bf16[4,64,6,64]{1,3,0,2:T(8,128)(2,1)S(1)}, bf16[4,64,6,64]{1,3,0,2:T(8,128)(2,1)S(1)}, u32[]{:S(2)}, u32[]{:S(2)}) collective-permute-start(bf16[4,64,6,64]{1,3,0,2:T(8,128)(2,1)S(1)} %fusion.359), channel_id=1, source_target_pairs={{8,0},{12,4},{16,8},{20,12},{24,16},{28,20},{32,24},{36,28},{40,32... | collective-permute-start | bytes 589832 | tf_op jit(solution)/shard_map/ppermute | solution.py:26
  189.7 28.9 %collective-permute-start.2 = (bf16[4,64,6,64]{1,3,0,2:T(8,128)(2,1)S(1)}, bf16[4,64,6,64]{1,3,0,2:T(8,128)(2,1)S(1)}, u32[]{:S(2)}, u32[]{:S(2)}) collective-permute-start(bf16[4,64,6,64]{1,3,0,2:T(8,128)(2,1)S(1)} %fusion.359), channel_id=1, source_target_pairs={{4,0},{8,4},{12,8},{16,12},{20,16},{24,20},{28,24},{32,28},{36,32}... | collective-permute-start | bytes 589832 | tf_op jit(solution)/shard_map/ppermute | solution.py:26
  192.0 26.5 %collective-permute-start.1 = (bf16[4,64,6,64]{1,3,0,2:T(8,128)(2,1)S(1)}, bf16[4,64,6,64]{1,3,0,2:T(8,128)(2,1)S(1)}, u32[]{:S(2)}, u32[]{:S(2)}) collective-permute-start(bf16[4,64,6,64]{1,3,0,2:T(8,128)(2,1)S(1)} %fusion.359), channel_id=1, source_target_pairs={{0,4},{4,8},{8,12},{12,16},{16,20},{20,24},{24,28},{28,32},{32,36}... | collective-permute-start | bytes 589832 | tf_op jit(solution)/shard_map/ppermute | solution.py:26
  221.4 121.4 %all-reduce.53.cloned.1.call-start = ((), (), s32[]{:S(2)}) async-start(), calls=%async_computation.11 | async-start | bytes 139264 | tf_op jit(solution)/shard_map/psum | solution.py:19
  294.2 82.8 %all-reduce.55.cloned.1.call-start = ((), (), s32[]{:S(2)}) async-start(), calls=%async_computation.12 | async-start | bytes 139264 | tf_op jit(solution)/shard_map/psum | solution.py:19
  342.8 144.6 %all-gather.14.cloned.1.call-start = ((), (), s32[]{:S(2)}) async-start(), calls=%async_computation.13 | async-start | bytes 3112960 | tf_op jit(solution)/shard_map/all_gather | solution.py:212
  451.3 115.8 %all-gather.16.cloned.1.call-start = ((), (), s32[]{:S(2)}) async-start(), calls=%async_computation.14 | async-start | bytes 2621440 | tf_op jit(solution)/shard_map/all_gather | solution.py:212
  536.8 123.7 %all-reduce.57.cloned.1.call-start = ((), (), s32[]{:S(2)}) async-start(), calls=%async_computation.15 | async-start | bytes 393216 | tf_op jit(solution)/shard_map/psum | solution.py:449
  619.3 135.1 %reduce-scatter.6.cloned.1.call-start = ((), (), s32[]{:S(2)}) async-start(), calls=%async_computation.16 | async-start | bytes 2621440 | tf_op jit(solution)/shard_map/reduce_scatter | solution.py:216
  721.1 120.6 %reduce-scatter.8.cloned.1.call-start = ((), (), s32[]{:S(2)}) async-start(), calls=%async_computation.17 | async-start | bytes 3112960 | tf_op jit(solution)/shard_map/reduce_scatter | solution.py:216
  805.9 118.2 %all-reduce.59.cloned.1.call-start = ((), (), s32[]{:S(2)}) async-start(), calls=%async_computation.20 | async-start | bytes 229376 | tf_op jit(solution)/shard_map/psum | solution.py:19
  855.2 117.3 %all-reduce.61.cloned.1.call-start = ((), (), s32[]{:S(2)}) async-start(), calls=%async_computation.21 | async-start | bytes 229376 | tf_op jit(solution)/shard_map/psum | solution.py:19
  924.2 79.3 %reduce-scatter.10.cloned.1.call-start = ((), (), s32[]{:S(2)}) async-start(), calls=%async_computation.18 | async-start | bytes 1638400 | tf_op jit(solution)/shard_map/reduce_scatter | solution.py:541
  929.0 185.4 %all-reduce.63.cloned.1.call-start = ((), (), s32[]{:S(2)}) async-start(), calls=%async_computation.22 | async-start | bytes 229376 | tf_op jit(solution)/shard_map/psum | solution.py:19
  972.5 208.8 %all-gather.18.cloned.1.call-start = ((), (), s32[]{:S(2)}) async-start(), calls=%async_computation.24 | async-start | bytes 9437184 | tf_op jit(solution)/shard_map/all_gather | solution.py:62
  1040.6 44.0 %collective-permute-start.31 = (bf16[4,64,3,64]{1,3,0,2:T(8,128)(2,1)}, bf16[4,64,3,64]{1,3,0,2:T(8,128)(2,1)}, u32[]{:S(2)}, u32[]{:S(2)}) collective-permute-start(bf16[4,64,3,64]{1,3,0,2:T(8,128)(2,1)} %slice.1059), channel_id=1, source_target_pairs={{0,16},{4,20},{8,24},{12,28},{16,32},{20,36},{24,40},{28,44},{32,4... | collective-permute-start | bytes 294920 | tf_op jit(solution)/shard_map/ppermute | solution.py:26
  1043.7 42.2 %collective-permute-start.30 = (bf16[4,64,3,64]{1,3,0,2:T(8,128)(2,1)}, bf16[4,64,3,64]{1,3,0,2:T(8,128)(2,1)}, u32[]{:S(2)}, u32[]{:S(2)}) collective-permute-start(bf16[4,64,3,64]{1,3,0,2:T(8,128)(2,1)} %slice.1059), channel_id=1, source_target_pairs={{0,20},{4,24},{8,28},{12,32},{16,36},{20,40},{24,44},{28,48},{32,5... | collective-permute-start | bytes 294920 | tf_op jit(solution)/shard_map/ppermute | solution.py:26
  1047.3 44.1 %collective-permute-start.29 = (bf16[4,64,3,64]{1,3,0,2:T(8,128)(2,1)}, bf16[4,64,3,64]{1,3,0,2:T(8,128)(2,1)S(1)}, u32[]{:S(2)}, u32[]{:S(2)}) collective-permute-start(bf16[4,64,3,64]{1,3,0,2:T(8,128)(2,1)} %slice.1059), channel_id=1, source_target_pairs={{20,0},{24,4},{28,8},{32,12},{36,16},{40,20},{44,24},{48,28},{52,3... | collective-permute-start | bytes 294920 | tf_op jit(solution)/shard_map/ppermute | solution.py:26
  1048.6 47.4 %collective-permute-start.28 = (bf16[4,64,3,64]{1,3,0,2:T(8,128)(2,1)}, bf16[4,64,3,64]{1,3,0,2:T(8,128)(2,1)}, u32[]{:S(2)}, u32[]{:S(2)}) collective-permute-start(bf16[4,64,3,64]{1,3,0,2:T(8,128)(2,1)} %slice.1059), channel_id=1, source_target_pairs={{16,0},{20,4},{24,8},{28,12},{32,16},{36,20},{40,24},{44,28},{48,3... | collective-permute-start | bytes 294920 | tf_op jit(solution)/shard_map/ppermute | solution.py:26
  1049.9 48.4 %collective-permute-start.27 = (bf16[4,64,3,64]{1,3,0,2:T(8,128)(2,1)}, bf16[4,64,3,64]{1,3,0,2:T(8,128)(2,1)}, u32[]{:S(2)}, u32[]{:S(2)}) collective-permute-start(bf16[4,64,3,64]{1,3,0,2:T(8,128)(2,1)} %slice.1059), channel_id=1, source_target_pairs={{0,12},{4,16},{8,20},{12,24},{16,28},{20,32},{24,36},{28,40},{32,4... | collective-permute-start | bytes 294920 | tf_op jit(solution)/shard_map/ppermute | solution.py:26
  1076.2 222.2 %reduce-scatter.12.cloned.1.call-start = ((), (), s32[]{:S(2)}) async-start(), calls=%async_computation.19 | async-start | bytes 1310720 | tf_op jit(solution)/shard_map/reduce_scatter | solution.py:600
  1114.2 185.9 %reduce-scatter.14.cloned.1.call-start = ((), (), s32[]{:S(2)}) async-start(), calls=%async_computation.23 | async-start | bytes 2621440 | tf_op jit(solution)/shard_map/reduce_scatter | solution.py:216
  1118.1 184.2 %all-gather.20.cloned.1.call-start = ((), (), s32[]{:S(2)}) async-start(), calls=%async_computation.25 | async-start | bytes 25165824 | tf_op jit(solution)/shard_map/all_gather | solution.py:62
  1190.2 35.6 %all-to-all-start = ((bf16[64,2,4096]{2,1,0:T(2,128)(2,1)}), bf16[64,2,4096]{2,1,0:T(2,128)(2,1)}, u32[]{:S(2)}, u32[]{:S(2)}) async-start(bf16[64,2,4096]{2,1,0:T(2,128)(2,1)} %reshape.1247), calls=%async_computation.5 | async-start | bytes 2097152 | tf_op jit(solution)/shard_map/all_to_all | solution.py:603
  1251.9 44.1 %all-to-all-start.2 = ((f32[64,4,1164]{2,1,0:T(4,128)}), f32[64,4,1164]{2,1,0:T(4,128)S(1)}, u32[]{:S(2)}, u32[]{:S(2)}) async-start(f32[64,4,1164]{2,1,0:T(4,128)} %concatenate.165), calls=%async_computation.7 | async-start | bytes 2621440 | tf_op jit(solution)/shard_map/all_to_all | solution.py:80
  (210 other events, 5220.1 us)
Sparse Core Ops, SparseCore 0:
  9.9 29.4 all-gather.11
  42.6 84.4 all-gather.9
  221.5 72.6 all-reduce.50
  296.4 46.3 all-reduce.52
  345.2 31.7 all-reduce.54
  451.4 35.9 all-gather.13
  537.0 30.0 all-gather.15
  619.5 41.0 all-reduce.56
  721.2 33.1 reduce-scatter.5
  806.1 35.6 reduce-scatter.7
  855.3 68.7 all-reduce.58
  926.5 45.9 all-reduce.60
  975.0 28.4 reduce-scatter.9
  1005.9 30.4 all-reduce.62
  1076.3 104.9 all-gather.17
  1184.3 22.2 reduce-scatter.11
  1209.1 33.8 reduce-scatter.13
  1244.6 35.8 all-gather.19
where the time goes:
time: 1430 us; the launch traced here: 1420 us
  waiting for transfers between devices  529 us (37%)
  blocking collectives  354 us (25%)
  local copies, waits for them, and re-layouts  170 us (12%)
  starting transfers between devices  133 us (9%)
  other arithmetic  107 us (7%)
  matrix products  105 us (7%)
  between operations  19.6 us (1%)
    psum x6, waiting for transfers between devices, by_axis(): array = lax.psum(array, axis)  232 us
    psum x21, blocking collectives, by_axis(): array = lax.psum(array, axis)  220 us
    ppermute x22, starting transfers between devices, from_behind(): return lax.ppermute(block, axis, route)  81.5 us
    all_gather x2, waiting for transfers between devices, gather_in_order(): pieces = lax.all_gather(pieces, axes[k], axis=0, tiled=True)  63.2 us
    all_gather x1, blocking collectives, on_device(): lax.all_gather(w_proj, ROWS, axis=0, tiled=True)  53.3 us
    all_gather x2, waiting for transfers between devices, channel_gather(): return lax.all_gather(values, 'ch', axis=1, tiled=True)  53.3 us
    reduce_scatter x3, waiting for transfers between devices, channel_sum(): lax.psum_scatter(values.astype(jnp.bfloat16), 'ch', scatter_dimension=1,...  49.7 us
    all_gather x1, blocking collectives, in_one_piece(): out, at, done = (lax.all_gather(both, axis, axis=dim, tiled=True), 0, [])  48.5 us
  transfers between devices with their start and end apart: 53, of which 25 were waited for; matrix products, arithmetic and copies ran while one was open for 12% of the time, Pallas kernels for 0%

commit v1 on v0

v1 whole, which is shorter than its diff:
```python
import jax
import jax.numpy as jnp
from jax import lax
from jax.sharding import Mesh
from jax.sharding import PartitionSpec as P

DILATIONS = (6, 12, 18)
REACH = 18
EPSILON = 1e-05
PRECISE = lax.Precision.HIGHEST
BF = jnp.bfloat16
F32 = jnp.float32

ROWS = ("z", "x", "core")
ALL = ("z", "x", "core", "y")
STRIP = ("z", "x")
GROUP = ("core", "y")


def hop(block, axes, distance):
    n = lax.axis_size(axes)
    return lax.ppermute(block, axes, [(i, (i + distance) % n) for i in range(n)])


def hop_open(block, axes, distance):
    n = lax.axis_size(axes)
    route = [(i, i + distance) for i in range(n) if 0 <= i + distance < n]
    return lax.ppermute(block, axes, route)


def summed_over(values, groups):
    for axes in groups:
        n = lax.axis_size(axes)
        copies = jnp.broadcast_to(values[None], (n,) + values.shape)
        values = jnp.sum(lax.all_to_all(copies, axes, 0, 0, tiled=True), axis=0)
    return values


def total_of(elements, groups):
    flat = jnp.concatenate([jnp.ravel(e) for e in elements])
    size = flat.shape[0]
    padded = jnp.pad(flat, (0, -size % 128)).reshape(-1, 128)
    out = summed_over(padded, groups).reshape(-1)
    results, at = [], 0
    for e in elements:
        results.append(out[at : at + e.size].reshape(e.shape))
        at += e.size
    return results


def total_all(elements):
    return total_of(elements, (("x", "core", "y"), ("z",)))


def scattered(pieces, axis):
    n = lax.axis_size(axis)
    me = lax.axis_index(axis)
    own = lax.dynamic_index_in_dim(pieces, me, 0, keepdims=False).astype(F32)
    low = pieces.astype(BF)
    for k in range(1, n):
        piece = lax.dynamic_index_in_dim(low, (me + k) % n, 0, keepdims=False)
        own = own + hop(piece, axis, k).astype(F32)
    return own


def gathered(block, axis):
    n = lax.axis_size(axis)
    me = lax.axis_index(axis)
    out = jnp.zeros((n,) + block.shape, block.dtype)
    out = lax.dynamic_update_index_in_dim(out, block, me, 0)
    for k in range(1, n):
        out = lax.dynamic_update_index_in_dim(out, hop(block, axis, k), (me - k) % n, 0)
    return out


def image_of(row_ids, image_ends):
    return jnp.sum((row_ids[:, None] >= image_ends[None, :]).astype(jnp.int32), axis=1)


def same_image(row_ids, offset, image_ends, extent):
    neighbour = row_ids + offset
    inside = (row_ids >= 0) & (row_ids < extent) & (neighbour >= 0) & (neighbour < extent)
    return (inside & (image_of(row_ids, image_ends) == image_of(neighbour, image_ends))).astype(F32)


def blend_matrix(fine_ids, coarse_ids, image_ends, extent):
    source = fine_ids // 4
    quarter = fine_ids % 4
    weight = jnp.where((quarter == 0) | (quarter == 3), 0.375, 0.125).astype(F32)
    upper = weight * (quarter < 2).astype(F32) * same_image(source, -1, image_ends, extent)
    lower = weight * (quarter >= 2).astype(F32) * same_image(source, 1, image_ends, extent)
    target = coarse_ids[None, :]
    centre = source[:, None]
    return (
        (target == centre).astype(F32) * (1.0 - upper - lower)[:, None]
        + (target == centre - 1).astype(F32) * upper[:, None]
        + (target == centre + 1).astype(F32) * lower[:, None]
    )


def shifted(values, step, axis):
    if step == 0:
        return values
    extent = values.shape[axis]
    pads = [(0, 0)] * values.ndim
    pads[axis] = (max(-step, 0), max(step, 0))
    padded = jnp.pad(values, pads)
    start = max(step, 0)
    return lax.slice_in_dim(padded, start, start + extent, axis=axis)


def silu_slope(pre):
    gate = jax.nn.sigmoid(pre)
    return gate * (1.0 + pre * (1.0 - gate))


def moments(sums, squares, count):
    average = sums / count
    return average, lax.rsqrt(squares / count - jnp.square(average) + EPSILON)


def split_two(values):
    high = values.astype(BF)
    return high, (values - high.astype(F32)).astype(BF)


def taps(values, sign):
    return jnp.concatenate([shifted(values, sign * b, 2) for b in (-1, 0, 1)], axis=1)


def dot(spec, a, b):
    return jnp.einsum(spec, a, b, preferred_element_type=F32)


def on_device(
    features,
    low_level,
    labels,
    crop_rows,
    w_one,
    w_atrous,
    w_pool,
    w_proj,
    w_low,
    w_unite_up,
    w_unite_low,
    w_refine,
    w_classes,
    b_classes,
    gain_aspp,
    shift_aspp,
    gain_proj,
    shift_proj,
    gain_low,
    shift_low,
    gain_dec,
    shift_dec,
):
    n_y, n_z, n_x = lax.axis_size("y"), lax.axis_size("z"), lax.axis_size("x")
    core, yi, xi, zi = (lax.axis_index(a) for a in ("core", "y", "x", "z"))
    strip = lax.axis_index(STRIP)
    row = lax.axis_index(ALL)
    groups = lax.axis_size(ROWS)
    rows_in, columns, c_part = features.shape
    total_rows = rows_in * groups
    c_in = c_part * n_y
    fine_strip, c_low, fine_columns = low_level.shape
    fine_total = fine_strip * groups
    branch = w_proj.shape[1] * n_y
    o_part = w_one.shape[1]
    half = o_part // 2
    low_out = w_low.shape[1] * n_y
    classes = w_classes.shape[1]
    images = crop_rows.shape[0]
    pixels = float(total_rows * columns)
    fine_pixels = float(fine_total * fine_columns)
    image_ends = jnp.cumsum(crop_rows)
    fine_ends = 4 * image_ends
    counts = crop_rows.astype(F32) * float(columns)
    tall = 2 * rows_in
    rows8 = strip * tall + jnp.arange(tall, dtype=jnp.int32)

    feats = lax.all_gather(features, GROUP, axis=0, tiled=False)
    feats = feats.reshape(2, n_y, rows_in, columns, c_part).transpose(0, 2, 3, 1, 4)
    feats = feats.reshape(tall * columns, c_in)

    atrous = w_atrous.transpose(0, 1, 3, 2, 4).reshape(w_one.shape[0], 27, o_part)
    own = jnp.concatenate([atrous, w_one[:, None], w_pool[:, None]], axis=1)
    paired = lax.all_to_all(own, "core", 2, 0, tiled=True)
    weights = lax.all_gather(paired.reshape(paired.shape[0], -1), STRIP, axis=0, tiled=True)

    vectors = [gain_dec, shift_dec, gain_proj, shift_proj, gain_low, shift_low]
    flat = jnp.concatenate([jnp.ravel(v) for v in vectors])
    flat = gathered(jnp.pad(flat, (0, -flat.shape[0] % 128)).reshape(-1, 128), "y").reshape(n_y, -1)
    whole, at = [], 0
    for v in vectors:
        piece = flat[:, at : at + v.size].reshape((n_y,) + v.shape)
        whole.append(jnp.moveaxis(piece, 0, -2).reshape(v.shape[:-1] + (-1,)))
        at += v.size
    gain_dec_all, shift_dec_all, gain_p, shift_p, gain_l, shift_l = whole
    gain_a = lax.dynamic_slice_in_dim(gain_aspp, core * half, half, 1)
    shift_a = lax.dynamic_slice_in_dim(shift_aspp, core * half, half, 1)

    def beside(block):
        parts = gathered(block.reshape(-1, 128), "y").reshape((n_y,) + block.shape)
        return jnp.moveaxis(parts, 0, -2).reshape(block.shape[:-1] + (-1,))

    k_row = w_refine.shape[0]
    up_all, refine_all, proj_w, shrink = (
        lax.all_gather(block, ROWS, axis=0, tiled=True)
        for block in (
            beside(w_unite_up).reshape(k_row, -1),
            beside(w_refine).reshape(k_row, -1),
            beside(w_proj),
            lax.all_gather(w_low, "y", axis=1, tiled=True),
        )
    )

    def whole_conv(block):
        return block.reshape(-1, 3, 3, branch).transpose(1, 2, 0, 3)

    up_w = whole_conv(up_all)
    refine_w = whole_conv(refine_all).reshape(3, 3 * branch, branch)
    low_w9 = whole_conv(beside(w_unite_low.reshape(-1, o_part)))
    unite_w = jnp.concatenate([up_w, low_w9], axis=2).reshape(3, -1, branch)
    classes_w = gathered(w_classes, "y").reshape(branch, classes)

    low_own = lax.dynamic_slice_in_dim(low_level, yi * 4, 4, 0)
    labels_own = lax.dynamic_slice_in_dim(labels, yi * 4, 4, 0)
    low_z = dot("fcv,co->fov", low_own, shrink)
    low_above = hop_open(low_z[2:], ALL, 1)
    low_below = hop_open(low_z[:2], ALL, -1)
    low_sums = [jnp.sum(low_z, axis=(0, 2)), jnp.sum(jnp.square(low_z), axis=(0, 2))]

    product = jnp.dot(feats, weights, preferred_element_type=F32).reshape(tall, columns, 29, half)
    centre, minus, plus = [], [], []
    for k, d in enumerate(DILATIONS):
        at = 9 * k
        mixed = (
            product[:, :, at + 3 : at + 6]
            + shifted(product[:, :, at : at + 3], -d, 1)
            + shifted(product[:, :, at + 6 : at + 9], d, 1)
        )
        centre.append(mixed[:, :, 1])
        minus.append(mixed[:, :, 0])
        plus.append(mixed[:, :, 2])
    pool_rows = jnp.sum(product[:, :, 28], axis=1)
    minus = [m.astype(BF) for m in minus]
    plus = [m.astype(BF) for m in plus]

    def packed(parts):
        return jnp.concatenate(parts, axis=0)

    p1 = hop_open(packed([plus[0][0:6], plus[1][4:8]]), STRIP, -1)
    p2 = hop_open(packed([plus[1][0:4], plus[2][2:8]]), STRIP, -2)
    p3 = hop_open(plus[2][0:2], STRIP, -3)
    m1 = hop_open(packed([minus[0][2:8], minus[1][0:4]]), STRIP, 1)
    m2 = hop_open(packed([minus[1][4:8], minus[2][0:6]]), STRIP, 2)
    m3 = hop_open(minus[2][6:8], STRIP, 3)
    from_plus = [
        packed([plus[0][6:8], p1[0:6]]),
        packed([p1[6:10], p2[0:4]]),
        packed([p2[4:10], p3]),
    ]
    from_minus = [
        packed([m1[0:6], minus[0][0:2]]),
        packed([m2[0:4], m1[6:10]]),
        packed([m3, m2[4:10]]),
    ]
    spatial = [product[:, :, 27]]
    for k, d in enumerate(DILATIONS):
        up = same_image(rows8, -d, image_ends, total_rows)[:, None, None]
        down = same_image(rows8, d, image_ends, total_rows)[:, None, None]
        spatial.append(
            centre[k] + up * from_minus[k].astype(F32) + down * from_plus[k].astype(F32)
        )
    spatial = jnp.concatenate(spatial, axis=2)
    member = (
        image_of(rows8, image_ends)[:, None] == jnp.arange(images, dtype=jnp.int32)[None, :]
    ).astype(F32)
    pool_part = jnp.dot(member.T, pool_rows, precision=PRECISE)
    sum_sp, square_sp, pool_sum = total_of(
        [jnp.sum(spatial, axis=(0, 1)), jnp.sum(jnp.square(spatial), axis=(0, 1)), pool_part],
        (STRIP,),
    )
    mean_sp, inverse_sp = moments(sum_sp, square_sp, pixels)
    gain_sp = gain_a[:4].reshape(-1)
    normed_sp = (spatial - mean_sp) * inverse_sp
    pre_sp = normed_sp * gain_sp + shift_a[:4].reshape(-1)
    act_sp = jax.nn.silu(pre_sp).astype(BF)
    pool_z = pool_sum / counts[:, None]
    pool_mean = jnp.mean(pool_z, axis=0, keepdims=True)
    pool_inverse = lax.rsqrt(
        jnp.mean(jnp.square(pool_z - pool_mean), axis=0, keepdims=True) + EPSILON
    )
    pool_normed = (pool_z - pool_mean) * pool_inverse
    pool_pre = pool_normed * gain_a[4] + shift_a[4]
    pool_act = jnp.dot(member, jax.nn.silu(pool_pre), precision=PRECISE).astype(BF)

    lanes = 4 * half
    extra = jnp.pad(pool_act[:, None], ((0, 0), (0, 15), (0, lanes - half)))
    payload = jnp.concatenate([act_sp, extra], axis=1)
    landed = lax.all_to_all(payload, GROUP, 0, 0, tiled=True)
    joined = landed[:, :columns].transpose(1, 0, 2).reshape(columns, -1)
    pool_in = landed[:, columns, :half].reshape(-1)
    main_w = proj_w[: 4 * branch].reshape(4, n_y, 2, half, branch).transpose(2, 1, 0, 3, 4)
    main_w = main_w.reshape(-1, branch)
    pool_w = proj_w[4 * branch :].reshape(n_y, 2, half, branch).transpose(1, 0, 2, 3)
    pool_w = pool_w.reshape(-1, branch)
    proj_z = jnp.dot(joined, main_w, preferred_element_type=F32) + jnp.dot(
        pool_in[None], pool_w, preferred_element_type=F32
    )
    proj_above = hop_open(proj_z, ALL, 1)
    proj_below = hop_open(proj_z, ALL, -1)
    sum_p, square_p, sum_l, square_l = total_all(
        [jnp.sum(proj_z, axis=0), jnp.sum(jnp.square(proj_z), axis=0)] + low_sums
    )
    mean_p, inverse_p = moments(sum_p, square_p, pixels)
    proj_ext = jnp.stack([proj_above, proj_z, proj_below])
    aspp = jax.nn.silu((proj_ext - mean_p) * inverse_p * gain_p + shift_p).astype(BF)

    rows3 = row - 1 + jnp.arange(3, dtype=jnp.int32)
    fine8 = 4 * row - 2 + jnp.arange(8, dtype=jnp.int32)
    row_blend = blend_matrix(fine8, rows3, image_ends, total_rows)
    column_blend = blend_matrix(
        jnp.arange(fine_columns, dtype=jnp.int32),
        jnp.arange(columns, dtype=jnp.int32),
        jnp.zeros((1,), jnp.int32),
        columns,
    ).astype(BF)
    up_rows = sum(
        row_blend[:, k][:, None, None] * aspp[k].astype(F32)[None] for k in range(3)
    )
    up_high, up_low = split_two(up_rows)
    upsampled = (
        dot("fwc,vw->fcv", up_high, column_blend) + dot("fwc,vw->fcv", up_low, column_blend)
    ).astype(BF)
    mean_l, inverse_l = moments(sum_l, square_l, fine_pixels)
    low_ext = jnp.concatenate([low_above, low_z, low_below], axis=0)
    normed_l = (low_ext - mean_l[:, None]) * inverse_l[:, None]
    pre_l = normed_l * gain_l[:, None] + shift_l[:, None]
    low_act = jax.nn.silu(pre_l).astype(BF)
    inside8 = ((fine8 >= 0) & (fine8 < fine_total))[:, None, None]
    united = jnp.where(inside8, jnp.concatenate([upsampled, low_act], axis=1), 0)
    united_t = taps(united, 1)

    fine6 = 4 * row - 1 + jnp.arange(6, dtype=jnp.int32)
    fine4 = 4 * row + jnp.arange(4, dtype=jnp.int32)

    def conv(tapped, weight, ids):
        height = ids.shape[0]
        out = None
        for a in range(3):
            keep = same_image(ids, a - 1, fine_ends, fine_total)[:, None, None]
            part = keep * dot("fkv,ko->fov", tapped[a : a + height], weight[a])
            out = part if out is None else out + part
        return out

    united_z = conv(united_t, unite_w, fine6)
    own_1 = united_z[1:5]
    sum_1, square_1 = total_all([jnp.sum(own_1, axis=(0, 2)), jnp.sum(jnp.square(own_1), axis=(0, 2))])
    mean_1, inverse_1 = moments(sum_1, square_1, fine_pixels)
    normed_1 = (united_z - mean_1[:, None]) * inverse_1[:, None]
    pre_1 = normed_1 * gain_dec_all[0][:, None] + shift_dec_all[0][:, None]
    inside6 = ((fine6 >= 0) & (fine6 < fine_total))[:, None, None]
    hidden = jnp.where(inside6, jax.nn.silu(pre_1).astype(BF), 0)
    hidden_t = taps(hidden, 1)
    refine_z = conv(hidden_t, refine_w, fine4)
    sum_2, square_2 = total_all(
        [jnp.sum(refine_z, axis=(0, 2)), jnp.sum(jnp.square(refine_z), axis=(0, 2))]
    )
    mean_2, inverse_2 = moments(sum_2, square_2, fine_pixels)
    normed_2 = (refine_z - mean_2[:, None]) * inverse_2[:, None]
    pre_2 = normed_2 * gain_dec_all[1][:, None] + shift_dec_all[1][:, None]
    refined = jax.nn.silu(pre_2).astype(BF)

    logits = dot("fcv,ck->fkv", refined, classes_w) + b_classes[None, :, None]
    highest = jnp.max(logits, axis=1, keepdims=True)
    exponent = jnp.exp(logits - highest)
    exp_total = jnp.sum(exponent, axis=1, keepdims=True)
    one_hot = (labels_own[:, None, :] == jnp.arange(classes, dtype=jnp.int32)[None, :, None]).astype(F32)
    entropy = jnp.log(exp_total[:, 0]) + highest[:, 0] - jnp.sum(logits * one_hot, axis=1)
    grad_logits = ((exponent / exp_total - one_hot) / images).astype(BF)
    classes_part = dot("fcv,fkv->ck", refined, grad_logits)
    bias_part = jnp.sum(grad_logits, axis=(0, 2), dtype=F32)
    loss_part = jnp.sum(entropy)
    grad_refined = dot("fkv,ck->fcv", grad_logits, classes_w)

    def back_sums(gp, normed):
        return [jnp.sum(gp * normed, axis=(0, 2)), jnp.sum(gp, axis=(0, 2))]

    def grad_z_of(gp, normed, gain, inverse, grad_gain, grad_shift):
        scale = (gain * inverse)[:, None]
        return (
            scale
            * (gp - (grad_shift[:, None] + normed * grad_gain[:, None]) / fine_pixels)
        ).astype(BF)

    gp_2 = grad_refined * silu_slope(pre_2)
    edge_2 = jnp.stack([gp_2, normed_2], axis=1).astype(BF)
    edge_above = hop_open(edge_2[3:], ALL, 1)
    edge_below = hop_open(edge_2[:1], ALL, -1)
    gain_grad_2, shift_grad_2, grad_bias, loss_sum = total_all(
        back_sums(gp_2, normed_2) + [bias_part, loss_part]
    )
    loss_value = loss_sum / images
    gp_2_ext = jnp.concatenate(
        [edge_above[:, 0].astype(F32), gp_2, edge_below[:, 0].astype(F32)], axis=0
    )
    normed_2_ext = jnp.concatenate(
        [edge_above[:, 1].astype(F32), normed_2, edge_below[:, 1].astype(F32)], axis=0
    )
    grad_refine_z = grad_z_of(
        gp_2_ext, normed_2_ext, gain_dec_all[1], inverse_2, gain_grad_2, shift_grad_2
    )
    grad_refine_z = jnp.where(inside6, grad_refine_z, 0)

    def conv_back(grad_ext, weight, channels):
        grad_t = taps(grad_ext, -1)
        out = None
        for a in range(3):
            start = 2 - a
            keep = same_image(fine4 - (a - 1), a - 1, fine_ends, fine_total)[:, None, None]
            part = keep * dot("fkv,kc->fcv", grad_t[start : start + 4], weight[a])
            out = part if out is None else out + part
        return out

    def turned(weight, channels):
        return weight.reshape(3, 3, channels, branch).transpose(0, 1, 3, 2).reshape(3, -1, channels)

    def conv_weight(tapped, start, grad_own):
        parts = []
        for a in range(3):
            keep = same_image(fine4, a - 1, fine_ends, fine_total)[:, None, None]
            masked = jnp.where(keep > 0, grad_own, jnp.zeros_like(grad_own))
            parts.append(dot("fkv,fov->ko", tapped[start + a : start + a + 4], masked))
        return jnp.stack(parts).reshape(3, 3, -1, n_y, o_part)

    grad_hidden = conv_back(grad_refine_z, turned(refine_w, branch), branch)
    refine_part = conv_weight(hidden_t, 0, grad_refine_z[1:5])

    own_normed_1 = normed_1[1:5]
    gp_1 = grad_hidden * silu_slope(pre_1[1:5])
    edge_1 = gp_1.astype(BF)
    edge_1_above = hop_open(edge_1[3:], ALL, 1)
    edge_1_below = hop_open(edge_1[:1], ALL, -1)
    gain_grad_1, shift_grad_1 = total_all(back_sums(gp_1, own_normed_1))
    gp_1_ext = jnp.concatenate([edge_1_above.astype(F32), gp_1, edge_1_below.astype(F32)], axis=0)
    grad_united_z = grad_z_of(
        gp_1_ext, normed_1, gain_dec_all[0], inverse_1, gain_grad_1, shift_grad_1
    )
    grad_united_z = jnp.where(inside6, grad_united_z, 0)
    grad_united = conv_back(grad_united_z, turned(unite_w, branch + low_out), branch + low_out)
    unite_part = conv_weight(united_t, 1, grad_united_z[1:5])

    grad_up = grad_united[:, :branch].astype(BF)
    grad_cols = dot("fcv,vw->fwc", grad_up, column_blend)
    back_blend = row_blend[2:6]
    to_row = [
        sum(back_blend[f, k] * grad_cols[f] for f in range(4)) for k in range(3)
    ]
    to_above = hop_open(to_row[0], ALL, -1)
    to_below = hop_open(to_row[2], ALL, 1)
    grad_aspp = to_row[1] + to_above + to_below
    normed_p = (proj_z - mean_p) * inverse_p
    pre_p = normed_p * gain_p + shift_p
    gp_p = grad_aspp * silu_slope(pre_p)
    gp_l = grad_united[:, branch:] * silu_slope(pre_l[2:6])
    own_normed_l = normed_l[2:6]
    gain_grad_p, shift_grad_p, gain_grad_l, shift_grad_l = total_all(
        [jnp.sum(gp_p * normed_p, axis=0), jnp.sum(gp_p, axis=0)] + back_sums(gp_l, own_normed_l)
    )
    grad_proj_z = (
        gain_p * inverse_p * (gp_p - (shift_grad_p + normed_p * gain_grad_p) / pixels)
    ).astype(BF)

    grad_sum = jnp.sum(grad_proj_z.astype(F32), axis=0)
    grad_joined = dot("wo,ko->wk", grad_proj_z, main_w)
    grad_joined = grad_joined.reshape(columns, 2 * n_y, lanes).transpose(1, 0, 2).astype(BF)
    pool_high, pool_low = split_two(
        jnp.dot(pool_w.astype(F32), grad_sum, precision=PRECISE).reshape(2 * n_y, half)
    )
    extra = jnp.stack([pool_high, pool_low], axis=1)
    extra = jnp.pad(extra, ((0, 0), (0, 14), (0, lanes - half)))
    back = lax.all_to_all(jnp.concatenate([grad_joined, extra], axis=1), GROUP, 0, 0, tiled=True)
    grad_act = back[:, :columns].astype(F32)
    pool_grad_rows = back[:, columns, :half].astype(F32) + back[:, columns + 1, :half].astype(F32)
    pool_grad_part = jnp.dot(member.T, pool_grad_rows, precision=PRECISE)
    gp_sp = grad_act * silu_slope(pre_sp)
    gain_grad_sp, shift_grad_sp, pool_grad = total_of(
        [jnp.sum(gp_sp * normed_sp, axis=(0, 1)), jnp.sum(gp_sp, axis=(0, 1)), pool_grad_part],
        (STRIP,),
    )
    grad_sp = (
        gain_sp * inverse_sp * (gp_sp - (shift_grad_sp + normed_sp * gain_grad_sp) / pixels)
    ).astype(BF)
    pool_gp = pool_grad * silu_slope(pool_pre)
    pool_gain_grad = jnp.sum(pool_gp * pool_normed, axis=0)
    pool_shift_grad = jnp.sum(pool_gp, axis=0)
    grad_pool_z = (
        gain_a[4]
        * pool_inverse
        * (pool_gp - (pool_shift_grad + pool_normed * pool_gain_grad) / images)
    )

    group_rows = n_x * tall
    wide = gathered(grad_sp, "x").reshape(group_rows, columns, lanes)
    reach_above = hop_open(wide[group_rows - REACH :], "z", 1)
    reach_below = hop_open(wide[:REACH], "z", -1)
    reach = jnp.concatenate([reach_above, wide, reach_below], axis=0)
    ids = zi * group_rows + jnp.arange(group_rows, dtype=jnp.int32)
    spread = []
    for k, d in enumerate(DILATIONS):
        lane = half * (k + 1)
        for b in (-1, 0, 1):
            for a in (-1, 0, 1):
                start = REACH - a * d
                window = reach[start : start + group_rows, :, lane : lane + half]
                keep = same_image(ids - a * d, a * d, image_ends, total_rows)[:, None, None]
                window = jnp.where(keep > 0, window, jnp.zeros_like(window))
                spread.append(shifted(window, -b * d, 1))
    spread.append(wide[:, :, :half])
    member_group = (
        image_of(ids, image_ends)[:, None] == jnp.arange(images, dtype=jnp.int32)[None, :]
    ).astype(F32)
    pool_window = jnp.dot(member_group, grad_pool_z / counts[:, None], precision=PRECISE).astype(BF)
    spread.append(jnp.broadcast_to(pool_window[:, None], (group_rows, columns, half)))
    spread = jnp.concatenate(spread, axis=2)

    own_spread = lax.dynamic_slice_in_dim(spread, xi * tall, tall, 0)
    grad_feats = dot("pk,ck->pc", own_spread.reshape(tall * columns, -1), weights)
    grad_feats = grad_feats.reshape(2, rows_in, columns, c_in)
    grad_feats = scattered(grad_feats, "core")
    grad_feats = jnp.moveaxis(grad_feats.reshape(rows_in, columns, n_y, c_part), 2, 0)
    grad_features = scattered(grad_feats, "y")

    digits = features.reshape(rows_in, columns, c_part // (n_x * o_part), n_x, o_part)
    by_x = lax.all_to_all(jnp.moveaxis(digits, 3, 0), "x", 0, 0, tiled=True)
    feats_x = lax.all_gather(by_x, GROUP, axis=0, tiled=False)
    feats_x = feats_x.reshape((2, n_y, n_x, rows_in, columns) + digits.shape[2:3] + (o_part,))
    feats_x = feats_x.transpose(2, 0, 3, 4, 1, 5, 6).reshape(group_rows * columns, -1)
    aspp_part = dot("pc,pk->ck", feats_x, spread.reshape(group_rows * columns, -1))
    aspp_part = scattered(aspp_part.reshape(n_z, o_part, -1), "z")
    aspp_part = aspp_part.reshape(2, half, 29, half)
    mine = lax.dynamic_index_in_dim(aspp_part, core, 0, keepdims=False)
    theirs = hop(lax.dynamic_index_in_dim(aspp_part, 1 - core, 0, keepdims=False).astype(BF), "core", 1)
    theirs = theirs.astype(F32)
    first = jnp.where(core == 0, mine, theirs)
    second = jnp.where(core == 0, theirs, mine)
    aspp_grad = jnp.concatenate([first, second], axis=2)
    grad_one = aspp_grad[:, 27]
    grad_pool = aspp_grad[:, 28]
    grad_atrous = aspp_grad[:, :27].reshape(-1, 3, 3, 3, o_part).transpose(0, 1, 3, 2, 4)

    grad_low_z = grad_z_of(gp_l, own_normed_l, gain_l, inverse_l, gain_grad_l, shift_grad_l)
    shrink_part = dot("fcv,fov->co", low_own, grad_low_z)
    grad_low_all = gathered(grad_low_z, "y").reshape(fine_strip, low_out, fine_columns)
    shrink_own = lax.dynamic_slice_in_dim(shrink, yi * (c_low // n_y), c_low // n_y, 0)
    grad_low_level = dot("fov,co->fcv", grad_low_all, shrink_own)

    def owned(part):
        return jnp.sum(lax.all_to_all(part.astype(BF), ROWS, 0, 0, tiled=True).astype(F32), axis=0)

    def by_group(part):
        return scattered(jnp.moveaxis(part, -2, 0), "y")

    def conv_pieces(part):
        return by_group(part).transpose(2, 0, 1, 3).reshape(part.shape[2], -1)

    refine_sum = conv_pieces(refine_part)
    unite_sum = conv_pieces(unite_part)
    class_sum = scattered(classes_part.reshape(n_y, -1, classes), "y")
    decoder_sum = owned(
        jnp.concatenate(
            [
                refine_sum.reshape(groups, -1),
                unite_sum[:branch].reshape(groups, -1),
                unite_sum[branch:].reshape(groups, -1),
                class_sum.reshape(groups, -1),
            ],
            axis=1,
        )
    )
    size_9 = k_row * 9 * o_part
    grad_refine = decoder_sum[:size_9].reshape(w_refine.shape)
    grad_unite_up = decoder_sum[size_9 : 2 * size_9].reshape(w_unite_up.shape)
    rest = decoder_sum[2 * size_9 :]
    size_low = low_out * 9 * o_part // groups
    rest = lax.all_to_all(
        jnp.broadcast_to(rest[None], (groups,) + rest.shape), ROWS, 0, 0, tiled=True
    )
    grad_unite_low = rest[:, :size_low].reshape(w_unite_low.shape)
    grad_classes = rest[:, size_low:].reshape(w_classes.shape)
    main_part = dot("wk,wo->ko", joined, grad_proj_z)
    main_part = main_part.reshape(2, n_y, 4, half, branch).transpose(2, 1, 0, 3, 4)
    pool_part_w = (pool_in.astype(F32)[:, None] * grad_sum[None]).reshape(2, n_y, half, branch)
    pool_part_w = pool_part_w.transpose(1, 0, 2, 3)
    proj_part = jnp.concatenate([main_part.reshape(-1, branch), pool_part_w.reshape(-1, branch)])
    proj_sum = by_group(proj_part.reshape(-1, n_y, o_part))
    shrink_sum = by_group(shrink_part.reshape(c_low, n_y, -1))
    late_sum = owned(
        jnp.concatenate([proj_sum.reshape(groups, -1), shrink_sum.reshape(groups, -1)], axis=1)
    )
    size_p = w_proj.size
    grad_proj = late_sum[:size_p].reshape(w_proj.shape)
    grad_shrink = late_sum[size_p:].reshape(w_low.shape)

    both = jnp.stack(
        [
            jnp.concatenate([gain_grad_sp.reshape(4, half), pool_gain_grad[None]]),
            jnp.concatenate([shift_grad_sp.reshape(4, half), pool_shift_grad[None]]),
        ]
    )
    both = gathered(both, "core")
    both = both.transpose(1, 2, 0, 3).reshape(2, 5, o_part)

    def own_channels(vector):
        size = vector.shape[-1] // n_y
        return lax.dynamic_slice_in_dim(vector, yi * size, size, vector.ndim - 1)

    return (
        loss_value,
        grad_features,
        grad_low_level,
        grad_one,
        grad_atrous,
        grad_pool,
        grad_proj,
        grad_shrink,
        grad_unite_up,
        grad_unite_low,
        grad_refine,
        grad_classes,
        grad_bias,
        both[0],
        both[1],
        own_channels(gain_grad_p),
        own_channels(shift_grad_p),
        own_channels(gain_grad_l),
        own_channels(shift_grad_l),
        own_channels(jnp.stack([gain_grad_1, gain_grad_2])),
        own_channels(jnp.stack([shift_grad_1, shift_grad_2])),
    )


def solution(mesh):
    torus = Mesh(mesh.devices.reshape(8, 4, 2, mesh.shape["ch"]), ALL)
    in_specs = (
        P(ROWS, None, "y"),
        P(ROWS, None, None),
        P(ROWS, None),
        P(),
        P(ROWS, "y"),
        P(ROWS, None, None, None, "y"),
        P(ROWS, "y"),
        P(ROWS, "y"),
        P(ROWS, "y"),
        P(ROWS, None, None, "y"),
        P(None, None, None, "y"),
        P(ROWS, None, None, "y"),
        P("y", None),
        P(),
        P(None, "y"),
        P(None, "y"),
        P("y"),
        P("y"),
        P("y"),
        P("y"),
        P(None, "y"),
        P(None, "y"),
    )
    out_specs = (
        P(),
        P(ROWS, None, "y"),
        P(ROWS, "y", None),
        P(ROWS, "y"),
        P(ROWS, None, None, None, "y"),
        P(ROWS, "y"),
        P(ROWS, "y"),
        P(ROWS, "y"),
        P(ROWS, None, None, "y"),
        P(None, None, None, "y"),
        P(ROWS, None, None, "y"),
        P("y", None),
        P(),
        P(None, "y"),
        P(None, "y"),
        P("y"),
        P("y"),
        P("y"),
        P("y"),
        P(None, "y"),
        P(None, "y"),
    )
    return jax.shard_map(
        on_device, mesh=torus, in_specs=in_specs, out_specs=out_specs, check_vma=False
    )
```

time: 1430 us -> 1000 us (0.70)
  waiting for transfers between devices: 529 us -> 59.1 us
  blocking collectives: 354 us -> 116 us
  starting transfers between devices: 133 us -> 332 us
  local copies, waits for them, and re-layouts: 170 us -> 276 us
  matrix products: 105 us -> 55.3 us
  other arithmetic: 107 us -> 126 us
    psum x7 -> x0, waiting for transfers between devices: 273 us -> none  [the longest x6 232 us: by_axis(): array = lax.psum(array, axis)]
    psum x21 -> x0, blocking collectives: 220 us -> none  [by_axis(): array = lax.psum(array, axis)]
    all_to_all x3 -> x20, starting transfers between devices: 25.2 us -> 144 us  [the longest x14 96.1 us: summed_over(): values = jnp.sum(lax.all_to_all(copies, axes, 0, 0, tiled=True), axis=0)]
    all_gather x6 -> x5, waiting for transfers between devices: 118 us -> 0.03 us  [the longest x2 0.02 us: on_device(): lax.all_gather(block, ROWS, axis=0, tiled=True)]
    reduce_scatter x5 -> x0, waiting for transfers between devices: 80.7 us -> none  [the longest x3 49.7 us: channel_sum(): lax.psum_scatter(values.astype(jnp.bfloat16), 'ch', scatter_dimension=1,...]
    ppermute x32 -> x70, starting transfers between devices: 107 us -> 188 us  [the longest x52 127 us: hop(): lax.ppermute(block, axes, [(i, (i + distance) % n) for i in range(n)])]
    dot_general x68 -> x39, matrix products: 105 us -> 55.3 us  [the longest x31 44.2 us: dot(): return jnp.einsum(spec, a, b, preferred_element_type=F32)]
    reshape x15 -> x37, local copies, waits for them, and re-layouts: 5.74 us -> 38.1 us  [the longest x1 10.1 us: on_device(): feats_x.transpose(2, 0, 3, 4, 1, 5, 6).reshape(group_rows * columns, -1)]
  transfers between devices with their start and end apart: 53 -> 95, of which waited for: 25 -> 19; matrix products, arithmetic and copies ran while one was open for 12% -> 43% of each run, Pallas kernels for 0% -> 0%
where the time goes in v1:
time: 1000 us; the launch traced here: 984 us
  starting transfers between devices  332 us (33%)
  local copies, waits for them, and re-layouts  276 us (28%)
  other arithmetic  126 us (13%)
  blocking collectives  116 us (12%)
  waiting for transfers between devices  59.1 us (6%)
  matrix products  55.3 us (6%)
  between operations  19.4 us (2%)
    ppermute x52, starting transfers between devices, hop(): lax.ppermute(block, axes, [(i, (i + distance) % n) for i in range(n)])  127 us
    all_gather x2, blocking collectives, on_device(): lax.all_gather(block, ROWS, axis=0, tiled=True)  102 us
    all_to_all x14, starting transfers between devices, summed_over(): values = jnp.sum(lax.all_to_all(copies, axes, 0, 0, tiled=True), axis=0)  96.1 us
    ppermute x18, starting transfers between devices, hop_open(): return lax.ppermute(block, axes, route)  60.8 us
    unnamed x401, local copies, waits for them, and re-layouts  53.3 us
    dot_general x31, matrix products, dot(): return jnp.einsum(spec, a, b, preferred_element_type=F32)  44.2 us
    all_to_all x14, waiting for transfers between devices, summed_over(): values = jnp.sum(lax.all_to_all(copies, axes, 0, 0, tiled=True), axis=0)  36.6 us
    another operation x22, local copies, waits for them, and re-layouts  26.6 us
  transfers between devices with their start and end apart: 95, of which 19 were waited for; matrix products, arithmetic and copies ran while one was open for 43% of the time, Pallas kernels for 0%

profile of v1, /device:TPU:1, one launch (start us, length us, event | category | flops | bytes accessed | tf_op | source)
XLA Modules:
  0.0 984.2 jit_solution(11995875752722236176)
XLA Ops:
  19.6 6.0 all_to_all.121
  30.0 7.9 all-gather.5
  38.6 48.0 %all-gather.6 = bf16[64,4,48]{2,1,0:T(4,128)(2,1)S(1)} all-gather(bf16[1,4,48]{2,1,0:T(4,128)(2,1)S(1)} %bitcast.761), channel_id=1, replica_groups=mesh['z'=8,'x'=4,'core'=2,'y'=4] {'z','x','core'}, dimensions={0}, use_global_device_ids=true | all-gather | bytes 24960 | tf_op jit(solution)/shard_map/all_gather | solution.py:210
  130.8 54.0 %all-gather.4 = bf16[64,20,256]{2,1,0:T(8,128)(2,1)S(1)} all-gather(bf16[1,20,256]{2,1,0:T(8,128)(2,1)S(1)} %reshape.1569), channel_id=1, replica_groups=mesh['z'=8,'x'=4,'core'=2,'y'=4] {'z','x','core'}, dimensions={0}, use_global_device_ids=true | all-gather | bytes 665600 | tf_op jit(solution)/shard_map/all_gather | solution.py:210
  199.0 6.7 convolution_bitcast_fusion.1
  279.3 11.6 %all-to-all-start.1 = ((f32[32,4,128]{2,1,0:T(4,128)}), f32[32,4,128]{2,1,0:T(4,128)S(1)}, u32[]{:S(2)}, u32[]{:S(2)}) async-start(f32[32,4,128]{2,1,0:T(4,128)} %broadcast_in_dim.372), calls=%async_computation.1 | async-start | bytes 131072 | tf_op jit(solution)/shard_map/all_to_all | solution.py:35
  292.3 7.4 all-to-all-done.1
  309.4 6.1 all-to-all-start.2
  332.0 7.5 all-to-all-start.3
  380.0 12.3 %all-to-all-start.5 = ((f32[32,4,128]{2,1,0:T(4,128)}), f32[32,4,128]{2,1,0:T(4,128)S(1)}, u32[]{:S(2)}, u32[]{:S(2)}) async-start(f32[32,4,128]{2,1,0:T(4,128)} %broadcast_in_dim.390), calls=%async_computation.5 | async-start | bytes 131072 | tf_op jit(solution)/shard_map/all_to_all | solution.py:35
  401.5 6.7 all-to-all-start.6
  424.6 8.2 all-to-all-start.7
  446.7 8.5 copy.647
  455.2 10.1 %reshape.1539 = bf16[2048,512]{1,0:T(8,128)(2,1)} reshape(bf16[4,2,4,64,4,2,64]{6,5,4,3,2,1,0:T(2,128)(2,1)} %copy.647) | data formatting | bytes 4194304 | tf_op jit(solution)/shard_map/reshape | solution.py:541
  484.4 8.7 all-to-all-start.9
  511.9 6.0 all-to-all-done.10
  529.4 9.1 all-to-all-start.11
  633.6 6.3 all-to-all-start.13
  642.4 8.1 all-to-all-done.13
  651.1 7.0 all-to-all-start.14
  751.3 13.6 %all-to-all-start.18 = ((bf16[64,2,664]{2,1,0:T(2,128)(2,1)}), bf16[64,2,664]{2,1,0:T(2,128)(2,1)}, u32[]{:S(2)}, u32[]{:S(2)}) async-start(bf16[64,2,664]{2,1,0:T(2,128)(2,1)} %reshape.1653), calls=%async_computation.18 | async-start | bytes 393216 | tf_op jit(solution)/shard_map/all_to_all | solution.py:562
  790.7 8.9 all-to-all-start.19
  801.5 6.3 fusion.122
  816.8 16.5 %concatenate.220 = bf16[32,64,928]{2,1,0:T(8,128)(2,1)} concatenate(bf16[32,64,32]{2,1,0:T(8,128)(2,1)} %get-tuple-element.325, bf16[32,64,32]{2,1,0:T(8,128)(2,1)} %get-tuple-element.323, bf16[32,64,32]{2,1,0:T(8,128)(2,1)} %get-tuple-element.321, bf16[32,64,32]{2,1,0:T(8,128)(2,1)} %copy-done.26, bf16[32,64,32]{2,1,0:T(8,128)(2,1)} %copy-done.18, ...), dimensions={2} | concatenate | bytes 7602176 | tf_op jit(solution)/shard_map/concatenate | solution.py:528
  833.4 6.3 convolution_bitcast_fusion
  846.1 9.7 collective-permute-start.47
  855.8 12.1 %collective-permute-start.48 = (bf16[64,928]{1,0:T(8,128)(2,1)S(1)}, bf16[64,928]{1,0:T(8,128)(2,1)S(1)}, u32[]{:S(2)}, u32[]{:S(2)}) collective-permute-start(bf16[64,928]{1,0:T(8,128)(2,1)S(1)} %get-tuple-element.280), channel_id=1, source_target_pairs={{0,96},{32,128},{64,160},{96,192},{128,224},{160,0},{192,32},{224,... | collective-permute-start | bytes 356360 | tf_op jit(solution)/shard_map/ppermute | solution.py:22
  867.9 11.8 %collective-permute-start.49 = (bf16[64,928]{1,0:T(8,128)(2,1)S(1)}, bf16[64,928]{1,0:T(8,128)(2,1)S(1)}, u32[]{:S(2)}, u32[]{:S(2)}) collective-permute-start(bf16[64,928]{1,0:T(8,128)(2,1)S(1)} %get-tuple-element.279), channel_id=1, source_target_pairs={{0,128},{32,160},{64,192},{96,224},{128,0},{160,32},{192,64},{224,... | collective-permute-start | bytes 356360 | tf_op jit(solution)/shard_map/ppermute | solution.py:22
  879.7 11.8 %collective-permute-start.50 = (bf16[64,928]{1,0:T(8,128)(2,1)S(1)}, bf16[64,928]{1,0:T(8,128)(2,1)S(1)}, u32[]{:S(2)}, u32[]{:S(2)}) collective-permute-start(bf16[64,928]{1,0:T(8,128)(2,1)S(1)} %get-tuple-element.278), channel_id=1, source_target_pairs={{0,160},{32,192},{64,224},{96,0},{128,32},{160,64},{192,96},{224,1... | collective-permute-start | bytes 356360 | tf_op jit(solution)/shard_map/ppermute | solution.py:22
  895.4 11.9 %collective-permute-start.51 = (bf16[64,928]{1,0:T(8,128)(2,1)S(1)}, bf16[64,928]{1,0:T(8,128)(2,1)S(1)}, u32[]{:S(2)}, u32[]{:S(2)}) collective-permute-start(bf16[64,928]{1,0:T(8,128)(2,1)S(1)} %get-tuple-element.277), channel_id=1, source_target_pairs={{0,192},{32,224},{64,0},{96,32},{128,64},{160,96},{192,128},{224,1... | collective-permute-start | bytes 356360 | tf_op jit(solution)/shard_map/ppermute | solution.py:22
  907.3 11.8 %collective-permute-start.52 = (bf16[64,928]{1,0:T(8,128)(2,1)S(1)}, bf16[64,928]{1,0:T(8,128)(2,1)S(1)}, u32[]{:S(2)}, u32[]{:S(2)}) collective-permute-start(bf16[64,928]{1,0:T(8,128)(2,1)S(1)} %get-tuple-element.276), channel_id=1, source_target_pairs={{0,224},{32,0},{64,32},{96,64},{128,96},{160,128},{192,160},{224,1... | collective-permute-start | bytes 356360 | tf_op jit(solution)/shard_map/ppermute | solution.py:22
  937.1 10.3 %all-to-all-start.20 = ((f32[64,1,453]{2,1,0:T(1,128)}), f32[64,1,453]{2,1,0:T(1,128)S(1)}, u32[]{:S(2)}, u32[]{:S(2)}) async-start(f32[64,1,453]{2,1,0:T(1,128)} %broadcast_in_dim.427), calls=%async_computation.20 | async-start | bytes 262144 | tf_op jit(solution)/shard_map/all_to_all | solution.py:589
  (1033 shorter events, 587.2 us)
Async XLA Ops:
  7.2 186.6 %all-gather.15.cloned.1.call-start = ((), (), s32[]{:S(2)}) async-start(), calls=%async_computation.22 | async-start | bytes 2359296 | tf_op jit(solution)/shard_map/all_gather | solution.py:183
  7.9 191.1 %all-gather.13.cloned.1.call-start = ((), (), s32[]{:S(2)}) async-start(), calls=%async_computation.21 | async-start | bytes 4325376 | tf_op jit(solution)/shard_map/all_gather | solution.py:190
  8.8 118.8 %collective-permute-start.18 = (bf16[10,128]{1,0:T(8,128)(2,1)S(1)}, bf16[10,128]{1,0:T(8,128)(2,1)S(1)}, u32[]{:S(2)}, u32[]{:S(2)}) collective-permute-start(bf16[10,128]{1,0:T(8,128)(2,1)S(1)} %reshape.1513), channel_id=1, source_target_pairs={{0,1},{1,2},{2,3},{3,0},{4,5},{5,6},{6,7},{7,4},{8,9},{9,10},{10,1... | collective-permute-start | bytes 7688 | tf_op jit(solution)/shard_map/ppermute | solution.py:22
  10.9 117.2 %collective-permute-start.19 = (bf16[10,128]{1,0:T(8,128)(2,1)S(1)}, bf16[10,128]{1,0:T(8,128)(2,1)S(1)}, u32[]{:S(2)}, u32[]{:S(2)}) collective-permute-start(bf16[10,128]{1,0:T(8,128)(2,1)S(1)} %reshape.1513), channel_id=1, source_target_pairs={{0,2},{1,3},{2,0},{3,1},{4,6},{5,7},{6,4},{7,5},{8,10},{9,11},{10,... | collective-permute-start | bytes 7688 | tf_op jit(solution)/shard_map/ppermute | solution.py:22
  13.5 116.4 %collective-permute-start.20 = (bf16[10,128]{1,0:T(8,128)(2,1)S(1)}, bf16[10,128]{1,0:T(8,128)(2,1)S(1)}, u32[]{:S(2)}, u32[]{:S(2)}) collective-permute-start(bf16[10,128]{1,0:T(8,128)(2,1)S(1)} %reshape.1513), channel_id=1, source_target_pairs={{0,3},{1,0},{2,1},{3,2},{4,7},{5,4},{6,5},{7,6},{8,11},{9,8},{10,9... | collective-permute-start | bytes 7688 | tf_op jit(solution)/shard_map/ppermute | solution.py:22
  15.4 83.2 %collective-permute-start.6 = (bf16[18,128]{1,0:T(8,128)(2,1)S(1)}, bf16[18,128]{1,0:T(8,128)(2,1)S(1)}, u32[]{:S(2)}, u32[]{:S(2)}) collective-permute-start(bf16[18,128]{1,0:T(8,128)(2,1)S(1)} %reshape.1501), channel_id=1, source_target_pairs={{0,1},{1,2},{2,3},{3,0},{4,5},{5,6},{6,7},{7,4},{8,9},{9,10},{10,1... | collective-permute-start | bytes 13832 | tf_op jit(solution)/shard_map/ppermute | solution.py:22
  15.8 86.9 %collective-permute-start.7 = (bf16[18,128]{1,0:T(8,128)(2,1)S(1)}, bf16[18,128]{1,0:T(8,128)(2,1)S(1)}, u32[]{:S(2)}, u32[]{:S(2)}) collective-permute-start(bf16[18,128]{1,0:T(8,128)(2,1)S(1)} %reshape.1501), channel_id=1, source_target_pairs={{0,2},{1,3},{2,0},{3,1},{4,6},{5,7},{6,4},{7,5},{8,10},{9,11},{10,... | collective-permute-start | bytes 13832 | tf_op jit(solution)/shard_map/ppermute | solution.py:22
  28.5 296.3 %all-gather.21.cloned.1.call-start = ((), (), s32[]{:S(2)}) async-start(), calls=%async_computation.25 | async-start | bytes 1198080 | tf_op jit(solution)/shard_map/all_gather | solution.py:210
  110.9 284.4 %all-gather.19.cloned.1.call-start = ((), (), s32[]{:S(2)}) async-start(), calls=%async_computation.24 | async-start | bytes 1198080 | tf_op jit(solution)/shard_map/all_gather | solution.py:210
  118.1 74.3 %collective-permute-start.9 = (bf16[216,128]{1,0:T(8,128)(2,1)}, bf16[216,128]{1,0:T(8,128)(2,1)}, u32[]{:S(2)}, u32[]{:S(2)}) collective-permute-start(bf16[216,128]{1,0:T(8,128)(2,1)} %reshape_reshape.15), channel_id=1, source_target_pairs={{0,1},{1,2},{2,3},{3,0},{4,5},{5,6},{6,7},{7,4},{8,9},{9,10},{10,1... | collective-permute-start | bytes 165896 | tf_op jit(solution)/shard_map/ppermute | solution.py:22
  119.5 171.4 %collective-permute-start.10 = (bf16[216,128]{1,0:T(8,128)(2,1)}, bf16[216,128]{1,0:T(8,128)(2,1)}, u32[]{:S(2)}, u32[]{:S(2)}) collective-permute-start(bf16[216,128]{1,0:T(8,128)(2,1)} %reshape_reshape.15), channel_id=1, source_target_pairs={{0,2},{1,3},{2,0},{3,1},{4,6},{5,7},{6,4},{7,5},{8,10},{9,11},{10,... | collective-permute-start | bytes 165896 | tf_op jit(solution)/shard_map/ppermute | solution.py:22
  127.5 57.6 %collective-permute-start = (bf16[64,21]{0,1:T(8,128)(2,1)S(1)}, bf16[64,21]{0,1:T(8,128)(2,1)}, u32[]{:S(2)}, u32[]{:S(2)}) collective-permute-start(bf16[64,21]{0,1:T(8,128)(2,1)S(1)} %copy-done.114), channel_id=1, source_target_pairs={{0,1},{1,2},{2,3},{3,0},{4,5},{5,6},{6,7},{7,4},{8,9},{9,10},{10,1... | collective-permute-start | bytes 8072 | tf_op jit(solution)/shard_map/ppermute | solution.py:22
  128.1 58.9 %collective-permute-start.1 = (bf16[64,21]{0,1:T(8,128)(2,1)S(1)}, bf16[64,21]{0,1:T(8,128)(2,1)}, u32[]{:S(2)}, u32[]{:S(2)}) collective-permute-start(bf16[64,21]{0,1:T(8,128)(2,1)S(1)} %copy-done.114), channel_id=1, source_target_pairs={{0,2},{1,3},{2,0},{3,1},{4,6},{5,7},{6,4},{7,5},{8,10},{9,11},{10,... | collective-permute-start | bytes 8072 | tf_op jit(solution)/shard_map/ppermute | solution.py:22
  130.0 60.1 %collective-permute-start.2 = (bf16[64,21]{0,1:T(8,128)(2,1)S(1)}, bf16[64,21]{0,1:T(8,128)(2,1)}, u32[]{:S(2)}, u32[]{:S(2)}) collective-permute-start(bf16[64,21]{0,1:T(8,128)(2,1)S(1)} %copy-done.114), channel_id=1, source_target_pairs={{0,3},{1,0},{2,1},{3,2},{4,7},{5,4},{6,5},{7,6},{8,11},{9,8},{10,9... | collective-permute-start | bytes 8072 | tf_op jit(solution)/shard_map/ppermute | solution.py:22
  185.2 130.5 %collective-permute-start.11 = (bf16[216,128]{1,0:T(8,128)(2,1)}, bf16[216,128]{1,0:T(8,128)(2,1)}, u32[]{:S(2)}, u32[]{:S(2)}) collective-permute-start(bf16[216,128]{1,0:T(8,128)(2,1)} %reshape_reshape.15), channel_id=1, source_target_pairs={{0,3},{1,0},{2,1},{3,2},{4,7},{5,4},{6,5},{7,6},{8,11},{9,8},{10,9... | collective-permute-start | bytes 165896 | tf_op jit(solution)/shard_map/ppermute | solution.py:22
  187.0 181.7 %collective-permute-start.26 = (f32[2,48,256]{2,1,0:T(8,128)}, f32[2,48,256]{2,1,0:T(8,128)}, u32[]{:S(2)}, u32[]{:S(2)}) collective-permute-start(f32[2,48,256]{2,1,0:T(8,128)} %get-tuple-element.348), channel_id=1, source_target_pairs={{0,1},{1,2},{2,3},{3,4},{4,5},{5,6},{6,7},{7,8},{8,9},{9,10},{10,1... | collective-permute-start | bytes 294920 | tf_op jit(solution)/shard_map/ppermute | solution.py:28
  271.3 97.4 %collective-permute-start.27 = (f32[2,48,256]{2,1,0:T(8,128)}, f32[2,48,256]{2,1,0:T(8,128)}, u32[]{:S(2)}, u32[]{:S(2)}) collective-permute-start(f32[2,48,256]{2,1,0:T(8,128)} %get-tuple-element.349), channel_id=1, source_target_pairs={{1,0},{2,1},{3,2},{4,3},{5,4},{6,5},{7,6},{8,7},{9,8},{10,9},{11,1... | collective-permute-start | bytes 294920 | tf_op jit(solution)/shard_map/ppermute | solution.py:28
  315.5 131.2 %all-gather.17.cloned.1.call-start = ((), (), s32[]{:S(2)}) async-start(), calls=%async_computation.23 | async-start | bytes 4718592 | tf_op jit(solution)/shard_map/all_gather | solution.py:539
  424.6 40.8 %all-to-all-start.7 = ((f32[32,4,128]{2,1,0:T(4,128)}), f32[32,4,128]{2,1,0:T(4,128)S(1)}, u32[]{:S(2)}, u32[]{:S(2)}) async-start(f32[32,4,128]{2,1,0:T(4,128)} %broadcast_in_dim.393), calls=%async_computation.7 | async-start | bytes 131072 | tf_op jit(solution)/shard_map/all_to_all | solution.py:35
  572.9 85.2 %collective-permute-start.60 = (bf16[3,3,256,64]{2,3,1,0:T(8,128)(2,1)}, bf16[3,3,256,64]{2,3,1,0:T(8,128)(2,1)}, u32[]{:S(2)}, u32[]{:S(2)}) collective-permute-start(bf16[3,3,256,64]{2,3,1,0:T(8,128)(2,1)} %bitcast.675), channel_id=1, source_target_pairs={{0,1},{1,2},{2,3},{3,0},{4,5},{5,6},{6,7},{7,4},{8,9},{9,10},{10,1... | collective-permute-start | bytes 884744 | tf_op jit(solution)/shard_map/ppermute | solution.py:22
  573.7 84.5 %collective-permute-start.61 = (bf16[3,3,256,64]{2,3,1,0:T(8,128)(2,1)}, bf16[3,3,256,64]{2,3,1,0:T(8,128)(2,1)}, u32[]{:S(2)}, u32[]{:S(2)}) collective-permute-start(bf16[3,3,256,64]{2,3,1,0:T(8,128)(2,1)} %bitcast.674), channel_id=1, source_target_pairs={{0,2},{1,3},{2,0},{3,1},{4,6},{5,7},{6,4},{7,5},{8,10},{9,11},{10,... | collective-permute-start | bytes 884744 | tf_op jit(solution)/shard_map/ppermute | solution.py:22
  576.8 81.4 %collective-permute-start.62 = (bf16[3,3,256,64]{2,3,1,0:T(8,128)(2,1)}, bf16[3,3,256,64]{2,3,1,0:T(8,128)(2,1)}, u32[]{:S(2)}, u32[]{:S(2)}) collective-permute-start(bf16[3,3,256,64]{2,3,1,0:T(8,128)(2,1)} %bitcast.673), channel_id=1, source_target_pairs={{0,3},{1,0},{2,1},{3,2},{4,7},{5,4},{6,5},{7,6},{8,11},{9,8},{10,9... | collective-permute-start | bytes 884744 | tf_op jit(solution)/shard_map/ppermute | solution.py:22
  625.3 117.2 %collective-permute-start.63 = (bf16[3,3,304,64]{2,3,1,0:T(8,128)(2,1)}, bf16[3,3,304,64]{2,3,1,0:T(8,128)(2,1)}, u32[]{:S(2)}, u32[]{:S(2)}) collective-permute-start(bf16[3,3,304,64]{2,3,1,0:T(8,128)(2,1)} %bitcast.672), channel_id=1, source_target_pairs={{0,1},{1,2},{2,3},{3,0},{4,5},{5,6},{6,7},{7,4},{8,9},{9,10},{10,1... | collective-permute-start | bytes 1050632 | tf_op jit(solution)/shard_map/ppermute | solution.py:22
  625.3 117.2 %collective-permute-start.64 = (bf16[3,3,304,64]{2,3,1,0:T(8,128)(2,1)}, bf16[3,3,304,64]{2,3,1,0:T(8,128)(2,1)}, u32[]{:S(2)}, u32[]{:S(2)}) collective-permute-start(bf16[3,3,304,64]{2,3,1,0:T(8,128)(2,1)} %bitcast.671), channel_id=1, source_target_pairs={{0,2},{1,3},{2,0},{3,1},{4,6},{5,7},{6,4},{7,5},{8,10},{9,11},{10,... | collective-permute-start | bytes 1050632 | tf_op jit(solution)/shard_map/ppermute | solution.py:22
  679.3 39.0 %all-to-all-start.15 = ((bf16[8,80,128]{2,1,0:T(8,128)(2,1)}), bf16[8,80,128]{2,1,0:T(8,128)(2,1)}, u32[]{:S(2)}, u32[]{:S(2)}) async-start(bf16[8,80,128]{2,1,0:T(8,128)(2,1)} %pad_maximum_fusion.17), calls=%async_computation.15 | async-start | bytes 327680 | tf_op jit(solution)/shard_map/all_to_all | solution.py:485
  751.3 39.4 %all-to-all-start.18 = ((bf16[64,2,664]{2,1,0:T(2,128)(2,1)}), bf16[64,2,664]{2,1,0:T(2,128)(2,1)}, u32[]{:S(2)}, u32[]{:S(2)}) async-start(bf16[64,2,664]{2,1,0:T(2,128)(2,1)} %reshape.1653), calls=%async_computation.18 | async-start | bytes 393216 | tf_op jit(solution)/shard_map/all_to_all | solution.py:562
  790.7 143.1 %all-to-all-start.19 = ((bf16[64,1,5061]{2,1,0:T(2,128)(2,1)}), bf16[64,1,5061]{2,1,0:T(2,128)(2,1)}, u32[]{:S(2)}, u32[]{:S(2)}) async-start(bf16[64,1,5061]{2,1,0:T(2,128)(2,1)} %copy.689), calls=%async_computation.19 | async-start | bytes 2621440 | tf_op jit(solution)/shard_map/all_to_all | solution.py:562
  844.6 50.7 %collective-permute-start.46 = (bf16[64,928]{1,0:T(8,128)(2,1)S(1)}, bf16[64,928]{1,0:T(8,128)(2,1)S(1)}, u32[]{:S(2)}, u32[]{:S(2)}) collective-permute-start(bf16[64,928]{1,0:T(8,128)(2,1)S(1)} %get-tuple-element.275), channel_id=1, source_target_pairs={{0,32},{32,64},{64,96},{96,128},{128,160},{160,192},{192,224},{224... | collective-permute-start | bytes 356360 | tf_op jit(solution)/shard_map/ppermute | solution.py:22
  846.1 61.2 %collective-permute-start.47 = (bf16[64,928]{1,0:T(8,128)(2,1)S(1)}, bf16[64,928]{1,0:T(8,128)(2,1)S(1)}, u32[]{:S(2)}, u32[]{:S(2)}) collective-permute-start(bf16[64,928]{1,0:T(8,128)(2,1)S(1)} %get-tuple-element.281), channel_id=1, source_target_pairs={{0,64},{32,96},{64,128},{96,160},{128,192},{160,224},{192,0},{224,... | collective-permute-start | bytes 356360 | tf_op jit(solution)/shard_map/ppermute | solution.py:22
  855.8 64.4 %collective-permute-start.48 = (bf16[64,928]{1,0:T(8,128)(2,1)S(1)}, bf16[64,928]{1,0:T(8,128)(2,1)S(1)}, u32[]{:S(2)}, u32[]{:S(2)}) collective-permute-start(bf16[64,928]{1,0:T(8,128)(2,1)S(1)} %get-tuple-element.280), channel_id=1, source_target_pairs={{0,96},{32,128},{64,160},{96,192},{128,224},{160,0},{192,32},{224,... | collective-permute-start | bytes 356360 | tf_op jit(solution)/shard_map/ppermute | solution.py:22
  867.9 54.4 %collective-permute-start.49 = (bf16[64,928]{1,0:T(8,128)(2,1)S(1)}, bf16[64,928]{1,0:T(8,128)(2,1)S(1)}, u32[]{:S(2)}, u32[]{:S(2)}) collective-permute-start(bf16[64,928]{1,0:T(8,128)(2,1)S(1)} %get-tuple-element.279), channel_id=1, source_target_pairs={{0,128},{32,160},{64,192},{96,224},{128,0},{160,32},{192,64},{224,... | collective-permute-start | bytes 356360 | tf_op jit(solution)/shard_map/ppermute | solution.py:22
  879.7 42.5 %collective-permute-start.50 = (bf16[64,928]{1,0:T(8,128)(2,1)S(1)}, bf16[64,928]{1,0:T(8,128)(2,1)S(1)}, u32[]{:S(2)}, u32[]{:S(2)}) collective-permute-start(bf16[64,928]{1,0:T(8,128)(2,1)S(1)} %get-tuple-element.278), channel_id=1, source_target_pairs={{0,160},{32,192},{64,224},{96,0},{128,32},{160,64},{192,96},{224,1... | collective-permute-start | bytes 356360 | tf_op jit(solution)/shard_map/ppermute | solution.py:22
  (244 other events, 2944.8 us)
Sparse Core Ops, SparseCore 0:
  9.9 31.9 all-gather.14
  45.1 78.9 all-gather.12
  127.3 76.9 all-gather.20
  207.5 74.4 all-gather.18
  324.9 33.0 all-gather.16

commit v2 on v1

v2 whole, which is shorter than its diff:
```python
import functools

import jax
import jax.numpy as jnp
from jax import lax
from jax.experimental import pallas as pl
from jax.experimental.pallas import tpu as pltpu
from jax.sharding import Mesh
from jax.sharding import PartitionSpec as P

DILATIONS = (6, 12, 18)
REACH = 18
EPSILON = 1e-05
PRECISE = lax.Precision.HIGHEST
BF = jnp.bfloat16
F32 = jnp.float32

ROWS = ("z", "x", "core")
ALL = ("z", "x", "core", "y")
STRIP = ("z", "x")
GROUP = ("core", "y")


def hop(block, axes, distance):
    n = lax.axis_size(axes)
    return lax.ppermute(block, axes, [(i, (i + distance) % n) for i in range(n)])


def hop_open(block, axes, distance):
    n = lax.axis_size(axes)
    route = [(i, i + distance) for i in range(n) if 0 <= i + distance < n]
    return lax.ppermute(block, axes, route)


def summed_over(values, groups):
    for axes in groups:
        n = lax.axis_size(axes)
        copies = jnp.broadcast_to(values[None], (n,) + values.shape)
        values = jnp.sum(lax.all_to_all(copies, axes, 0, 0, tiled=True), axis=0)
    return values


def total_of(elements, groups):
    flat = jnp.concatenate([jnp.ravel(e) for e in elements])
    size = flat.shape[0]
    padded = jnp.pad(flat, (0, -size % 128)).reshape(-1, 128)
    out = summed_over(padded, groups).reshape(-1)
    results, at = [], 0
    for e in elements:
        results.append(out[at : at + e.size].reshape(e.shape))
        at += e.size
    return results


def total_all(elements):
    return total_of(elements, (("x", "core", "y"), ("z",)))


def scattered(pieces, axis):
    n = lax.axis_size(axis)
    me = lax.axis_index(axis)
    own = lax.dynamic_index_in_dim(pieces, me, 0, keepdims=False).astype(F32)
    low = pieces.astype(BF)
    for k in range(1, n):
        piece = lax.dynamic_index_in_dim(low, (me + k) % n, 0, keepdims=False)
        own = own + hop(piece, axis, k).astype(F32)
    return own


def gathered(block, axis):
    n = lax.axis_size(axis)
    me = lax.axis_index(axis)
    out = jnp.zeros((n,) + block.shape, block.dtype)
    out = lax.dynamic_update_index_in_dim(out, block, me, 0)
    for k in range(1, n):
        out = lax.dynamic_update_index_in_dim(out, hop(block, axis, k), (me - k) % n, 0)
    return out


def image_of(row_ids, image_ends):
    return jnp.sum((row_ids[:, None] >= image_ends[None, :]).astype(jnp.int32), axis=1)


def same_image(row_ids, offset, image_ends, extent):
    neighbour = row_ids + offset
    inside = (row_ids >= 0) & (row_ids < extent) & (neighbour >= 0) & (neighbour < extent)
    return (inside & (image_of(row_ids, image_ends) == image_of(neighbour, image_ends))).astype(F32)


def blend_matrix(fine_ids, coarse_ids, image_ends, extent):
    source = fine_ids // 4
    quarter = fine_ids % 4
    weight = jnp.where((quarter == 0) | (quarter == 3), 0.375, 0.125).astype(F32)
    upper = weight * (quarter < 2).astype(F32) * same_image(source, -1, image_ends, extent)
    lower = weight * (quarter >= 2).astype(F32) * same_image(source, 1, image_ends, extent)
    target = coarse_ids[None, :]
    centre = source[:, None]
    return (
        (target == centre).astype(F32) * (1.0 - upper - lower)[:, None]
        + (target == centre - 1).astype(F32) * upper[:, None]
        + (target == centre + 1).astype(F32) * lower[:, None]
    )


def shifted(values, step, axis):
    if step == 0:
        return values
    extent = values.shape[axis]
    pads = [(0, 0)] * values.ndim
    pads[axis] = (max(-step, 0), max(step, 0))
    padded = jnp.pad(values, pads)
    start = max(step, 0)
    return lax.slice_in_dim(padded, start, start + extent, axis=axis)


def silu_slope(pre):
    gate = jax.nn.sigmoid(pre)
    return gate * (1.0 + pre * (1.0 - gate))


def moments(sums, squares, count):
    average = sums / count
    return average, lax.rsqrt(squares / count - jnp.square(average) + EPSILON)


def split_two(values):
    high = values.astype(BF)
    return high, (values - high.astype(F32)).astype(BF)


def taps(values, sign):
    return jnp.concatenate([shifted(values, sign * b, 2) for b in (-1, 0, 1)], axis=1)


def dot(spec, a, b):
    return jnp.einsum(spec, a, b, preferred_element_type=F32)


VMEM = pltpu.VMEM
SMEM = pltpu.SMEM


def mm(a, b):
    return lax.dot_general(a, b, (((1,), (0,)), ((), ())), preferred_element_type=F32)


def mm_nt(a, b):
    return lax.dot_general(a, b, (((1,), (1,)), ((), ())), preferred_element_type=F32)


def mm_tn(a, b):
    return lax.dot_general(a, b, (((0,), (0,)), ((), ())), preferred_element_type=F32)


def run_kernel(body, scalars, arrays, outs, scratch=(), limit=40):
    return pl.pallas_call(
        body,
        out_shape=[jax.ShapeDtypeStruct(shape, kind) for shape, kind in outs],
        in_specs=[pl.BlockSpec(memory_space=SMEM)] * len(scalars)
        + [pl.BlockSpec(memory_space=VMEM)] * len(arrays),
        out_specs=[pl.BlockSpec(memory_space=VMEM)] * len(outs),
        scratch_shapes=[VMEM(shape, kind) for shape, kind in scratch],
        compiler_params=pltpu.CompilerParams(vmem_limit_bytes=limit * 2**20),
    )(*scalars, *arrays)


def tap_rows(values, step):
    if step == 0:
        return values
    extent = values.shape[0]
    ids = lax.broadcasted_iota(jnp.int32, values.shape, 0)
    moved = pltpu.roll(values, (-step) % extent, 0)
    return jnp.where((ids + step >= 0) & (ids + step < extent), moved, 0.0)


def column_sum(values):
    return jnp.sum(values, axis=0, keepdims=True)


def norm_of(total, count):
    mean = total[0:1] / count
    return mean, lax.rsqrt(total[1:2] / count - jnp.square(mean) + EPSILON)


def silu(pre):
    return pre * jax.nn.sigmoid(pre)


def slot_mask(shape, slot):
    lanes = lax.broadcasted_iota(jnp.int32, shape, len(shape) - 1)
    return (lanes >= 32 * slot) & (lanes < 32 * slot + 32)


def lane_roll(values, shift):
    shift = shift % 128
    return values if shift == 0 else pltpu.roll(values, shift, values.ndim - 1)


def product_kernel(
    x_ref, w_ref, pad_ref, a0_ref, a1_ref, a2_ref, p1, p2, p3, m1, m2, m3, acc
):
    rows = x_ref.shape[1]
    depth = x_ref.shape[2]
    n_y = w_ref.shape[0] // depth
    for g in range(9):
        pad_ref[:, 128 * g : 128 * g + 96] = w_ref[:, 96 * g : 96 * g + 96]
        at = {1: 864, 4: 896}.get(g)
        if at is None:
            pad_ref[:, 128 * g + 96 : 128 * g + 128] = jnp.zeros((w_ref.shape[0], 32), BF)
        else:
            pad_ref[:, 128 * g + 96 : 128 * g + 128] = w_ref[:, at : at + 32]
    acc[...] = jnp.zeros_like(acc)

    @pl.loop(0, 2 * n_y)
    def _(i):
        part = pl.ds(pl.multiple_of((i // n_y) * rows, rows), rows)
        deep = pl.ds(pl.multiple_of((i % n_y) * depth, depth), depth)
        acc[part, :] += mm(x_ref[i], pad_ref[deep, :])

    outs = (a0_ref, a1_ref, a2_ref)
    shape = a0_ref.shape
    columns = lax.broadcasted_iota(jnp.int32, shape, 1)
    for k, d in enumerate(DILATIONS):
        left, own, right = (
            acc[:, 128 * (3 * k + j) : 128 * (3 * k + j) + 128].reshape(shape) for j in range(3)
        )
        outs[k][...] = (
            own
            + jnp.where(columns >= d, pltpu.roll(left, d, 1), 0.0)
            + jnp.where(columns < shape[1] - d, pltpu.roll(right, shape[1] - d, 1), 0.0)
        )
    p1[0:6] = a0_ref[0:6].astype(BF)
    p1[6:10] = a1_ref[4:8].astype(BF)
    p2[0:4] = a1_ref[0:4].astype(BF)
    p2[4:10] = a2_ref[2:8].astype(BF)
    p3[...] = a2_ref[0:2].astype(BF)
    m1[0:6] = a0_ref[2:8].astype(BF)
    m1[6:10] = a1_ref[0:4].astype(BF)
    m2[0:4] = a1_ref[4:8].astype(BF)
    m2[4:10] = a2_ref[0:6].astype(BF)
    m3[...] = a2_ref[6:8].astype(BF)


def spatial_kernel(
    up, down, member, a0, a1, a2, p1, p2, p3, m1, m2, m3, out_ref, payload_ref
):
    own = (a0, a1, a2)
    shape = out_ref.shape[1:]
    masks = [slot_mask(shape, slot) for slot in range(4)]

    def plus_of(k, r):
        if k == 0:
            return a0[6 + r] if r < 2 else p1[r - 2].astype(F32)
        if k == 1:
            return p1[6 + r].astype(F32) if r < 4 else p2[r - 4].astype(F32)
        return p2[4 + r].astype(F32) if r < 6 else p3[r - 6].astype(F32)

    def minus_of(k, r):
        if k == 0:
            return m1[r].astype(F32) if r < 6 else a0[r - 6]
        if k == 1:
            return m2[r].astype(F32) if r < 4 else m1[2 + r].astype(F32)
        return m3[r].astype(F32) if r < 2 else m2[2 + r].astype(F32)

    sums = jnp.zeros((1, 128), F32)
    squares = jnp.zeros((1, 128), F32)
    pools = []
    for r in range(out_ref.shape[0]):
        total = jnp.where(masks[0], lane_roll(a0[r], 32), 0.0)
        for k in range(3):
            term = (
                lane_roll(own[k][r], 32 * k)
                + up[k, r] * lane_roll(minus_of(k, r), 32 * (k + 1))
                + down[k, r] * lane_roll(plus_of(k, r), 32 * (k - 1))
            )
            total = jnp.where(masks[k + 1], term, total)
        out_ref[r] = total
        sums = sums + column_sum(total)
        squares = squares + column_sum(total * total)
        pools.append(lane_roll(column_sum(a1[r]), 32))
    first = slot_mask((1, 128), 0)
    packed = [jnp.zeros((1, 128), F32), jnp.zeros((1, 128), F32)]
    for m in range(8):
        part = sum(member[r, m] * pools[r] for r in range(len(pools)))
        packed[m // 4] = packed[m // 4] + lane_roll(jnp.where(first, part, 0.0), 32 * (m % 4))
    payload = jnp.concatenate([sums, squares] + packed, axis=0)
    payload_ref[...] = jnp.broadcast_to(payload[None], payload_ref.shape)


def pool_rows_of(total, slot_rows):
    first = slot_mask((1, 128), 0)
    rows = []
    for m in range(8):
        row = total[slot_rows + m // 4 : slot_rows + m // 4 + 1]
        rows.append(jnp.where(first, lane_roll(row, -32 * (m % 4)), 0.0))
    return rows


def pool_norm(total, counts, gains):
    rows = pool_rows_of(total, 2)
    z = jnp.concatenate([rows[m] / counts[m] for m in range(8)], axis=0)
    mean = jnp.mean(z, axis=0, keepdims=True)
    inverse = lax.rsqrt(jnp.mean(jnp.square(z - mean), axis=0, keepdims=True) + EPSILON)
    normed = (z - mean) * inverse
    return normed, inverse, normed * gains[2:3] + gains[3:4]


def act_kernel(pixels, counts, member, spatial_ref, landed_ref, gains_ref, out_ref):
    total = jnp.sum(landed_ref[...], axis=0)
    gains = gains_ref[...]
    mean, inverse = norm_of(total, pixels)
    _, _, pre = pool_norm(total, counts, gains)
    act = silu(pre)
    columns = spatial_ref.shape[1]
    first_row = lax.broadcasted_iota(jnp.int32, (16, 128), 0) == 0
    for r in range(spatial_ref.shape[0]):
        normed = (spatial_ref[r] - mean) * inverse
        out_ref[r, 0:columns] = silu(normed * gains[0:1] + gains[1:2]).astype(BF)
        row = sum(member[r, m] * act[m : m + 1] for m in range(8))
        row = jnp.where(slot_mask((1, 128), 0), row, 0.0)
        out_ref[r, columns : columns + 16] = jnp.where(first_row, row, 0.0).astype(BF)


def proj_kernel(landed_ref, main_ref, pool_ref, low_ref, out_ref, payload_ref):
    columns = out_ref.shape[0]
    acc = jnp.zeros(out_ref.shape, F32)
    extra = jnp.zeros((16, out_ref.shape[1]), F32)
    for s in range(landed_ref.shape[0]):
        acc = acc + mm(landed_ref[s, 0:columns], main_ref[s])
        extra = extra + mm(landed_ref[s, columns : columns + 16], pool_ref[s])
    z = acc + extra[0:1]
    out_ref[...] = z
    payload = jnp.concatenate([column_sum(z), column_sum(z * z), low_ref[...]], axis=0)
    payload_ref[...] = jnp.broadcast_to(payload[None], payload_ref.shape)


def unite_kernel(
    counts,
    blend,
    keep,
    inside,
    own_ref,
    above_ref,
    below_ref,
    landed_ref,
    gain_ref,
    low_ref,
    low_above_ref,
    low_below_ref,
    low_gain_ref,
    columns_ref,
    up_w_ref,
    low_w_ref,
    z_ref,
    up_ref,
    act_ref,
    payload_ref,
    moments_ref,
    taps_ref,
    low_taps_ref,
    coarse_ref,
    low_all_ref,
):
    total = jnp.sum(landed_ref[...], axis=0)
    mean, inverse = norm_of(total, counts[0])
    mean_l, inverse_l = norm_of(total[2:4, 0:128], counts[1])
    moments_ref[0:1] = mean
    moments_ref[1:2] = inverse
    moments_ref[2:3] = total[2:3] / counts[1]
    moments_ref[3:4] = lax.rsqrt(
        total[3:4] / counts[1] - jnp.square(total[2:3] / counts[1]) + EPSILON
    )
    gain = gain_ref[...]
    low_gain = low_gain_ref[...]
    for k, ref in enumerate((above_ref, own_ref, below_ref)):
        pre = (ref[...] - mean) * inverse * gain[0:1] + gain[1:2]
        coarse_ref[k] = silu(pre).astype(BF).astype(F32)
    low_all_ref[0:2] = low_above_ref[...].astype(F32)
    low_all_ref[2:6] = low_ref[...]
    low_all_ref[6:8] = low_below_ref[...].astype(F32)
    width = z_ref.shape[1]

    @pl.loop(0, 8)
    def _(f):
        row = (
            blend[f, 0] * coarse_ref[0] + blend[f, 1] * coarse_ref[1] + blend[f, 2] * coarse_ref[2]
        )
        high = row.astype(BF)
        rest = (row - high.astype(F32)).astype(BF)
        grown = mm(columns_ref[...], jnp.concatenate([high, rest], axis=0)) * inside[f]
        taps_ref[f] = grown.astype(BF)
        pre = (low_all_ref[f] - mean_l) * inverse_l * low_gain[0:1] + low_gain[1:2]
        act = silu(pre).astype(BF).astype(F32) * inside[f]
        pair = tap_rows(act, -1) + pltpu.roll(act, 64, 1)
        low_taps_ref[f] = jnp.concatenate([pair, tap_rows(act, 1)], axis=1).astype(BF)

        @pl.when((f >= 1) & (f <= 6))
        def _():
            up_ref[f - 1] = grown[width : 2 * width].astype(BF)
            act_ref[f - 1] = act.astype(BF)

    payload_ref[...] = jnp.zeros_like(payload_ref)

    @pl.loop(0, 6)
    def _(f):
        acc = jnp.zeros(z_ref.shape[1:], F32)
        for a in range(3):
            part = mm(low_taps_ref[f + a], low_w_ref[a])
            for b in range(3):
                t = 3 * a + b
                part = part + mm(
                    taps_ref[f + a, b * width : (b + 1) * width, :],
                    up_w_ref[:, 256 * t : 256 * t + 256],
                )
            acc = acc + keep[f, a] * part
        z_ref[f] = acc

        @pl.when((f >= 1) & (f <= 4))
        def _():
            both = jnp.concatenate([column_sum(acc), column_sum(acc * acc)], axis=0)
            payload_ref[...] += jnp.broadcast_to(both[None], payload_ref.shape)


def refine_kernel(
    counts,
    keep,
    inside,
    z_in_ref,
    landed_ref,
    gain_ref,
    w_ref,
    hidden_ref,
    z_ref,
    payload_ref,
    moments_ref,
    taps_ref,
):
    total = jnp.sum(landed_ref[...], axis=0)
    mean, inverse = norm_of(total, counts[1])
    moments_ref[0:1] = mean
    moments_ref[1:2] = inverse
    gain = gain_ref[...]
    width = z_ref.shape[1]

    @pl.loop(0, 6)
    def _(f):
        pre = (z_in_ref[f] - mean) * inverse * gain[0:1] + gain[1:2]
        hidden = silu(pre).astype(BF).astype(F32) * inside[f + 1]
        hidden_ref[f] = hidden.astype(BF)
        for b in range(3):
            taps_ref[f, b * width : (b + 1) * width, :] = tap_rows(hidden, b - 1).astype(BF)

    payload_ref[...] = jnp.zeros_like(payload_ref)

    @pl.loop(0, 4)
    def _(f):
        acc = jnp.zeros(z_ref.shape[1:], F32)
        for a in range(3):
            part = None
            for b in range(3):
                t = 3 * a + b
                term = mm(
                    taps_ref[f + a, b * width : (b + 1) * width, :],
                    w_ref[:, 256 * t : 256 * t + 256],
                )
                part = term if part is None else part + term
            acc = acc + keep[f + 1, a] * part
        z_ref[f] = acc
        both = jnp.concatenate([column_sum(acc), column_sum(acc * acc)], axis=0)
        payload_ref[...] += jnp.broadcast_to(both[None], payload_ref.shape)


def classes_kernel(
    images,
    classes,
    counts,
    z_ref,
    landed_ref,
    gain_ref,
    labels_ref,
    w_ref,
    bias_ref,
    gp_ref,
    payload_ref,
    moments_ref,
    top_ref,
    bottom_ref,
    part_ref,
):
    total = jnp.sum(landed_ref[...], axis=0)
    mean, inverse = norm_of(total, counts[1])
    moments_ref[0:1] = mean
    moments_ref[1:2] = inverse
    gain = gain_ref[...]
    weight = w_ref[...]
    width = z_ref.shape[1]
    shape = (weight.shape[0], width)
    ids = lax.broadcasted_iota(jnp.int32, shape, 0)
    ones = jnp.ones((8, width), BF)
    rows = [jnp.zeros((1, 256), F32) for _ in range(4)]
    part_ref[...] = jnp.zeros_like(part_ref)
    for f in range(4):
        normed = (z_ref[f] - mean) * inverse
        pre = normed * gain[0:1] + gain[1:2]
        gate = jax.nn.sigmoid(pre)
        refined = (pre * gate).astype(BF)
        logits = mm_nt(weight, refined) + bias_ref[:, 0:1]
        valid = ids < classes
        logits = jnp.where(valid, logits, -1e30)
        highest = jnp.max(logits, axis=0, keepdims=True)
        exponent = jnp.exp(logits - highest)
        exp_total = jnp.sum(exponent, axis=0, keepdims=True)
        one_hot = ids == labels_ref[f : f + 1, :]
        picked = jnp.sum(jnp.where(one_hot, logits, 0.0), axis=0, keepdims=True)
        rows[3] = rows[3] + jnp.log(exp_total) + highest - picked
        share = exponent / exp_total - jnp.where(one_hot, 1.0, 0.0)
        grad = jnp.where(valid, share / images, 0.0).astype(BF)
        part_ref[...] += mm(grad, refined)
        counted = mm_nt(ones, grad)[0:1]
        rows[2] = rows[2] + jnp.concatenate(
            [counted, jnp.zeros((1, 256 - shape[0]), F32)], axis=1
        )
        gp = mm_tn(grad, weight) * (gate * (1.0 + pre * (1.0 - gate)))
        gp_ref[f] = gp
        rows[0] = rows[0] + column_sum(gp * normed)
        rows[1] = rows[1] + column_sum(gp)
        if f == 0:
            bottom_ref[0] = gp.astype(BF)
            bottom_ref[1] = normed.astype(BF)
        if f == 3:
            top_ref[0] = gp.astype(BF)
            top_ref[1] = normed.astype(BF)
    payload = jnp.concatenate(rows, axis=0)
    payload_ref[...] = jnp.broadcast_to(payload[None], payload_ref.shape)


def grad_z(gp, normed, scale, total, count):
    return (scale * (gp - (total[1:2] + normed * total[0:1]) / count)).astype(BF)


def store_taps(ref, f, values):
    width = values.shape[0]
    wide = values.astype(F32)
    for b in range(3):
        ref[f, b * width : (b + 1) * width, :] = tap_rows(wide, 1 - b).astype(BF)


def refine_back_kernel(
    counts,
    keep,
    inside,
    gp_ref,
    z_ref,
    above_ref,
    below_ref,
    landed_ref,
    moments_ref,
    gain_ref,
    w_ref,
    z1_ref,
    moments1_ref,
    gain1_ref,
    out_ref,
    taps_ref,
    payload_ref,
    top_ref,
    bottom_ref,
    ends_ref,
):
    total = jnp.sum(landed_ref[...], axis=0)
    mean, inverse = moments_ref[0:1], moments_ref[1:2]
    scale = gain_ref[0:1] * inverse
    count = counts[1]
    for ref, at, f in ((above_ref, 0, 0), (below_ref, 1, 5)):
        edge = grad_z(ref[0].astype(F32), ref[1].astype(F32), scale, total, count)
        store_taps(ends_ref, at, edge.astype(F32) * inside[f + 1])

    @pl.loop(0, 4)
    def _(f):
        normed = (z_ref[f] - mean) * inverse
        store_taps(taps_ref, f, grad_z(gp_ref[f], normed, scale, total, count))

    width = out_ref.shape[1]
    mean1, inverse1 = moments1_ref[0:1], moments1_ref[1:2]
    gain1 = gain1_ref[...]
    payload_ref[...] = jnp.zeros_like(payload_ref)
    for g in range(4):
        acc = jnp.zeros(out_ref.shape[1:], F32)
        for a in range(3):
            source = g + 1 - a
            if source < 0:
                rows = ends_ref.at[0]
            elif source > 3:
                rows = ends_ref.at[1]
            else:
                rows = taps_ref.at[source]
            part = None
            for b in range(3):
                t = 3 * a + b
                term = mm_nt(
                    rows[b * width : (b + 1) * width, :], w_ref[:, 256 * t : 256 * t + 256]
                )
                part = term if part is None else part + term
            acc = acc + keep[g, a] * part
        normed = (z1_ref[g + 1] - mean1) * inverse1
        pre = normed * gain1[0:1] + gain1[1:2]
        gate = jax.nn.sigmoid(pre)
        gp = acc * (gate * (1.0 + pre * (1.0 - gate)))
        out_ref[g] = gp
        both = jnp.concatenate([column_sum(gp * normed), column_sum(gp)], axis=0)
        payload_ref[...] += jnp.broadcast_to(both[None], payload_ref.shape)
        if g == 0:
            bottom_ref[...] = gp.astype(BF)
        if g == 3:
            top_ref[...] = gp.astype(BF)


def unite_back_kernel(
    counts,
    keep,
    inside,
    blend,
    gp_ref,
    z_ref,
    above_ref,
    below_ref,
    landed_ref,
    moments_ref,
    gain_ref,
    up_w_ref,
    low_w_ref,
    columns_ref,
    low_z_ref,
    moments0_ref,
    low_gain_ref,
    taps_ref,
    rows_ref,
    low_gp_ref,
    sums_ref,
    ends_ref,
    flat_ref,
):
    total = jnp.sum(landed_ref[...], axis=0)
    mean, inverse = moments_ref[0:1], moments_ref[1:2]
    scale = gain_ref[0:1] * inverse
    count = counts[1]
    for ref, at, f in ((above_ref, 0, 0), (below_ref, 1, 5)):
        normed = (z_ref[f] - mean) * inverse
        edge = grad_z(ref[...].astype(F32), normed, scale, total, count)
        edge = edge.astype(F32) * inside[f + 1]
        store_taps(ends_ref, at, edge)
        flat_ref[5 * at] = edge.astype(BF)

    @pl.loop(0, 4)
    def _(f):
        normed = (z_ref[f + 1] - mean) * inverse
        edge = grad_z(gp_ref[f], normed, scale, total, count)
        store_taps(taps_ref, f, edge)
        flat_ref[f + 1] = edge

    width = gp_ref.shape[1]
    mean_l, inverse_l = moments0_ref[2:3, 0:128], moments0_ref[3:4, 0:128]
    low_gain = low_gain_ref[...]
    first = lax.broadcasted_iota(jnp.int32, (width, 128), 1) < 64
    rows_ref[...] = jnp.zeros_like(rows_ref)
    sums = [jnp.zeros((1, 128), F32), jnp.zeros((1, 128), F32)]
    for g in range(4):
        acc = jnp.zeros(gp_ref.shape[1:], F32)
        low = jnp.zeros((width, 256), F32)
        for a in range(3):
            source = g + 1 - a
            if source < 0:
                rows = ends_ref.at[0]
            elif source > 3:
                rows = ends_ref.at[1]
            else:
                rows = taps_ref.at[source]
            part = None
            for b in range(3):
                t = 3 * a + b
                term = mm_nt(
                    rows[b * width : (b + 1) * width, :], up_w_ref[:, 256 * t : 256 * t + 256]
                )
                part = term if part is None else part + term
            acc = acc + keep[g, a] * part
            low = low + keep[g, a] * mm_nt(flat_ref[source + 1], low_w_ref[a])
        pair, last = low[:, 0:128], low[:, 128:256]
        low_in = (
            tap_rows(jnp.where(first, pair, 0.0), 1)
            + jnp.where(first, pltpu.roll(pair, 64, 1), 0.0)
            + tap_rows(last, -1)
        )
        grown = mm(columns_ref[...], acc.astype(BF))
        for k in range(3):
            rows_ref[k] += blend[g + 2, k] * grown
        normed = (low_z_ref[g] - mean_l) * inverse_l
        pre = normed * low_gain[0:1] + low_gain[1:2]
        gate = jax.nn.sigmoid(pre)
        gp = low_in * (gate * (1.0 + pre * (1.0 - gate)))
        low_gp_ref[g] = gp
        sums[0] = sums[0] + column_sum(gp * normed)
        sums[1] = sums[1] + column_sum(gp)
    both = jnp.concatenate(sums, axis=0)
    sums_ref[...] = jnp.concatenate([both, jnp.zeros_like(both)], axis=1)


def conv_weight_kernel(keep, h_ref, taps_ref, out_ref):
    width = taps_ref.shape[1] // 3
    channels = out_ref.shape[1]
    low = lax.broadcasted_iota(jnp.int32, (channels, 128), 1) < 64
    grads = []
    for t in range(9):
        a, b = t // 3, t % 3
        acc = jnp.zeros((channels, 256), F32)
        for f in range(4):
            acc = acc + keep[f + 1, a] * mm_tn(
                h_ref[f + a, :, 0:channels] if channels < h_ref.shape[2] else h_ref[f + a],
                taps_ref[f, b * width : (b + 1) * width, :],
            )
        grads.append(acc)
        if t % 2 == 1 or t == 8:
            other = grads[t - 1] if t % 2 == 1 else acc
            mate = acc if t % 2 == 1 else jnp.zeros_like(acc)
            at = 128 * (t // 2)
            for j in range(2):
                x, y = other[:, 128 * j : 128 * j + 128], mate[:, 128 * j : 128 * j + 128]
                out_ref[2 * j, :, at : at + 128] = jnp.where(low, x, pltpu.roll(y, 64, 1)).astype(BF)
                out_ref[2 * j + 1, :, at : at + 128] = jnp.where(
                    low, pltpu.roll(x, 64, 1), y
                ).astype(BF)


def proj_back_sums_kernel(own_ref, above_ref, below_ref, z_ref, moments_ref, gain_ref, low_ref, gp_ref, payload_ref):
    normed = (z_ref[...] - moments_ref[0:1]) * moments_ref[1:2]
    pre = normed * gain_ref[0:1] + gain_ref[1:2]
    gate = jax.nn.sigmoid(pre)
    grad = own_ref[...] + above_ref[...] + below_ref[...]
    gp = grad * (gate * (1.0 + pre * (1.0 - gate)))
    gp_ref[...] = gp
    payload = jnp.concatenate([column_sum(gp * normed), column_sum(gp), low_ref[...]], axis=0)
    payload_ref[...] = jnp.broadcast_to(payload[None], payload_ref.shape)


def proj_back_kernel(
    counts,
    gp_ref,
    z_ref,
    landed_sums_ref,
    moments_ref,
    gain_ref,
    landed_ref,
    main_ref,
    pool_ref,
    out_ref,
    main_grad_ref,
    pool_grad_ref,
    total_ref,
):
    total = jnp.sum(landed_sums_ref[...], axis=0)
    total_ref[...] = total
    mean, inverse = moments_ref[0:1], moments_ref[1:2]
    normed = (z_ref[...] - mean) * inverse
    grad = grad_z(gp_ref[...], normed, gain_ref[0:1] * inverse, total, counts[0])
    columns = grad.shape[0]
    summed = column_sum(grad.astype(F32))
    high = summed.astype(BF).astype(F32)
    first = lax.broadcasted_iota(jnp.int32, (16, 256), 0) == 0
    high_rows = jnp.where(first, high, 0.0).astype(BF)
    low_rows = jnp.where(first, summed - high, 0.0).astype(BF)
    top = lax.broadcasted_iota(jnp.int32, (16, 128), 0)
    for s in range(out_ref.shape[0]):
        out_ref[s, 0:columns] = mm_nt(grad, main_ref[s]).astype(BF)
        pool = mm_nt(high_rows, pool_ref[s]) + mm_nt(low_rows, pool_ref[s])
        pool_high = pool[0:1].astype(BF).astype(F32)
        pair = jnp.where(top == 0, pool_high, jnp.where(top == 1, pool[0:1] - pool_high, 0.0))
        out_ref[s, columns : columns + 16] = pair.astype(BF)
        main_grad_ref[s] = mm_tn(landed_ref[s, 0:columns], grad).astype(BF)
        extra = landed_ref[s, columns : columns + 16]
        outer = mm_tn(extra, high_rows) + mm_tn(extra, low_rows)
        pool_grad_ref[s] = outer[0:32].astype(BF)


def spatial_back_sums_kernel(pixels, member, back_ref, spatial_ref, landed_ref, gains_ref, gp_ref, payload_ref):
    total = jnp.sum(landed_ref[...], axis=0)
    gains = gains_ref[...]
    mean, inverse = norm_of(total, pixels)
    columns = spatial_ref.shape[1]
    rows = [jnp.zeros((1, 128), F32), jnp.zeros((1, 128), F32)]
    pools = []
    for r in range(spatial_ref.shape[0]):
        normed = (spatial_ref[r] - mean) * inverse
        pre = normed * gains[0:1] + gains[1:2]
        gate = jax.nn.sigmoid(pre)
        gp = back_ref[r, 0:columns].astype(F32) * (gate * (1.0 + pre * (1.0 - gate)))
        gp_ref[r] = gp
        rows[0] = rows[0] + column_sum(gp * normed)
        rows[1] = rows[1] + column_sum(gp)
        pools.append(column_sum(back_ref[r, columns : columns + 16].astype(F32)))
    first = slot_mask((1, 128), 0)
    packed = [jnp.zeros((1, 128), F32), jnp.zeros((1, 128), F32)]
    for m in range(8):
        part = sum(member[r, m] * pools[r] for r in range(len(pools)))
        packed[m // 4] = packed[m // 4] + lane_roll(jnp.where(first, part, 0.0), 32 * (m % 4))
    payload = jnp.concatenate(rows + packed, axis=0)
    payload_ref[...] = jnp.broadcast_to(payload[None], payload_ref.shape)


def spatial_back_kernel(
    pixels, counts, gp_ref, spatial_ref, landed_ref, landed_back_ref, gains_ref, out_ref, pool_ref, gains_out_ref
):
    total = jnp.sum(landed_ref[...], axis=0)
    back = jnp.sum(landed_back_ref[...], axis=0)
    gains = gains_ref[...]
    mean, inverse = norm_of(total, pixels)
    scale = gains[0:1] * inverse
    for r in range(spatial_ref.shape[0]):
        normed = (spatial_ref[r] - mean) * inverse
        out_ref[r] = grad_z(gp_ref[r], normed, scale, back, pixels)
    normed, inverse_p, pre = pool_norm(total, counts, gains)
    gate = jax.nn.sigmoid(pre)
    gp = jnp.concatenate(pool_rows_of(back, 2), axis=0) * (gate * (1.0 + pre * (1.0 - gate)))
    gain_grad = column_sum(gp * normed)
    shift_grad = column_sum(gp)
    grad = gains[2:3] * inverse_p * (gp - (shift_grad + normed * gain_grad) / 8.0)
    pool_ref[...] = jnp.concatenate([grad[m : m + 1] / counts[m] for m in range(8)], axis=0)
    gains_out_ref[...] = jnp.concatenate([back[0:2], gain_grad, shift_grad], axis=0)


def aspp_back_kernel(
    place,
    keep,
    wide_ref,
    above_ref,
    below_ref,
    pool_ref,
    w_ref,
    feats_ref,
    grad_ref,
    weight_ref,
    reach_ref,
    spread_ref,
):
    height = wide_ref.shape[0]
    columns = wide_ref.shape[1]
    reach_ref[0:REACH] = above_ref[...]
    reach_ref[REACH : REACH + height] = wide_ref[...]
    reach_ref[REACH + height :] = below_ref[...]
    shape = (columns, 128)
    masks = [slot_mask(shape, slot) for slot in range(4)]
    ids = lax.broadcasted_iota(jnp.int32, shape, 0)

    @pl.loop(0, height)
    def _(r):
        own = reach_ref[REACH + r].astype(F32)
        start = pl.multiple_of(r * columns, columns)
        for k, d in enumerate(DILATIONS):
            mixed = jnp.zeros(shape, F32)
            for a in range(3):
                source = own if a == 1 else reach_ref[REACH + r - (a - 1) * d].astype(F32)
                moved = lane_roll(source, 32 * (a - k - 1)) * keep[3 * k + a, r]
                mixed = jnp.where(masks[a], moved, mixed)
            left = jnp.where(ids < columns - d, pltpu.roll(mixed, columns - d, 0), 0.0)
            right = jnp.where(ids >= d, pltpu.roll(mixed, d, 0), 0.0)
            if k == 0:
                mixed = jnp.where(masks[3], lane_roll(own, 96), mixed)
            if k == 1:
                window = lane_roll(pool_ref[pl.ds(r, 1), :], 96)
                mixed = jnp.where(masks[3], window, mixed)
            for j, value in enumerate((left, mixed, right)):
                at = 128 * (3 * k + j)
                spread_ref[pl.ds(start, columns), at : at + 128] = value.astype(BF)

    n_y = feats_ref.shape[0] // 2
    block = grad_ref.shape[2]
    strip = 2 * block
    base = pl.multiple_of(place[0] * strip, strip)
    depth = grad_ref.shape[3]

    @pl.loop(0, 2 * n_y)
    def _(i):
        part = pl.multiple_of(base + (i // n_y) * block, block)
        deep = pl.multiple_of((i % n_y) * depth, depth)
        grad_ref[i // n_y, i % n_y] = mm_nt(
            spread_ref[pl.ds(part, block), :], w_ref[pl.ds(deep, depth), :]
        ).astype(BF)

    wide = feats_ref.shape[2]

    @pl.loop(0, n_y)
    def _(y):
        acc = jnp.zeros((wide, spread_ref.shape[1]), F32)
        for core in range(2):
            for x in range(spread_ref.shape[0] // strip):
                acc = acc + mm_tn(
                    feats_ref[core * n_y + y, x * block : (x + 1) * block, :],
                    spread_ref[x * strip + core * block : x * strip + (core + 1) * block, :],
                )
        weight_ref[pl.ds(pl.multiple_of(y * wide, wide), wide), :] = acc.astype(BF)


def on_device(
    features,
    low_level,
    labels,
    crop_rows,
    w_one,
    w_atrous,
    w_pool,
    w_proj,
    w_low,
    w_unite_up,
    w_unite_low,
    w_refine,
    w_classes,
    b_classes,
    gain_aspp,
    shift_aspp,
    gain_proj,
    shift_proj,
    gain_low,
    shift_low,
    gain_dec,
    shift_dec,
):
    n_y, n_z, n_x = lax.axis_size("y"), lax.axis_size("z"), lax.axis_size("x")
    core, yi, xi, zi = (lax.axis_index(a) for a in ("core", "y", "x", "z"))
    strip = lax.axis_index(STRIP)
    row = lax.axis_index(ALL)
    groups = lax.axis_size(ROWS)
    rows_in, columns, c_part = features.shape
    total_rows = rows_in * groups
    c_in = c_part * n_y
    fine_strip, c_low, fine_columns = low_level.shape
    fine_total = fine_strip * groups
    branch = w_proj.shape[1] * n_y
    o_part = w_one.shape[1]
    half = o_part // 2
    low_out = w_low.shape[1] * n_y
    classes = w_classes.shape[1]
    images = crop_rows.shape[0]
    pixels = float(total_rows * columns)
    fine_pixels = float(fine_total * fine_columns)
    image_ends = jnp.cumsum(crop_rows)
    fine_ends = 4 * image_ends
    counts = crop_rows.astype(F32) * float(columns)
    tall = 2 * rows_in
    rows8 = strip * tall + jnp.arange(tall, dtype=jnp.int32)

    counts_static = (pixels, fine_pixels)
    rows3 = row - 1 + jnp.arange(3, dtype=jnp.int32)
    fine8 = 4 * row - 2 + jnp.arange(8, dtype=jnp.int32)
    fine6, fine4 = fine8[1:7], fine8[2:6]
    inside = ((fine8 >= 0) & (fine8 < fine_total)).astype(F32)
    keep = jnp.stack([same_image(fine6, a - 1, fine_ends, fine_total) for a in range(3)], axis=1)
    keep_back = jnp.stack(
        [same_image(fine4 - (a - 1), a - 1, fine_ends, fine_total) for a in range(3)], axis=1
    )
    row_blend = blend_matrix(fine8, rows3, image_ends, total_rows)
    column_blend = blend_matrix(
        jnp.arange(fine_columns, dtype=jnp.int32),
        jnp.arange(columns, dtype=jnp.int32),
        jnp.zeros((1,), jnp.int32),
        columns,
    )
    columns_up = jnp.concatenate([shifted(column_blend, b, 0) for b in (-1, 0, 1)], axis=0)
    columns_up = jnp.concatenate([columns_up, columns_up], axis=1).astype(BF)
    columns_back = column_blend.T.astype(BF)
    up = jnp.stack([same_image(rows8, -d, image_ends, total_rows) for d in DILATIONS])
    down = jnp.stack([same_image(rows8, d, image_ends, total_rows) for d in DILATIONS])
    crops = jnp.arange(images, dtype=jnp.int32)
    member = (image_of(rows8, image_ends)[:, None] == crops[None, :]).astype(F32)

    feats = lax.all_gather(features.reshape(-1, c_part), GROUP, axis=0, tiled=False)

    atrous = w_atrous.transpose(0, 1, 3, 2, 4).reshape(w_one.shape[0], 27, o_part)
    own = jnp.concatenate([atrous, w_one[:, None], w_pool[:, None]], axis=1)
    paired = lax.all_to_all(own, "core", 2, 0, tiled=True)
    weights = lax.all_gather(paired.reshape(paired.shape[0], -1), STRIP, axis=0, tiled=True)

    vectors = [gain_dec, shift_dec, gain_proj, shift_proj, gain_low, shift_low]
    flat = jnp.concatenate([jnp.ravel(v) for v in vectors])
    flat = gathered(jnp.pad(flat, (0, -flat.shape[0] % 128)).reshape(-1, 128), "y").reshape(n_y, -1)
    whole, at = [], 0
    for v in vectors:
        piece = flat[:, at : at + v.size].reshape((n_y,) + v.shape)
        whole.append(jnp.moveaxis(piece, 0, -2).reshape(v.shape[:-1] + (-1,)))
        at += v.size
    gain_1, gain_2 = (jnp.stack([whole[0][i], whole[1][i]]) for i in range(2))
    gain_p = jnp.stack([whole[2], whole[3]])
    gain_l = jnp.pad(jnp.stack([whole[4], whole[5]]), ((0, 0), (0, 128 - low_out)))
    halves = jnp.stack([gain_aspp, shift_aspp])
    halves = lax.dynamic_slice_in_dim(halves, core * half, half, 2)
    gains_sp = jnp.concatenate(
        [
            halves[:, :4].reshape(2, -1),
            jnp.pad(halves[:, 4], ((0, 0), (0, 3 * half))),
        ]
    )

    def beside(block):
        parts = gathered(block.reshape(-1, 128), "y").reshape((n_y,) + block.shape)
        return jnp.moveaxis(parts, 0, -2).reshape(block.shape[:-1] + (-1,))

    k_row = w_refine.shape[0]
    shard = jnp.concatenate(
        [
            w_unite_up.reshape(k_row, 9, o_part),
            w_refine.reshape(k_row, 9, o_part),
            w_proj.reshape(k_row, -1, o_part),
            jnp.pad(w_low, ((0, 0), (0, o_part - w_low.shape[1])))[:, None],
        ],
        axis=1,
    )
    shard = jnp.pad(shard, ((0, 0), (0, -shard.shape[1] % 2), (0, 0)))
    dec = lax.all_gather(beside(shard).reshape(k_row, -1), ROWS, axis=0, tiled=True)
    up_w = dec[:, : 9 * branch]
    refine_w = dec[:, 9 * branch : 18 * branch]
    proj_rows = w_proj.shape[0] // k_row
    proj_w = dec[:, 18 * branch : (18 + proj_rows) * branch].reshape(-1, branch)
    shrink = dec[:, (18 + proj_rows) * branch : (19 + proj_rows) * branch]
    shrink = shrink.reshape(c_low, n_y, o_part)[:, :, : w_low.shape[1]].reshape(c_low, low_out)
    shrink = jnp.pad(shrink, ((0, 0), (0, 128 - low_out)))
    low_w9 = beside(w_unite_low.reshape(-1, o_part)).reshape(low_out, 3, 3, branch)
    low_w9 = low_w9.transpose(1, 2, 0, 3)
    low_w = jnp.pad(low_w9, ((0, 0), (0, 0), (0, 64 - low_out), (0, 0)))
    low_w = jnp.pad(low_w.reshape(3, 192, branch), ((0, 0), (0, 64), (0, 0)))
    classes_w = jnp.pad(gathered(w_classes, "y").reshape(branch, classes).T, ((0, 32 - classes), (0, 0)))
    class_bias = jnp.pad(b_classes[:, None], ((0, 32 - classes), (0, 127)))
    main_w = proj_w[: 4 * branch].reshape(4, n_y, 2, half, branch).transpose(2, 1, 0, 3, 4)
    main_w = main_w.reshape(2 * n_y, 4 * half, branch)
    pool_w = proj_w[4 * branch :].reshape(n_y, 2, half, branch).transpose(1, 0, 2, 3)
    pool_w = jnp.pad(pool_w.reshape(2 * n_y, half, branch), ((0, 0), (0, 3 * half), (0, 0)))

    low_own = lax.dynamic_slice_in_dim(low_level, yi * 4, 4, 0)
    labels_own = lax.dynamic_slice_in_dim(labels, yi * 4, 4, 0)
    low_z = dot("fcv,co->fvo", low_own, shrink)
    low_above = hop_open(low_z[2:].astype(BF), ALL, 1)
    low_below = hop_open(low_z[:2].astype(BF), ALL, -1)
    low_sums = jnp.stack([jnp.sum(low_z, axis=(0, 1)), jnp.sum(jnp.square(low_z), axis=(0, 1))])
    low_sums = jnp.pad(low_sums, ((0, 0), (0, branch - 128)))

    digits = features.reshape(rows_in, columns, c_part // (n_x * o_part), n_x, o_part)
    digits = jnp.moveaxis(digits, 3, 0).reshape(n_x, rows_in * columns, -1)
    by_x = lax.all_to_all(digits, "x", 0, 0, tiled=True)
    feats_x = lax.all_gather(by_x.reshape(-1, by_x.shape[2]), GROUP, axis=0, tiled=False)

    wide_c = 4 * half
    edge10, edge2 = ((10, columns, wide_c), BF), ((2, columns, wide_c), BF)
    part = ((tall, columns, wide_c), F32)
    padded_w, a0, a1, a2, p1, p2, p3, m1, m2, m3 = run_kernel(
        product_kernel,
        [],
        [feats, weights],
        [((c_in, 9 * wide_c), BF), part, part, part, edge10, edge10, edge2, edge10, edge10, edge2],
        [((tall * columns, 9 * wide_c), F32)],
    )
    edges = [
        hop_open(p1, STRIP, -1),
        hop_open(p2, STRIP, -2),
        hop_open(p3, STRIP, -3),
        hop_open(m1, STRIP, 1),
        hop_open(m2, STRIP, 2),
        hop_open(m3, STRIP, 3),
    ]
    n_strips = n_z * n_x
    spatial, payload = run_kernel(
        spatial_kernel,
        [up, down, member],
        [a0, a1, a2] + edges,
        [part, ((n_strips, 4, wide_c), F32)],
    )
    landed_sp = lax.all_to_all(payload, STRIP, 0, 0, tiled=True)
    (payload,) = run_kernel(
        functools.partial(act_kernel, pixels),
        [counts, member],
        [spatial, landed_sp, gains_sp],
        [((tall, columns + 16, wide_c), BF)],
    )

    landed = lax.all_to_all(payload, GROUP, 0, 0, tiled=True)
    n_first = 2 * n_x * n_y
    proj_z, payload = run_kernel(
        proj_kernel,
        [],
        [landed, main_w, pool_w, low_sums],
        [((columns, branch), F32), ((n_first, 4, branch), F32)],
    )

    def exchanged(block):
        block = lax.all_to_all(block, ("x", "core", "y"), 0, 0, tiled=True)
        block = jnp.broadcast_to(jnp.sum(block, axis=0)[None], (n_z,) + block.shape[1:])
        return lax.all_to_all(block, "z", 0, 0, tiled=True)

    proj_above = hop_open(proj_z, ALL, 1)
    proj_below = hop_open(proj_z, ALL, -1)
    landed_p = exchanged(payload)

    fine = (fine_columns, branch)
    sums2, sums4 = ((n_first, 2, branch), F32), ((n_first, 4, branch), F32)
    united_z, united_up, low_act, payload, moments_0 = run_kernel(
        functools.partial(unite_kernel, counts_static),
        [row_blend, keep, inside],
        [
            proj_z,
            proj_above,
            proj_below,
            landed_p,
            gain_p,
            low_z,
            low_above,
            low_below,
            gain_l,
            columns_up,
            up_w,
            low_w,
        ],
        [
            ((6,) + fine, F32),
            ((6,) + fine, BF),
            ((6, fine_columns, 128), BF),
            sums2,
            ((4, branch), F32),
        ],
        [
            ((8, 3 * fine_columns, branch), BF),
            ((8, fine_columns, 256), BF),
            ((3, columns, branch), F32),
            ((8, fine_columns, 128), F32),
        ],
    )
    landed_1 = exchanged(payload)
    hidden, refine_z, payload, moments_1 = run_kernel(
        functools.partial(refine_kernel, counts_static),
        [keep, inside],
        [united_z, landed_1, gain_1, refine_w],
        [((6,) + fine, BF), ((4,) + fine, F32), sums2, ((2, branch), F32)],
        [((6, 3 * fine_columns, branch), BF)],
    )
    landed_2 = exchanged(payload)
    edge = ((2,) + fine, BF)
    gp_2, payload, moments_2, top, bottom, classes_part = run_kernel(
        functools.partial(classes_kernel, images, classes, counts_static),
        [],
        [refine_z, landed_2, gain_2, labels_own, classes_w, class_bias],
        [((4,) + fine, F32), sums4, ((2, branch), F32), edge, edge, ((32, branch), F32)],
    )
    edge_above = hop_open(top, ALL, 1)
    edge_below = hop_open(bottom, ALL, -1)
    landed_g2 = exchanged(payload)
    edge = (fine, BF)
    gp_1, taps_2, payload, top, bottom = run_kernel(
        functools.partial(refine_back_kernel, counts_static),
        [keep_back, inside],
        [
            gp_2,
            refine_z,
            edge_above,
            edge_below,
            landed_g2,
            moments_2,
            gain_2,
            refine_w,
            united_z,
            moments_1,
            gain_1,
        ],
        [((4,) + fine, F32), ((4, 3 * fine_columns, branch), BF), sums2, edge, edge],
        [((2, 3 * fine_columns, branch), BF)],
    )
    edge_above = hop_open(top, ALL, 1)
    edge_below = hop_open(bottom, ALL, -1)
    landed_g1 = exchanged(payload)
    grad_lanes = 5 * 2 * o_part
    (refine_part,) = run_kernel(
        conv_weight_kernel, [keep], [hidden, taps_2], [((n_y, branch, grad_lanes), BF)]
    )
    taps_1, to_rows, gp_l, low_back = run_kernel(
        functools.partial(unite_back_kernel, counts_static),
        [keep_back, inside, row_blend],
        [
            gp_1,
            united_z,
            edge_above,
            edge_below,
            landed_g1,
            moments_1,
            gain_1,
            up_w,
            low_w,
            columns_back,
            low_z,
            moments_0,
            gain_l,
        ],
        [
            ((4, 3 * fine_columns, branch), BF),
            ((3, columns, branch), F32),
            ((4, fine_columns, 128), F32),
            ((2, branch), F32),
        ],
        [((2, 3 * fine_columns, branch), BF), ((6,) + fine, BF)],
    )
    (up_part,) = run_kernel(
        conv_weight_kernel, [keep], [united_up, taps_1], [((n_y, branch, grad_lanes), BF)]
    )
    (low_part,) = run_kernel(
        conv_weight_kernel, [keep], [low_act, taps_1], [((n_y, 128, grad_lanes), BF)]
    )

    to_above = hop_open(to_rows[0], ALL, -1)
    to_below = hop_open(to_rows[2], ALL, 1)
    gp_p, payload = run_kernel(
        proj_back_sums_kernel,
        [],
        [to_rows[1], to_above, to_below, proj_z, moments_0, gain_p, low_back],
        [((columns, branch), F32), sums4],
    )
    landed_gp = exchanged(payload)
    payload, main_part, pool_part, total_p = run_kernel(
        functools.partial(proj_back_kernel, counts_static),
        [],
        [gp_p, proj_z, landed_gp, moments_0, gain_p, landed, main_w, pool_w],
        [
            ((2 * n_y, columns + 16, wide_c), BF),
            ((2 * n_y, wide_c, branch), BF),
            ((2 * n_y, half, branch), BF),
            ((4, branch), F32),
        ],
    )
    back = lax.all_to_all(payload, GROUP, 0, 0, tiled=True)
    gp_sp, payload = run_kernel(
        functools.partial(spatial_back_sums_kernel, pixels),
        [member],
        [back, spatial, landed_sp, gains_sp],
        [part, ((n_strips, 4, wide_c), F32)],
    )
    landed_gsp = lax.all_to_all(payload, STRIP, 0, 0, tiled=True)
    grad_sp, pool_grad, gain_grads = run_kernel(
        functools.partial(spatial_back_kernel, pixels),
        [counts],
        [gp_sp, spatial, landed_sp, landed_gsp, gains_sp],
        [((tall, columns, wide_c), BF), ((8, wide_c), F32), ((4, wide_c), F32)],
    )

    group_rows = n_x * tall
    wide = gathered(grad_sp, "x").reshape(group_rows, columns, wide_c)
    reach_above = hop_open(wide[group_rows - REACH :], "z", 1)
    reach_below = hop_open(wide[:REACH], "z", -1)
    ids = zi * group_rows + jnp.arange(group_rows, dtype=jnp.int32)
    keep_group = jnp.stack(
        [
            same_image(ids - (a - 1) * d, (a - 1) * d, image_ends, total_rows)
            for d in DILATIONS
            for a in range(3)
        ]
    )
    member_group = (image_of(ids, image_ends)[:, None] == crops[None, :]).astype(F32)
    pool_window = jnp.dot(member_group, pool_grad, precision=PRECISE)
    grad_feats, aspp_part = run_kernel(
        aspp_back_kernel,
        [xi.astype(jnp.int32)[None], keep_group],
        [wide, reach_above, reach_below, pool_window, padded_w, feats_x],
        [
            ((2, n_y, rows_in * columns, c_part), BF),
            ((c_in // n_x, 9 * wide_c), BF),
        ],
        [
            ((group_rows + 2 * REACH, columns, wide_c), BF),
            ((group_rows * columns, 9 * wide_c), BF),
        ],
        limit=52,
    )

    mine = lax.dynamic_index_in_dim(grad_feats, core, 0, keepdims=False)
    theirs = hop(lax.dynamic_index_in_dim(grad_feats, 1 - core, 0, keepdims=False), "core", 1)
    paired = mine.astype(F32) + theirs.astype(F32)
    grad_features = scattered(paired, "y").reshape(features.shape)

    aspp_sum = lax.all_to_all(aspp_part.reshape(n_z, o_part, -1), "z", 0, 0, tiled=True)
    aspp_sum = jnp.sum(aspp_sum.astype(F32), axis=0).reshape(2, half, -1)
    mine = lax.dynamic_index_in_dim(aspp_sum, core, 0, keepdims=False)
    theirs = hop(lax.dynamic_index_in_dim(aspp_sum, 1 - core, 0, keepdims=False).astype(BF), "core", 1)
    theirs = theirs.astype(F32)
    pair = jnp.stack([jnp.where(core == 0, mine, theirs), jnp.where(core == 0, theirs, mine)], axis=1)
    pair = pair.reshape(half, 2, 3, 3, 4, half)
    grad_atrous = pair[:, :, :, :, :3].transpose(0, 2, 4, 3, 1, 5).reshape(w_atrous.shape)
    grad_one = pair[:, :, 0, 1, 3].reshape(w_one.shape)
    grad_pool = pair[:, :, 1, 1, 3].reshape(w_pool.shape)

    mean_l, inverse_l = moments_0[2, :128], moments_0[3, :128]
    normed_l = (low_z - mean_l) * inverse_l
    grad_low_z = (
        gain_l[0] * inverse_l * (gp_l - (total_p[3, :128] + normed_l * total_p[2, :128]) / fine_pixels)
    ).astype(BF)[:, :, :low_out]
    shrink_part = dot("fcv,fvo->co", low_own, grad_low_z)
    grad_low_all = gathered(grad_low_z.transpose(0, 2, 1), "y").reshape(fine_strip, low_out, fine_columns)
    shrink_own = lax.dynamic_slice_in_dim(shrink, yi * (c_low // n_y), c_low // n_y, 0)
    grad_low_level = dot("fov,co->fcv", grad_low_all, shrink_own[:, :low_out])

    def owned(part):
        return jnp.sum(lax.all_to_all(part.astype(BF), ROWS, 0, 0, tiled=True).astype(F32), axis=0)

    refine_sum = scattered(refine_part, "y")
    up_sum = scattered(up_part, "y")
    low_sum = scattered(low_part[:, :low_out], "y")[:, : 9 * o_part]
    class_sum = scattered(classes_part[:classes].T.reshape(n_y, -1, classes), "y")
    decoder_sum = owned(
        jnp.concatenate(
            [
                refine_sum.reshape(groups, -1),
                up_sum.reshape(groups, -1),
                low_sum.reshape(groups, -1),
                class_sum.reshape(groups, -1),
            ],
            axis=1,
        )
    )
    size_9 = k_row * grad_lanes

    def conv_grad(flat):
        return flat.reshape(k_row, grad_lanes)[:, : 9 * o_part].reshape(w_refine.shape)

    grad_refine = conv_grad(decoder_sum[:size_9])
    grad_unite_up = conv_grad(decoder_sum[size_9 : 2 * size_9])
    rest = decoder_sum[2 * size_9 :]
    size_low = low_out * 9 * o_part // groups
    rest = lax.all_to_all(
        jnp.broadcast_to(rest[None], (groups,) + rest.shape), ROWS, 0, 0, tiled=True
    )
    grad_unite_low = rest[:, :size_low].reshape(w_unite_low.shape)
    grad_classes = rest[:, size_low:].reshape(w_classes.shape)
    main_part = main_part.reshape(2, n_y, 4, half, branch).transpose(2, 1, 0, 3, 4)
    pool_part = pool_part.reshape(2, n_y, half, branch).transpose(1, 0, 2, 3)
    proj_part = jnp.concatenate([main_part.reshape(-1, branch), pool_part.reshape(-1, branch)])
    proj_sum = scattered(jnp.moveaxis(proj_part.reshape(-1, n_y, o_part), 1, 0), "y")
    shrink_sum = scattered(jnp.moveaxis(shrink_part.reshape(c_low, n_y, -1), 1, 0), "y")
    late_sum = owned(
        jnp.concatenate([proj_sum.reshape(groups, -1), shrink_sum.reshape(groups, -1)], axis=1)
    )
    size_p = w_proj.size
    grad_proj = late_sum[:size_p].reshape(w_proj.shape)
    grad_shrink = late_sum[size_p:].reshape(w_low.shape)

    total_2 = jnp.sum(landed_g2, axis=0)
    total_1 = jnp.sum(landed_g1, axis=0)
    grad_bias = total_2[2, :classes]
    loss_value = jnp.sum(total_2[3]) / images
    both = gathered(gain_grads, "core")
    both = both.reshape(2, 2, 2, 4, half)
    both = jnp.concatenate([both[:, 0], both[:, 1, :, :1]], axis=2)
    both = both.transpose(1, 2, 0, 3).reshape(2, 5, o_part)

    def own_channels(vector):
        size = vector.shape[-1] // n_y
        return lax.dynamic_slice_in_dim(vector, yi * size, size, vector.ndim - 1)

    return (
        loss_value,
        grad_features,
        grad_low_level,
        grad_one,
        grad_atrous,
        grad_pool,
        grad_proj,
        grad_shrink,
        grad_unite_up,
        grad_unite_low,
        grad_refine,
        grad_classes,
        grad_bias,
        both[0],
        both[1],
        own_channels(total_p[0]),
        own_channels(total_p[1]),
        own_channels(total_p[2, :low_out]),
        own_channels(total_p[3, :low_out]),
        own_channels(jnp.stack([total_1[0], total_2[0]])),
        own_channels(jnp.stack([total_1[1], total_2[1]])),
    )


def solution(mesh):
    torus = Mesh(mesh.devices.reshape(8, 4, 2, mesh.shape["ch"]), ALL)
    in_specs = (
        P(ROWS, None, "y"),
        P(ROWS, None, None),
        P(ROWS, None),
        P(),
        P(ROWS, "y"),
        P(ROWS, None, None, None, "y"),
        P(ROWS, "y"),
        P(ROWS, "y"),
        P(ROWS, "y"),
        P(ROWS, None, None, "y"),
        P(None, None, None, "y"),
        P(ROWS, None, None, "y"),
        P("y", None),
        P(),
        P(None, "y"),
        P(None, "y"),
        P("y"),
        P("y"),
        P("y"),
        P("y"),
        P(None, "y"),
        P(None, "y"),
    )
    out_specs = (
        P(),
        P(ROWS, None, "y"),
        P(ROWS, "y", None),
        P(ROWS, "y"),
        P(ROWS, None, None, None, "y"),
        P(ROWS, "y"),
        P(ROWS, "y"),
        P(ROWS, "y"),
        P(ROWS, None, None, "y"),
        P(None, None, None, "y"),
        P(ROWS, None, None, "y"),
        P("y", None),
        P(),
        P(None, "y"),
        P(None, "y"),
        P("y"),
        P("y"),
        P("y"),
        P("y"),
        P(None, "y"),
        P(None, "y"),
    )
    return jax.shard_map(
        on_device, mesh=torus, in_specs=in_specs, out_specs=out_specs, check_vma=False
    )
```

time: 1000 us -> 787 us (0.79)
  waiting for transfers between devices: 59.1 us -> 188 us
  blocking collectives: 116 us -> 6.71 us
  starting transfers between devices: 332 us -> 248 us
  local copies, waits for them, and re-layouts: 276 us -> 199 us
  other arithmetic: 126 us -> 51.1 us
  Pallas kernels: 0 us -> 56.7 us
  matrix products: 55.3 us -> 5.42 us
    all_gather x3 -> x0, blocking collectives: 110 us -> none  [the longest x2 102 us: on_device(): lax.all_gather(block, ROWS, axis=0, tiled=True)]
    all_gather x1, waiting for transfers between devices: 0.01 us -> 80.3 us  [on_device(): lax.all_gather(paired.reshape(paired.shape[0], -1), STRIP, axis=0, tiled=...]
    ppermute x52 -> x42, starting transfers between devices: 127 us -> 54.6 us  [hop(): lax.ppermute(block, axes, [(i, (i + distance) % n) for i in range(n)])]
    pallas_call x0 -> x17, Pallas kernels: none -> 56.7 us  [run_kernel(): pl.pallas_call(body, out_shape=[jax.ShapeDtypeStruct(shape, kind) for sha...]
    dot_general x31 -> x3, matrix products: 44.2 us -> 5.24 us  [dot(): return jnp.einsum(spec, a, b, preferred_element_type=F32)]
    another operation x33 -> x18, local copies, waits for them, and re-layouts: 44.2 us -> 7.05 us  [the longest x3 3.4 us: on_device(): jnp.stack([jnp.where(core == 0, mine, theirs), jnp.where(core == 0, their...]
    unnamed x401 -> x283, local copies, waits for them, and re-layouts: 53.3 us -> 85.5 us
    all_gather x4 -> x3, waiting for transfers between devices: 0.03 us -> 30.9 us  [the longest x1 30.9 us: on_device(): lax.all_gather(beside(shard).reshape(k_row, -1), ROWS, axis=0, tiled=True)]
  transfers between devices with their start and end apart: 95 -> 85, of which waited for: 19 -> 18; matrix products, arithmetic and copies ran while one was open for 43% -> 23% of each run, Pallas kernels for 0% -> 7%
where the time goes in v2:
time: 787 us; the launch traced here: 773 us
  starting transfers between devices  248 us (32%)
  local copies, waits for them, and re-layouts  199 us (25%)
  waiting for transfers between devices  188 us (24%)
  Pallas kernels  56.7 us (7%)
  other arithmetic  51.1 us (6%)
  between operations  18.2 us (2%)
    unnamed x283, local copies, waits for them, and re-layouts  85.5 us
    all_gather x1, waiting for transfers between devices, on_device(): lax.all_gather(paired.reshape(paired.shape[0], -1), STRIP, axis=0, tiled=...  80.3 us
    ppermute x18, starting transfers between devices, hop_open(): return lax.ppermute(block, axes, route)  56.9 us
    pallas_call x17, Pallas kernels, run_kernel(): pl.pallas_call(body, out_shape=[jax.ShapeDtypeStruct(shape, kind) for sha...  56.7 us
    ppermute x42, starting transfers between devices, hop(): lax.ppermute(block, axes, [(i, (i + distance) % n) for i in range(n)])  54.6 us
    all_to_all x6, starting transfers between devices, exchanged(): block = lax.all_to_all(block, ('x', 'core', 'y'), 0, 0, tiled=True)  44.5 us
    all_gather x1, waiting for transfers between devices, on_device(): lax.all_gather(beside(shard).reshape(k_row, -1), ROWS, axis=0, tiled=True)  30.9 us
    all_to_all x6, starting transfers between devices, exchanged(): return lax.all_to_all(block, 'z', 0, 0, tiled=True)  27.3 us
  transfers between devices with their start and end apart: 85, of which 18 were waited for; matrix products, arithmetic and copies ran while one was open for 23% of the time, Pallas kernels for 7%

profile of v2, /device:TPU:1, one launch (start us, length us, event | category | flops | bytes accessed | tf_op | source)
XLA Modules:
  0.0 772.6 jit_solution(15928273225217370218)
XLA Ops:
  10.9 6.7 all_to_all.126
  46.3 80.3 %all-gather.8.cloned.1.call-done.w_ref = bf16[2048,928]{1,0:T(8,128)(2,1)} async-done(((bf16[64,928]{1,0:T(8,128)(2,1)}), bf16[2048,928]{1,0:T(8,128)(2,1)}) %all-gather.8.cloned.1.call-update) | async-done | bytes 3801104 | tf_op jit(solution)/shard_map/all_gather | solution.py:978
  130.3 6.7 shard_map.373
  141.8 5.2 collective-permute-start.5
  155.4 6.1 collective-permute-start.4
  167.5 8.8 %all-to-all-start.1 = ((f32[32,4,128]{2,1,0:T(4,128)}), f32[32,4,128]{2,1,0:T(4,128)S(1)}, u32[]{:S(2)}, u32[]{:S(2)}) async-start(f32[32,4,128]{2,1,0:T(4,128)} %get-tuple-element.82), calls=%async_computation.1 | async-start | bytes 131072 | tf_op jit(solution)/shard_map/all_to_all | solution.py:1072
  177.7 30.9 %all-gather.12.cloned.1.call-done = bf16[64,4,6144]{2,1,0:T(4,128)(2,1)} async-done(((bf16[1,4,6144]{2,1,0:T(4,128)(2,1)}), bf16[64,4,6144]{2,1,0:T(4,128)(2,1)}) %all-gather.12.cloned.1.call-update) | async-done | bytes 3145744 | tf_op jit(solution)/shard_map/all_gather | solution.py:1015
  208.6 5.7 reshape.1165
  228.1 4.9 all-to-all-start.3
  277.6 6.9 shard_map.377
  288.2 6.9 all-to-all-start.5
  308.8 8.1 %all-to-all-start.6 = ((f32[8,2,256]{2,1,0:T(2,128)}), f32[8,2,256]{2,1,0:T(2,128)}, u32[]{:S(2)}, u32[]{:S(2)}) async-start(f32[8,2,256]{2,1,0:T(2,128)} %broadcast_in_dim.160), calls=%async_computation.6 | async-start | bytes 32768 | tf_op jit(solution)/shard_map/all_to_all | solution.py:1092
  316.9 6.7 all-to-all-done.6.landed_ref
  334.2 8.7 %all-to-all-start.7 = ((f32[32,2,256]{2,1,0:T(2,128)}), f32[32,2,256]{2,1,0:T(2,128)}, u32[]{:S(2)}, u32[]{:S(2)}) async-start(f32[32,2,256]{2,1,0:T(2,128)} %copy-done.61), calls=%async_computation.7 | async-start | bytes 131072 | tf_op jit(solution)/shard_map/all_to_all | solution.py:1090
  343.8 6.5 all-to-all-done.7
  358.2 5.3 all-to-all-done.8.landed_ref
  373.2 5.9 all-to-all-start.9
  428.5 8.9 %all-to-all-start.11 = ((f32[32,2,256]{2,1,0:T(2,128)}), f32[32,2,256]{2,1,0:T(2,128)}, u32[]{:S(2)}, u32[]{:S(2)}) async-start(f32[32,2,256]{2,1,0:T(2,128)} %copy-done.60), calls=%async_computation.11 | async-start | bytes 131072 | tf_op jit(solution)/shard_map/all_to_all | solution.py:1090
  479.9 5.0 collective-permute-start.26
  500.4 9.1 %all-to-all-start.13 = ((f32[32,4,256]{2,1,0:T(4,128)}), f32[32,4,256]{2,1,0:T(4,128)}, u32[]{:S(2)}, u32[]{:S(2)}) async-start(f32[32,4,256]{2,1,0:T(4,128)} %copy-done.49), calls=%async_computation.13 | async-start | bytes 262144 | tf_op jit(solution)/shard_map/all_to_all | solution.py:1090
  537.3 5.8 all-to-all-start.15
  554.6 6.5 constant_dynamic-slice_fusion.19
  588.6 8.4 %concatenate.81 = bf16[64,1,5573]{2,1,0:T(2,128)(2,1)} concatenate(bf16[64,1,2560]{2,1,0:T(2,128)(2,1)} %concatenate.83, bf16[64,1,2560]{2,1,0:T(2,128)(2,1)S(1)} %concatenate.84, bf16[64,1,432]{2,1,0:T(2,128)(2,1)} %concatenate.85, bf16[64,1,21]{2,1,0:T(2,128)(2,1)} %copy.417), dimensions={2} | concatenate | bytes 1426688 | tf_op jit(solution)/shard_map/concatenate | solution.py:1308
  602.5 8.1 %all-to-all-start.16 = ((f32[32,4,128]{2,1,0:T(4,128)}), f32[32,4,128]{2,1,0:T(4,128)S(1)}, u32[]{:S(2)}, u32[]{:S(2)}) async-start(f32[32,4,128]{2,1,0:T(4,128)} %get-tuple-element.106), calls=%async_computation.16 | async-start | bytes 131072 | tf_op jit(solution)/shard_map/all_to_all | solution.py:1237
  619.5 10.3 %all-to-all-start.20 = ((bf16[64,1,5573]{2,1,0:T(2,128)(2,1)}), bf16[64,1,5573]{2,1,0:T(2,128)(2,1)}, u32[]{:S(2)}, u32[]{:S(2)}) async-start(bf16[64,1,5573]{2,1,0:T(2,128)(2,1)} %concatenate.81), calls=%async_computation.20 | async-start | bytes 2883584 | tf_op jit(solution)/shard_map/all_to_all | solution.py:1301
  643.3 7.9 %collective-permute-done.29 = bf16[8,64,128]{2,1,0:T(8,128)(2,1)S(1)} collective-permute-done((bf16[8,64,128]{2,1,0:T(8,128)(2,1)S(1)}, bf16[8,64,128]{2,1,0:T(8,128)(2,1)S(1)}, u32[]{:S(2)}, u32[]{:S(2)}) %collective-permute-start.29) | collective-permute-done | bytes 131104 | tf_op jit(solution)/shard_map/ppermute | solution.py:26
  651.3 14.7 %all-to-all-done.20 = bf16[64,1,5573]{2,1,0:T(2,128)(2,1)} async-done(((bf16[64,1,5573]{2,1,0:T(2,128)(2,1)}), bf16[64,1,5573]{2,1,0:T(2,128)(2,1)}, u32[]{:S(2)}, u32[]{:S(2)}) %all-to-all-start.20) | async-done | bytes 713376 | tf_op jit(solution)/shard_map/all_to_all | solution.py:1301
  666.1 6.3 all-to-all-start.19
  685.1 9.4 %all-to-all-start.21 = ((f32[64,1,453]{2,1,0:T(1,128)}), f32[64,1,453]{2,1,0:T(1,128)}, u32[]{:S(2)}, u32[]{:S(2)}) async-start(f32[64,1,453]{2,1,0:T(1,128)} %broadcast_in_dim.339), calls=%async_computation.21 | async-start | bytes 262144 | tf_op jit(solution)/shard_map/all_to_all | solution.py:1327
  697.7 15.9 %shard_map.386 = (bf16[2,4,256,512]{3,2,1,0:T(8,128)(2,1)}, bf16[512,1152]{1,0:T(8,128)(2,1)}) custom-call(s32[1]{0:T(128)} %bitcast.57.place, f32[9,32]{1,0:T(8,128)S(1)} %copy-done.73, bf16[32,64,128]{2,1,0:T(8,128)(2,1)S(1)} %bitcast.327, bf16[18,64,128]{2,1,0:T(8,128)(2,1)S(1)} %collective-permute-done.31.above_ref, ...), custom_call_target="tpu_custom_call" | custom-call | tf_op jit(solution)/shard_map/pallas_call | solution.py:156
  713.6 6.5 all-to-all-start.18
  738.5 13.8 %all-to-all-done.18 = bf16[8,64,1152]{2,1,0:T(8,128)(2,1)} async-done(((bf16[8,64,1152]{2,1,0:T(8,128)(2,1)}), bf16[8,64,1152]{2,1,0:T(8,128)(2,1)}, u32[]{:S(2)}, u32[]{:S(2)}) %all-to-all-start.18) | async-done | bytes 1179680 | tf_op jit(solution)/shard_map/all_to_all | solution.py:1279
  (728 shorter events, 407.4 us)
Async XLA Ops:
  7.2 39.0 %all-gather.6.cloned.1.call-start = ((), (), s32[]{:S(2)}) async-start(), calls=%async_computation.22 | async-start | bytes 2359296 | tf_op jit(solution)/shard_map/all_gather | solution.py:973
  7.9 118.6 %all-gather.8.cloned.1.call-start = ((), (), s32[]{:S(2)}) async-start(), calls=%async_computation.23 | async-start | bytes 4325376 | tf_op jit(solution)/shard_map/all_gather | solution.py:978
  20.7 188.0 %all-gather.12.cloned.1.call-start = ((), (), s32[]{:S(2)}) async-start(), calls=%async_computation.25 | async-start | bytes 3194880 | tf_op jit(solution)/shard_map/all_gather | solution.py:1015
  25.0 125.1 %collective-permute-start.16 = (bf16[216,128]{1,0:T(8,128)(2,1)}, bf16[216,128]{1,0:T(8,128)(2,1)}, u32[]{:S(2)}, u32[]{:S(2)}) collective-permute-start(bf16[216,128]{1,0:T(8,128)(2,1)} %reshape_reshape.10), channel_id=1, source_target_pairs={{0,1},{1,2},{2,3},{3,0},{4,5},{5,6},{6,7},{7,4},{8,9},{9,10},{10,1... | collective-permute-start | bytes 165896 | tf_op jit(solution)/shard_map/ppermute | solution.py:26
  25.4 150.9 %collective-permute-start.17 = (bf16[216,128]{1,0:T(8,128)(2,1)}, bf16[216,128]{1,0:T(8,128)(2,1)}, u32[]{:S(2)}, u32[]{:S(2)}) collective-permute-start(bf16[216,128]{1,0:T(8,128)(2,1)} %reshape_reshape.10), channel_id=1, source_target_pairs={{0,2},{1,3},{2,0},{3,1},{4,6},{5,7},{6,4},{7,5},{8,10},{9,11},{10,... | collective-permute-start | bytes 165896 | tf_op jit(solution)/shard_map/ppermute | solution.py:26
  163.0 70.0 %collective-permute-start.18 = (bf16[216,128]{1,0:T(8,128)(2,1)}, bf16[216,128]{1,0:T(8,128)(2,1)}, u32[]{:S(2)}, u32[]{:S(2)}) collective-permute-start(bf16[216,128]{1,0:T(8,128)(2,1)} %reshape_reshape.10), channel_id=1, source_target_pairs={{0,3},{1,0},{2,1},{3,2},{4,7},{5,4},{6,5},{7,6},{8,11},{9,8},{10,9... | collective-permute-start | bytes 165896 | tf_op jit(solution)/shard_map/ppermute | solution.py:26
  165.5 131.0 %collective-permute-start.19 = (bf16[64,21]{0,1:T(8,128)(2,1)}, bf16[64,21]{0,1:T(8,128)(2,1)}, u32[]{:S(2)}, u32[]{:S(2)}) collective-permute-start(bf16[64,21]{0,1:T(8,128)(2,1)} %param.34), channel_id=1, source_target_pairs={{0,1},{1,2},{2,3},{3,0},{4,5},{5,6},{6,7},{7,4},{8,9},{9,10},{10,1... | collective-permute-start | bytes 8072 | tf_op jit(solution)/shard_map/ppermute | solution.py:26
  167.5 47.9 %all-to-all-start.1 = ((f32[32,4,128]{2,1,0:T(4,128)}), f32[32,4,128]{2,1,0:T(4,128)S(1)}, u32[]{:S(2)}, u32[]{:S(2)}) async-start(f32[32,4,128]{2,1,0:T(4,128)} %get-tuple-element.82), calls=%async_computation.1 | async-start | bytes 131072 | tf_op jit(solution)/shard_map/all_to_all | solution.py:1072
  260.2 28.0 %all-to-all-start.17 = ((bf16[4,256,128]{2,1,0:T(8,128)(2,1)}), bf16[4,256,128]{2,1,0:T(8,128)(2,1)}, u32[]{:S(2)}, u32[]{:S(2)}) async-start(bf16[4,256,128]{2,1,0:T(8,128)(2,1)} %reshape.1141), calls=%async_computation.17 | async-start | bytes 524288 | tf_op jit(solution)/shard_map/all_to_all | solution.py:1044
  267.9 29.9 %collective-permute-start.20 = (bf16[64,21]{0,1:T(8,128)(2,1)}, bf16[64,21]{0,1:T(8,128)(2,1)}, u32[]{:S(2)}, u32[]{:S(2)}) collective-permute-start(bf16[64,21]{0,1:T(8,128)(2,1)} %param.34), channel_id=1, source_target_pairs={{0,2},{1,3},{2,0},{3,1},{4,6},{5,7},{6,4},{7,5},{8,10},{9,11},{10,... | collective-permute-start | bytes 8072 | tf_op jit(solution)/shard_map/ppermute | solution.py:26
  269.2 29.9 %collective-permute-start.21 = (bf16[64,21]{0,1:T(8,128)(2,1)}, bf16[64,21]{0,1:T(8,128)(2,1)}, u32[]{:S(2)}, u32[]{:S(2)}) collective-permute-start(bf16[64,21]{0,1:T(8,128)(2,1)} %param.34), channel_id=1, source_target_pairs={{0,3},{1,0},{2,1},{3,2},{4,7},{5,4},{6,5},{7,6},{8,11},{9,8},{10,9... | collective-permute-start | bytes 8072 | tf_op jit(solution)/shard_map/ppermute | solution.py:26
  295.1 402.6 %all-gather.10.cloned.1.call-start = ((), (), s32[]{:S(2)}) async-start(), calls=%async_computation.24 | async-start | bytes 2359296 | tf_op jit(solution)/shard_map/all_gather | solution.py:1045
  389.6 23.8 %collective-permute-start.22 = (bf16[2,256,256]{2,1,0:T(8,128)(2,1)}, bf16[2,256,256]{2,1,0:T(8,128)(2,1)}, u32[]{:S(2)}, u32[]{:S(2)}) collective-permute-start(bf16[2,256,256]{2,1,0:T(8,128)(2,1)} %copy-done.97), channel_id=1, source_target_pairs={{0,1},{1,2},{2,3},{3,4},{4,5},{5,6},{6,7},{7,8},{8,9},{9,10},{10,1... | collective-permute-start | bytes 786440 | tf_op jit(solution)/shard_map/ppermute | solution.py:32
  428.5 23.4 %all-to-all-start.11 = ((f32[32,2,256]{2,1,0:T(2,128)}), f32[32,2,256]{2,1,0:T(2,128)}, u32[]{:S(2)}, u32[]{:S(2)}) async-start(f32[32,2,256]{2,1,0:T(2,128)} %copy-done.60), calls=%async_computation.11 | async-start | bytes 131072 | tf_op jit(solution)/shard_map/all_to_all | solution.py:1090
  439.3 26.6 %collective-permute-start.24 = (bf16[256,256]{1,0:T(8,128)(2,1)}, bf16[256,256]{1,0:T(8,128)(2,1)}, u32[]{:S(2)}, u32[]{:S(2)}) collective-permute-start(bf16[256,256]{1,0:T(8,128)(2,1)} %copy-done.101), channel_id=1, source_target_pairs={{0,1},{1,2},{2,3},{3,4},{4,5},{5,6},{6,7},{7,8},{8,9},{9,10},{10,1... | collective-permute-start | bytes 393224 | tf_op jit(solution)/shard_map/ppermute | solution.py:32
  442.6 23.4 %collective-permute-start.25 = (bf16[256,256]{1,0:T(8,128)(2,1)}, bf16[256,256]{1,0:T(8,128)(2,1)}, u32[]{:S(2)}, u32[]{:S(2)}) collective-permute-start(bf16[256,256]{1,0:T(8,128)(2,1)} %copy-done.100), channel_id=1, source_target_pairs={{1,0},{2,1},{3,2},{4,3},{5,4},{6,5},{7,6},{8,7},{9,8},{10,9},{11,1... | collective-permute-start | bytes 393224 | tf_op jit(solution)/shard_map/ppermute | solution.py:32
  458.9 63.9 %collective-permute-start.47 = (bf16[256,640]{1,0:T(8,128)(2,1)}, bf16[256,640]{1,0:T(8,128)(2,1)}, u32[]{:S(2)}, u32[]{:S(2)}) collective-permute-start(bf16[256,640]{1,0:T(8,128)(2,1)} %get-tuple-element.286), channel_id=1, source_target_pairs={{0,1},{1,2},{2,3},{3,0},{4,5},{5,6},{6,7},{7,4},{8,9},{9,10},{10,1... | collective-permute-start | bytes 983048 | tf_op jit(solution)/shard_map/ppermute | solution.py:26
  458.9 64.6 %collective-permute-start.48 = (bf16[256,640]{1,0:T(8,128)(2,1)}, bf16[256,640]{1,0:T(8,128)(2,1)}, u32[]{:S(2)}, u32[]{:S(2)}) collective-permute-start(bf16[256,640]{1,0:T(8,128)(2,1)} %get-tuple-element.288), channel_id=1, source_target_pairs={{0,2},{1,3},{2,0},{3,1},{4,6},{5,7},{6,4},{7,5},{8,10},{9,11},{10,... | collective-permute-start | bytes 983048 | tf_op jit(solution)/shard_map/ppermute | solution.py:26
  493.8 29.8 %collective-permute-start.49 = (bf16[256,640]{1,0:T(8,128)(2,1)}, bf16[256,640]{1,0:T(8,128)(2,1)}, u32[]{:S(2)}, u32[]{:S(2)}) collective-permute-start(bf16[256,640]{1,0:T(8,128)(2,1)} %get-tuple-element.287), channel_id=1, source_target_pairs={{0,3},{1,0},{2,1},{3,2},{4,7},{5,4},{6,5},{7,6},{8,11},{9,8},{10,9... | collective-permute-start | bytes 983048 | tf_op jit(solution)/shard_map/ppermute | solution.py:26
  509.5 70.7 %collective-permute-start.50 = (bf16[256,640]{1,0:T(8,128)(2,1)}, bf16[256,640]{1,0:T(8,128)(2,1)}, u32[]{:S(2)}, u32[]{:S(2)}) collective-permute-start(bf16[256,640]{1,0:T(8,128)(2,1)} %get-tuple-element.283), channel_id=1, source_target_pairs={{0,1},{1,2},{2,3},{3,0},{4,5},{5,6},{6,7},{7,4},{8,9},{9,10},{10,1... | collective-permute-start | bytes 983048 | tf_op jit(solution)/shard_map/ppermute | solution.py:26
  511.0 71.0 %collective-permute-start.51 = (bf16[256,640]{1,0:T(8,128)(2,1)}, bf16[256,640]{1,0:T(8,128)(2,1)}, u32[]{:S(2)}, u32[]{:S(2)}) collective-permute-start(bf16[256,640]{1,0:T(8,128)(2,1)} %get-tuple-element.285), channel_id=1, source_target_pairs={{0,2},{1,3},{2,0},{3,1},{4,6},{5,7},{6,4},{7,5},{8,10},{9,11},{10,... | collective-permute-start | bytes 983048 | tf_op jit(solution)/shard_map/ppermute | solution.py:26
  522.8 59.7 %collective-permute-start.52 = (bf16[256,640]{1,0:T(8,128)(2,1)}, bf16[256,640]{1,0:T(8,128)(2,1)}, u32[]{:S(2)}, u32[]{:S(2)}) collective-permute-start(bf16[256,640]{1,0:T(8,128)(2,1)} %get-tuple-element.284), channel_id=1, source_target_pairs={{0,3},{1,0},{2,1},{3,2},{4,7},{5,4},{6,5},{7,6},{8,11},{9,8},{10,9... | collective-permute-start | bytes 983048 | tf_op jit(solution)/shard_map/ppermute | solution.py:26
  537.3 63.4 %all-to-all-start.15 = ((bf16[8,80,128]{2,1,0:T(8,128)(2,1)}), bf16[8,80,128]{2,1,0:T(8,128)(2,1)}, u32[]{:S(2)}, u32[]{:S(2)}) async-start(bf16[8,80,128]{2,1,0:T(8,128)(2,1)} %copy-done.38), calls=%async_computation.15 | async-start | bytes 327680 | tf_op jit(solution)/shard_map/all_to_all | solution.py:1230
  579.0 31.7 %collective-permute-start.38 = (bf16[4,48,256]{1,2,0:T(8,128)(2,1)}, bf16[4,48,256]{1,2,0:T(8,128)(2,1)}, u32[]{:S(2)}, u32[]{:S(2)}) collective-permute-start(bf16[4,48,256]{1,2,0:T(8,128)(2,1)} %bitcast.90), channel_id=1, source_target_pairs={{0,2},{1,3},{2,0},{3,1},{4,6},{5,7},{6,4},{7,5},{8,10},{9,11},{10,... | collective-permute-start | bytes 294920 | tf_op jit(solution)/shard_map/ppermute | solution.py:26
  580.3 34.4 %collective-permute-start.39 = (bf16[4,48,256]{1,2,0:T(8,128)(2,1)}, bf16[4,48,256]{1,2,0:T(8,128)(2,1)}, u32[]{:S(2)}, u32[]{:S(2)}) collective-permute-start(bf16[4,48,256]{1,2,0:T(8,128)(2,1)} %bitcast.90), channel_id=1, source_target_pairs={{0,3},{1,0},{2,1},{3,2},{4,7},{5,4},{6,5},{7,6},{8,11},{9,8},{10,9... | collective-permute-start | bytes 294920 | tf_op jit(solution)/shard_map/ppermute | solution.py:26
  582.0 47.8 %collective-permute-start.41 = (bf16[1280,64]{1,0:T(8,128)(2,1)}, bf16[1280,64]{1,0:T(8,128)(2,1)}, u32[]{:S(2)}, u32[]{:S(2)}) collective-permute-start(bf16[1280,64]{1,0:T(8,128)(2,1)} %bitcast.356), channel_id=1, source_target_pairs={{0,1},{1,2},{2,3},{3,0},{4,5},{5,6},{6,7},{7,4},{8,9},{9,10},{10,1... | collective-permute-start | bytes 491528 | tf_op jit(solution)/shard_map/ppermute | solution.py:26
  582.5 47.2 %collective-permute-start.42 = (bf16[1280,64]{1,0:T(8,128)(2,1)}, bf16[1280,64]{1,0:T(8,128)(2,1)}, u32[]{:S(2)}, u32[]{:S(2)}) collective-permute-start(bf16[1280,64]{1,0:T(8,128)(2,1)} %bitcast.355), channel_id=1, source_target_pairs={{0,2},{1,3},{2,0},{3,1},{4,6},{5,7},{6,4},{7,5},{8,10},{9,11},{10,... | collective-permute-start | bytes 491528 | tf_op jit(solution)/shard_map/ppermute | solution.py:26
  597.0 32.7 %collective-permute-start.43 = (bf16[1280,64]{1,0:T(8,128)(2,1)}, bf16[1280,64]{1,0:T(8,128)(2,1)}, u32[]{:S(2)}, u32[]{:S(2)}) collective-permute-start(bf16[1280,64]{1,0:T(8,128)(2,1)} %bitcast.354), channel_id=1, source_target_pairs={{0,3},{1,0},{2,1},{3,2},{4,7},{5,4},{6,5},{7,6},{8,11},{9,8},{10,9... | collective-permute-start | bytes 491528 | tf_op jit(solution)/shard_map/ppermute | solution.py:26
  619.5 46.6 %all-to-all-start.20 = ((bf16[64,1,5573]{2,1,0:T(2,128)(2,1)}), bf16[64,1,5573]{2,1,0:T(2,128)(2,1)}, u32[]{:S(2)}, u32[]{:S(2)}) async-start(bf16[64,1,5573]{2,1,0:T(2,128)(2,1)} %concatenate.81), calls=%async_computation.20 | async-start | bytes 2883584 | tf_op jit(solution)/shard_map/all_to_all | solution.py:1301
  673.3 24.4 %collective-permute-start.31 = (bf16[18,64,128]{2,1,0:T(8,128)(2,1)}, bf16[18,64,128]{2,1,0:T(8,128)(2,1)S(1)}, u32[]{:S(2)}, u32[]{:S(2)}) collective-permute-start(bf16[18,64,128]{2,1,0:T(8,128)(2,1)} %get-tuple-element.299), channel_id=1, source_target_pairs={{0,32},{32,64},{64,96},{96,128},{128,160},{160,192},{192,224},{1,3... | collective-permute-start | bytes 884744 | tf_op jit(solution)/shard_map/ppermute | solution.py:32
  685.1 28.5 %all-to-all-start.21 = ((f32[64,1,453]{2,1,0:T(1,128)}), f32[64,1,453]{2,1,0:T(1,128)}, u32[]{:S(2)}, u32[]{:S(2)}) async-start(f32[64,1,453]{2,1,0:T(1,128)} %broadcast_in_dim.339), calls=%async_computation.21 | async-start | bytes 262144 | tf_op jit(solution)/shard_map/all_to_all | solution.py:1327
  713.6 38.7 %all-to-all-start.18 = ((bf16[8,64,1152]{2,1,0:T(8,128)(2,1)}), bf16[8,64,1152]{2,1,0:T(8,128)(2,1)}, u32[]{:S(2)}, u32[]{:S(2)}) async-start(bf16[8,64,1152]{2,1,0:T(8,128)(2,1)} %bitcast.341), calls=%async_computation.18 | async-start | bytes 2359296 | tf_op jit(solution)/shard_map/all_to_all | solution.py:1279
  (189 other events, 3241.6 us)
Sparse Core Ops, SparseCore 0:
  9.9 33.8 all-gather.5
  46.9 79.5 all-gather.7
  129.9 78.7 all-gather.11
  307.4 30.6 all-gather.9
